TPU v7x, 256 devices: a whole 4x4x8 slice. The times are simulated.
256 devices in a mesh: group: 16 (over z, core), mode: 16 (over y, x).
Axes of the slice: x: 4, y: 4, z: 8, core: 2. Of those that a mesh axis runs over, the one named last changes fastest.
Arguments:
- shapes: bfloat16 [2, 16, 512, 2048], P(None, 'group', None, 'mode'), may hold values from -0.75 to 0.75
- pairs: int32 [16, 2], P('group'), may hold values from 0 to 15
- omega: float32 [2048], P('mode'), may hold values from 0.5 to 4
- damping: float32 [2048], P('mode'), may hold values from 0.02 to 0.2
- speeds: float32 [4], replicated, may hold values from 0.6 to 3
Outputs:
- receptance: float32 [512, 16, 4, 2, 512], P('mode', 'group')
All inputs are finite; a program needn't handle non-finite values.
Results may differ from a plain program's by a relative error of at most 0.0029.
Values may be sent and summed in bfloat16 or wider, within the bound.
No kernel may reach another device: no remote copies, remote signals or barrier semaphores. Data moves between devices by JAX's collectives and lax.ppermute only.
A program may use at most 64 MiB of HBM per device.

v0:
```python
import jax
import jax.numpy as jnp
from jax import lax
from jax.sharding import PartitionSpec as P


def modal_weights(omega, damping, speeds):
    real_part = omega[None, :] ** 2 - speeds[:, None] ** 2
    imag_part = 2.0 * damping[None, :] * omega[None, :] * speeds[:, None]
    denom = real_part * real_part + imag_part * imag_part
    return (real_part / denom, -imag_part / denom)


def loaded_right(excite, weight_re, weight_im):
    excite_re = excite[0][None]
    excite_im = excite[1][None]
    wre = weight_re[:, None, None, :]
    wim = weight_im[:, None, None, :]
    loaded_re = (wre * excite_re - wim * excite_im).astype(jnp.bfloat16)
    loaded_im = (wre * excite_im + wim * excite_re).astype(jnp.bfloat16)
    right_re = jnp.concatenate([loaded_re, -loaded_im], axis=-1)
    right_im = jnp.concatenate([loaded_im, loaded_re], axis=-1)
    return (right_re, right_im)


def block_product(left_rows, right_re, right_im):
    out_re = jnp.einsum("pkm,spjm->kpsj", left_rows, right_re, preferred_element_type=jnp.float32)
    out_im = jnp.einsum("pkm,spjm->kpsj", left_rows, right_im, preferred_element_type=jnp.float32)
    return jnp.stack([out_re, out_im], axis=3)


def shards(shapes, pairs, omega, damping, speeds):
    wanted = pairs.reshape(-1)
    pieces = lax.all_gather(shapes, "group", axis=1, tiled=True)
    region_ids = jnp.arange(pieces.shape[1], dtype=jnp.int32)
    onehot = (wanted[:, None] == region_ids[None, :]).astype(jnp.bfloat16)
    found = jnp.einsum("nq,cqrm->cnrm", onehot, pieces, preferred_element_type=jnp.float32)
    picked = found.astype(jnp.bfloat16)
    response = picked[:, 0::2]
    excite = picked[:, 1::2]
    weight_re, weight_im = modal_weights(omega, damping, speeds)
    right_re, right_im = loaded_right(excite, weight_re, weight_im)
    left_all = jnp.concatenate([response[0], response[1]], axis=-1)
    return lax.psum_scatter(
        block_product(left_all, right_re, right_im), "mode", scatter_dimension=0, tiled=True
    )


def solution(mesh):
    in_specs = (P(None, "group", None, "mode"), P("group", None), P("mode"), P("mode"), P())
    out_specs = P("mode", "group", None, None, None)
    return jax.shard_map(shards, mesh=mesh, in_specs=in_specs, out_specs=out_specs, check_vma=False)
```

profile of v0, /device:TPU:6, one launch (start us, length us, event | category | flops | bytes accessed | tf_op | source)
XLA Modules:
  0.0 234.1 jit_solution(12381365579292583048)
XLA Ops:
  6.5 0.0 all-gather.2.cloned.1.call-start
  6.5 0.7 all-gather.2.cloned.1.call-update
  7.3 0.0 all-reduce.3.cloned.1.call-start
  7.3 0.7 integer_pow.9
  8.0 0.7 multiply_multiply_fusion.1
  8.7 0.7 subtract_divide_fusion
  9.4 44.8 %all-gather.2.cloned.1.call-done = bf16[2,16,512,128]{3,2,0,1:T(8,128)(2,1)} async-done(((bf16[2,1,512,128]{3,2,0,1:T(8,128)(2,1)}), bf16[2,16,512,128]{3,2,0,1:T(8,128)(2,1)}) %all-gather.2.cloned.1.call-update) | async-done | bytes 4194320 | tf_op jit(solution)/shard_map/all_gather | solution.py:34
  54.2 4.7 %fusion.5 = bf16[2,2,512,128]{3,1,2,0:T(2,128)(2,1)S(1)} fusion(bf16[2,16,512,128]{3,2,0,1:T(8,128)(2,1)} %all-gather.2.cloned.1.call-done, s32[2]{0:T(128)} %bitcast.44), kind=kOutput, calls=%fused_computation.6 | convolution fusion | flops 8650784 | bytes 4718600 | tf_op jit(solution)/shard_map/nq,cqrm->cnrm/dot_general | solution.py:37
  59.0 0.7 fusion.21
  59.7 0.2 fusion.20
  59.9 0.1 subtract_convert_fusion
  60.1 0.7 convolution_bitcast_fusion.1
  60.9 0.7 convolution_bitcast_fusion
  61.6 4.3 %pad_maximum_fusion = f32[512,1,4,2,512]{0,4,2,3,1:T(8,128)} fusion(f32[512,1,4,1,512]{0,4,2,3,1:T(8,128)S(1)} %convolution_bitcast_fusion, f32[512,1,4,1,512]{0,4,2,3,1:T(8,128)S(1)} %convolution_bitcast_fusion.1), kind=kLoop, calls=%fused_computation | loop fusion | flops 2097152 | bytes 16777216 | tf_op jit(solution)/shard_map/stack | solution.py:29
  65.9 10.3 %copy.15 = f32[512,1,4,2,512]{4,2,3,1,0:T(4,128)} copy(f32[512,1,4,2,512]{0,4,2,3,1:T(8,128)} %pad_maximum_fusion) | data formatting | bytes 16777216 | tf_op jit(solution)/shard_map/stack | solution.py:29
  76.2 0.0 copy-start
  76.2 0.0 all-reduce.3.cloned.1.call-update
  76.2 0.6 copy-done
  76.9 0.6 dynamic-slice
  78.1 147.0 %all-reduce.3.cloned.1.call-done = f32[512,1,4,2,512]{4,2,3,1,0:T(4,128)} async-done(((f32[512,1,4,2,512]{4,2,3,1,0:T(4,128)}), f32[512,1,4,2,512]{4,2,3,1,0:T(4,128)}) %all-reduce.3.cloned.1.call-update) | async-done | bytes 8388624
  225.1 1.1 constant_dynamic-slice_fusion
  226.2 1.1 copy.16
  (1 shorter events, 0.0 us)
Async XLA Ops:
  6.5 47.7 %all-gather.2.cloned.1.call-start = ((), (), s32[]{:S(2)}) async-start(), calls=%async_computation | async-start | bytes 4456448 | tf_op jit(solution)/shard_map/all_gather | solution.py:34
  7.3 217.8 %all-reduce.3.cloned.1.call-start = ((), (), s32[]{:S(2)}) async-start(), calls=%async_computation.1 | async-start | bytes 16777216
  76.2 0.7 copy-start
Sparse Core Ops, SparseCore 0:
  9.2 45.0 all-gather.1
  76.3 148.7 all-reduce.2
where the time goes:
time: 236 us; the launch traced here: 234 us
  waiting for transfers between devices  192 us (81%)
  between operations  14.1 us (6%)
  local copies, waits for them, and re-layouts  13.7 us (6%)
  other arithmetic  7.51 us (3%)
  matrix products  6.2 us (3%)
    unnamed x3, waiting for transfers between devices  148 us
    all_gather x1, waiting for transfers between devices, shards(): pieces = lax.all_gather(shapes, 'group', axis=1, tiled=True)  44.8 us
    another operation x1, local copies, waits for them, and re-layouts, block_product(): return jnp.stack([out_re, out_im], axis=3)  10.3 us
    dot_general x1, matrix products, shards(): jnp.einsum('nq,cqrm->cnrm', onehot, pieces, preferred_element_type=jnp.fl...  4.73 us
  transfers between devices with their start and end apart: 2, of which 2 were waited for; matrix products, arithmetic and copies ran while one was open for 1% of the time, Pallas kernels for 0%

commit v1 on v0

v1 whole, which is shorter than its diff:
```python
import jax
import jax.numpy as jnp
from jax import lax
from jax.experimental import pallas as pl
from jax.experimental.pallas import tpu as pltpu
from jax.sharding import PartitionSpec as P

BF = jnp.bfloat16
F32 = jnp.float32
VMEM = pl.BlockSpec(memory_space=pltpu.VMEM)
SMEM = pl.BlockSpec(memory_space=pltpu.SMEM)
PARAMS = pltpu.CompilerParams(vmem_limit_bytes=40 * 1024 * 1024)


def call(kernel, out_shape, in_specs, name, scratch=()):
    return pl.pallas_call(
        kernel,
        out_shape=out_shape,
        in_specs=in_specs,
        out_specs=VMEM,
        scratch_shapes=list(scratch),
        compiler_params=PARAMS,
        name=name,
    )


def slice_kernel(shapes_ref, pairs_ref, out_ref):
    rows = lax.broadcasted_iota(jnp.int32, (16, 128), 0)
    pair = jnp.where(rows < 8, pairs_ref[0, 0], pairs_ref[0, 1])
    pair = pair.astype(F32).astype(BF)
    for i in range(16):
        out_ref[i, 0:32, :] = shapes_ref[0, 0, 32 * i : 32 * i + 32, :]
        out_ref[i, 32:64, :] = shapes_ref[1, 0, 32 * i : 32 * i + 32, :]
        out_ref[i, 64:80, :] = pair


def pick_kernel(all_ref, out_ref):
    for g in range(16):
        pair = all_ref[g, 64:80, :].astype(F32)
        response = pair[0, 0].astype(jnp.int32)
        excite = pair[8, 0].astype(jnp.int32)
        out_ref[g, 0:64, :] = all_ref[response, 0:64, :]
        out_ref[g, 64:128, :] = all_ref[excite, 0:64, :]


def split3(x):
    first = x.astype(BF)
    rest = x - first.astype(F32)
    second = rest.astype(BF)
    third = (rest - second.astype(F32)).astype(BF)
    return first.astype(F32), second.astype(F32), third.astype(F32)


def fan_kernel(mine_ref, omega_ref, damping_ref, out_ref):
    pieces = split3(omega_ref[...]) + split3(damping_ref[...])
    rows = lax.broadcasted_iota(jnp.int32, (16, 128), 0)
    table = jnp.zeros((16, 128), F32)
    for n, piece in enumerate(pieces):
        table = jnp.where(rows == n, piece, table)
    table = table.astype(BF)
    for y in range(4):
        for i in range(16):
            out_ref[y, 32 * i : 32 * i + 32, :] = mine_ref[i, 64:96, :]
            out_ref[y, 512 + 32 * i : 544 + 32 * i, :] = mine_ref[i, 96:128, :]
        for q in range(4):
            out_ref[y, 1024 + 32 * q : 1056 + 32 * q, :] = mine_ref[4 * y + q, 0:32, :]
            out_ref[y, 1152 + 32 * q : 1184 + 32 * q, :] = mine_ref[4 * y + q, 32:64, :]
        out_ref[y, 1280:1296, :] = table


def product_kernel(parts_ref, speeds_ref, out_ref):
    left = []
    weights = []
    for y in range(4):
        res_re = parts_ref[y, 1024:1152, :]
        res_im = parts_ref[y, 1152:1280, :]
        left.append(jnp.concatenate([res_re, res_im], axis=0))
        left.append(jnp.concatenate([-res_im, res_re], axis=0))
        table = parts_ref[y, 1280:1296, :].astype(F32)
        omega = table[0:1] + table[1:2] + table[2:3]
        damping = table[3:4] + table[4:5] + table[5:6]
        weights.append((omega, damping))
    left = jnp.concatenate(left, axis=1)
    for s in range(4):
        speed = speeds_ref[s]
        right = []
        for y in range(4):
            omega, damping = weights[y]
            a = omega * omega - speed * speed
            b = 2.0 * damping * omega * speed
            denom = a * a + b * b
            wre = a / denom
            wim = -b / denom
            ere = parts_ref[y, 0:512, :].astype(F32)
            eim = parts_ref[y, 512:1024, :].astype(F32)
            right.append((wre * ere - wim * eim).astype(BF))
            right.append((wre * eim + wim * ere).astype(BF))
        right = jnp.concatenate(right, axis=1)
        both = lax.dot_general(
            left, right, (((1,), (1,)), ((), ())), preferred_element_type=F32
        )
        for c in range(2):
            at = (2 * s + c) * 512
            out_ref[:, at : at + 512] = both[128 * c : 128 * c + 128].astype(BF)


def sum_kernel(parts_ref, out_ref):
    for s in range(4):
        for c in range(2):
            at = (2 * s + c) * 512
            total = parts_ref[0, :, at : at + 512].astype(F32)
            for x in range(1, 4):
                total = total + parts_ref[x, :, at : at + 512].astype(F32)
            out_ref[:, 0, s, c, :] = total


def shards(shapes, pairs, omega, damping, speeds):
    along_y = [[4 * y + x for y in range(4)] for x in range(4)]
    along_x = [[4 * y + x for x in range(4)] for y in range(4)]
    sliced = call(
        slice_kernel, jax.ShapeDtypeStruct((16, 80, 128), BF), [VMEM, SMEM], "slice_rows"
    )(shapes, pairs)
    regions = lax.all_to_all(sliced, "group", 0, 0, tiled=True)
    picked = call(
        pick_kernel, jax.ShapeDtypeStruct((16, 128, 128), BF), [VMEM], "pick_regions"
    )(regions)
    mine = lax.all_to_all(picked, "group", 0, 0, tiled=True)
    fanned = call(
        fan_kernel, jax.ShapeDtypeStruct((4, 1296, 128), BF), [VMEM] * 3, "fan_out"
    )(mine, omega.reshape(1, 128), damping.reshape(1, 128))
    parts = lax.all_to_all(fanned, "mode", 0, 0, tiled=True, axis_index_groups=along_y)
    partial = call(
        product_kernel, jax.ShapeDtypeStruct((128, 4096), BF), [VMEM, SMEM], "products"
    )(parts, speeds)
    terms = lax.all_to_all(
        partial.reshape(4, 32, 4096), "mode", 0, 0, tiled=True, axis_index_groups=along_x
    )
    return call(
        sum_kernel, jax.ShapeDtypeStruct((32, 1, 4, 2, 512), F32), [VMEM], "sum_terms"
    )(terms)


def solution(mesh):
    in_specs = (P(None, "group", None, "mode"), P("group", None), P("mode"), P("mode"), P())
    out_specs = P("mode", "group", None, None, None)
    return jax.shard_map(shards, mesh=mesh, in_specs=in_specs, out_specs=out_specs, check_vma=False)
```

time: 236 us -> 89.3 us (0.38)
  waiting for transfers between devices: 192 us -> 0 us
  blocking collectives: 0 us -> 81.5 us
  between operations: 14.1 us -> 0.06 us
  local copies, waits for them, and re-layouts: 13.7 us -> 1.62 us
  other arithmetic: 7.51 us -> 0 us
  matrix products: 6.2 us -> 0 us
  Pallas kernels: 0 us -> 4.48 us
    unnamed x3 -> x0, waiting for transfers between devices: 148 us -> none
    all_to_all x0 -> x4, blocking collectives: none -> 81.5 us  [the longest x1 23.4 us: shards(): lax.all_to_all(fanned, 'mode', 0, 0, tiled=True, axis_index_groups=along_y)]
    all_gather x1 -> x0, waiting for transfers between devices: 44.8 us -> none  [shards(): pieces = lax.all_gather(shapes, 'group', axis=1, tiled=True)]
    another operation x1 -> x0, local copies, waits for them, and re-layouts: 10.3 us -> none  [block_product(): return jnp.stack([out_re, out_im], axis=3)]
    dot_general x3 -> x0, matrix products: 6.2 us -> none  [the longest x1 4.73 us: shards(): jnp.einsum('nq,cqrm->cnrm', onehot, pieces, preferred_element_type=jnp.fl...]
    pallas_call x0 -> x5, Pallas kernels: none -> 4.48 us  [the longest x1 2.65 us: shards(): call(product_kernel, jax.ShapeDtypeStruct((128, 4096), BF), [VMEM, SMEM],...]
    another operation x1 -> x0, other arithmetic: 4.29 us -> none  [block_product(): return jnp.stack([out_re, out_im], axis=3)]
  transfers between devices with their start and end apart: 2 -> 0, of which waited for: 2 -> 0; matrix products, arithmetic and copies ran while one was open for 1% -> 0% of each run, Pallas kernels for 0% -> 0%
where the time goes in v1:
time: 89.3 us; the launch traced here: 87.7 us
  blocking collectives  81.5 us (91%)
  Pallas kernels  4.48 us (5%)
  local copies, waits for them, and re-layouts  1.62 us (2%)
    all_to_all x1, blocking collectives, shards(): lax.all_to_all(fanned, 'mode', 0, 0, tiled=True, axis_index_groups=along_y)  23.4 us
    all_to_all x1, blocking collectives, shards(): regions = lax.all_to_all(sliced, 'group', 0, 0, tiled=True)  20.8 us
    all_to_all x1, blocking collectives, shards(): mine = lax.all_to_all(picked, 'group', 0, 0, tiled=True)  19.4 us
    all_to_all x1, blocking collectives, shards(): lax.all_to_all(partial.reshape(4, 32, 4096), 'mode', 0, 0, tiled=True, ax...  17.9 us
    pallas_call x1, Pallas kernels, shards(): call(product_kernel, jax.ShapeDtypeStruct((128, 4096), BF), [VMEM, SMEM],...  2.65 us

profile of v1, /device:TPU:6, one launch (start us, length us, event | category | flops | bytes accessed | tf_op | source)
XLA Modules:
  0.0 87.7 jit_solution(17728598208016022324)
XLA Ops:
  0.0 0.0 copy-start
  0.0 0.9 %copy-done = bf16[2,1,512,128]{3,2,1,0:T(8,128)(2,1)S(1)} copy-done((bf16[2,1,512,128]{3,2,1,0:T(8,128)(2,1)S(1)}, bf16[2,1,512,128]{3,2,1,0:T(8,128)(2,1)}, u32[]{:S(2)}) %copy-start) | copy-done | bytes 262168
  1.0 0.0 copy-start.3
  1.0 0.7 copy-done.3
  1.6 0.6 slice_rows.1
  2.2 0.0 copy-start.1
  2.2 0.0 copy-start.2
  2.2 20.8 %all_to_all.20.all_ref = bf16[16,80,128]{2,1,0:T(8,128)(2,1)S(1)} all-to-all(bf16[16,80,128]{2,1,0:T(8,128)(2,1)S(1)} %slice_rows.1), channel_id=1, replica_groups=mesh['group'=16,'mode'=16] {'group'}, dimensions={0} | all-to-all | bytes 655360 | tf_op jit(solution)/shard_map/all_to_all | solution.py:123
  23.0 0.1 pick_regions.1
  23.1 19.4 %all_to_all.21.mine_ref = bf16[16,128,128]{2,1,0:T(8,128)(2,1)S(1)} all-to-all(bf16[16,128,128]{2,1,0:T(8,128)(2,1)S(1)} %pick_regions.1), channel_id=1, replica_groups=mesh['group'=16,'mode'=16] {'group'}, dimensions={0} | all-to-all | bytes 1048576 | tf_op jit(solution)/shard_map/all_to_all | solution.py:127
  42.5 0.0 copy-done.1
  42.5 0.0 copy-done.2
  42.5 0.2 fan_out.1
  42.7 0.0 copy-start.4
  42.7 23.4 %all_to_all.22.parts_ref = bf16[4,1296,128]{2,1,0:T(8,128)(2,1)S(1)} all-to-all(bf16[4,1296,128]{2,1,0:T(8,128)(2,1)S(1)} %fan_out.1), channel_id=1, replica_groups={{0,4,8,12},{1,5,9,13},{2,6,10,14},{3,7,11,15},{16,20,24,28},{17,21,25,2..., dimensions={0} | all-to-all | bytes 2654208 | tf_op jit(solution)/shard_map/all_to_all | solution.py:131
  66.1 0.0 copy-done.4
  66.1 2.6 %products.1 = bf16[128,4096]{1,0:T(8,128)(2,1)S(1)} custom-call(bf16[4,1296,128]{2,1,0:T(8,128)(2,1)S(1)} %all_to_all.22.parts_ref, f32[4]{0:T(128)S(1)} %copy-done.4), custom_call_target="tpu_custom_call" | custom-call | tf_op jit(solution)/shard_map/products/pallas_call | solution.py:132
  68.7 17.9 %all_to_all.23.parts_ref = bf16[4,32,4096]{2,1,0:T(8,128)(2,1)S(1)} all-to-all(bf16[4,32,4096]{2,1,0:T(8,128)(2,1)S(1)} %bitcast.3), channel_id=1, replica_groups={{0,1,2,3},{4,5,6,7},{8,9,10,11},{12,13,14,15},{16,17,18,19},{20,21,22,2..., dimensions={0} | all-to-all | bytes 2097152 | tf_op jit(solution)/shard_map/all_to_all | solution.py:135
  86.7 1.0 %sum_terms.1 = f32[32,1,4,2,512]{4,3,2,1,0:T(2,128)} custom-call(bf16[4,32,4096]{2,1,0:T(8,128)(2,1)S(1)} %all_to_all.23.parts_ref), custom_call_target="tpu_custom_call" | custom-call | tf_op jit(solution)/shard_map/sum_terms/pallas_call | solution.py:138
Async XLA Ops:
  0.0 0.9 %copy-start = (bf16[2,1,512,128]{3,2,1,0:T(8,128)(2,1)S(1)}, bf16[2,1,512,128]{3,2,1,0:T(8,128)(2,1)}, u32[]{:S(2)}) copy-start(bf16[2,1,512,128]{3,2,1,0:T(8,128)(2,1)} %shapes_ref.1) | copy-start | bytes 786436
  1.0 0.7 copy-start.3
  2.2 40.3 %copy-start.1 = (f32[128]{0:T(128)S(1)}, f32[128]{0:T(128)}, u32[]{:S(2)}) copy-start(f32[128]{0:T(128)} %param.7) | copy-start | bytes 1540
  2.2 40.3 %copy-start.2 = (f32[128]{0:T(128)S(1)}, f32[128]{0:T(128)}, u32[]{:S(2)}) copy-start(f32[128]{0:T(128)} %param.8) | copy-start | bytes 1540
  42.7 23.4 %copy-start.4 = (f32[4]{0:T(128)S(1)}, f32[4]{0:T(128)}, u32[]{:S(2)}) copy-start(f32[4]{0:T(128)} %speeds_ref.1) | copy-start | bytes 52

commit v2 on v1

v2 whole, which is shorter than its diff:
```python
import functools

import jax
import jax.numpy as jnp
from jax import lax
from jax.experimental import pallas as pl
from jax.experimental.pallas import tpu as pltpu
from jax.sharding import PartitionSpec as P

BF = jnp.bfloat16
F32 = jnp.float32
VMEM = pl.BlockSpec(memory_space=pltpu.VMEM)
SMEM = pl.BlockSpec(memory_space=pltpu.SMEM)
PARAMS = pltpu.CompilerParams(vmem_limit_bytes=40 * 1024 * 1024)
ORDER = (2, 1, 3)
BLOCKS = 49


def call(kernel, out_shape, in_specs, name, flops=0, size=1 << 20):
    many = isinstance(out_shape, tuple)
    return pl.pallas_call(
        kernel,
        out_shape=out_shape,
        in_specs=in_specs,
        out_specs=tuple(VMEM for _ in out_shape) if many else VMEM,
        compiler_params=PARAMS,
        cost_estimate=pl.CostEstimate(flops=flops, bytes_accessed=size, transcendentals=0),
        name=name,
    )


def slice_kernel(shapes_ref, pairs_ref, out_ref):
    rows = lax.broadcasted_iota(jnp.int32, (16, 128), 0)
    pair = jnp.where(rows < 8, pairs_ref[0, 0], pairs_ref[0, 1])
    pair = pair.astype(F32).astype(BF)
    for i in range(16):
        out_ref[i, 0:32, :] = shapes_ref[0, 0, 32 * i : 32 * i + 32, :]
        out_ref[i, 32:64, :] = shapes_ref[1, 0, 32 * i : 32 * i + 32, :]
        out_ref[i, 64:80, :] = pair


def pick_kernel(all_ref, out_ref):
    for g in range(16):
        pair = all_ref[g, 64:80, :].astype(F32)
        response = pair[0, 0].astype(jnp.int32)
        excite = pair[8, 0].astype(jnp.int32)
        out_ref[g, 0:64, :] = all_ref[response, 0:64, :]
        out_ref[g, 64:128, :] = all_ref[excite, 0:64, :]


def split3(x):
    first = x.astype(BF)
    rest = x - first.astype(F32)
    second = rest.astype(BF)
    third = (rest - second.astype(F32)).astype(BF)
    return first.astype(F32), second.astype(F32), third.astype(F32)


def position():
    me = lax.axis_index("mode")
    return lax.div(me, 4), lax.rem(me, 4)


def response_slice(half, tile, part):
    return 4 * tile + part if half == 0 else 4 * part + tile


def fan_kernel(mine_ref, omega_ref, damping_ref, *out_refs):
    here = position()
    pieces = split3(omega_ref[...]) + split3(damping_ref[...])
    rows = lax.broadcasted_iota(jnp.int32, (16, 128), 0)
    table = jnp.zeros((16, 128), F32)
    for n, piece in enumerate(pieces):
        table = jnp.where(rows == n, piece, table)
    table = table.astype(BF)
    for half in range(2):
        for n, d in enumerate(ORDER):
            out_ref = out_refs[3 * half + n]
            tile = lax.rem(here[half] + d, 4)
            for i in range(8):
                for b in range(4):
                    out_ref[4 * i + b] = mine_ref[8 * half + i, 64 + 16 * b : 80 + 16 * b, :]
            for q in range(4):
                row_slice = response_slice(half, tile, q)
                for b in range(4):
                    out_ref[32 + 4 * q + b] = mine_ref[row_slice, 16 * b : 16 * b + 16, :]
            out_ref[48] = table


def product_kernel(half, mine_ref, omega_ref, damping_ref, one_ref, two_ref, three_ref, speeds_ref, *out_refs):
    here = position()
    tile, part = here[half], here[1 - half]
    left, excite, weights = [], [], []
    for ref in (mine_ref, one_ref, two_ref, three_ref):
        res_re, res_im = [], []
        for d in range(4):
            q = lax.rem(part + d, 4)
            if ref is mine_ref:
                row_slice = response_slice(half, tile, q)
                res_re.append(mine_ref[row_slice, 0:32, :])
                res_im.append(mine_ref[row_slice, 32:64, :])
            else:
                res_re.append(ref[pl.ds(32 + 4 * q, 2)].reshape(32, 128))
                res_im.append(ref[pl.ds(34 + 4 * q, 2)].reshape(32, 128))
        res_re = jnp.concatenate(res_re, axis=0)
        res_im = jnp.concatenate(res_im, axis=0)
        left.append(jnp.concatenate([res_re, res_im], axis=0))
        left.append(jnp.concatenate([-res_im, res_re], axis=0))
        if ref is mine_ref:
            ere = [mine_ref[8 * half + i, 64:96, :] for i in range(8)]
            eim = [mine_ref[8 * half + i, 96:128, :] for i in range(8)]
            weights.append((omega_ref[...], damping_ref[...]))
        else:
            ere = [ref[4 * i : 4 * i + 2].reshape(32, 128) for i in range(8)]
            eim = [ref[4 * i + 2 : 4 * i + 4].reshape(32, 128) for i in range(8)]
            table = ref[48].astype(F32)
            weights.append((table[0:1] + table[1:2] + table[2:3], table[3:4] + table[4:5] + table[5:6]))
        excite.append((jnp.concatenate(ere, axis=0), jnp.concatenate(eim, axis=0)))
    left = jnp.concatenate(left, axis=1)
    for s in range(4):
        speed = speeds_ref[s]
        right = []
        for (ere, eim), (omega, damping) in zip(excite, weights):
            ere, eim = ere.astype(F32), eim.astype(F32)
            a = omega * omega - speed * speed
            b = 2.0 * damping * omega * speed
            denom = a * a + b * b
            wre = a / denom
            wim = -b / denom
            right.append((wre * ere - wim * eim).astype(BF))
            right.append((wre * eim + wim * ere).astype(BF))
        right = jnp.concatenate(right, axis=1)
        both = lax.dot_general(
            left, right, (((1,), (1,)), ((), ())), preferred_element_type=F32
        )
        for c in range(2):
            at = (2 * s + c) * 256
            for d in range(4):
                row = 128 * c + 32 * d
                out_refs[d][:, at : at + 256] = both[row : row + 32].astype(BF)


def sum_kernel(*refs):
    out_ref = refs[-1]
    for half in range(2):
        for s in range(4):
            for c in range(2):
                at = (2 * s + c) * 256
                total = refs[4 * half][:, at : at + 256].astype(F32)
                for n in range(1, 4):
                    total = total + refs[4 * half + n][:, at : at + 256].astype(F32)
                out_ref[:, 0, s, c, 256 * half : 256 * half + 256] = total


def shift(value, axis, d):
    if axis == 0:
        perm = [(4 * y + x, 4 * ((y + d) % 4) + x) for y in range(4) for x in range(4)]
    else:
        perm = [(4 * y + x, 4 * y + (x + d) % 4) for y in range(4) for x in range(4)]
    return lax.ppermute(value, "mode", perm)


def shards(shapes, pairs, omega, damping, speeds):
    sliced = call(
        slice_kernel, jax.ShapeDtypeStruct((16, 80, 128), BF), [VMEM, SMEM], "slice_rows"
    )(shapes, pairs)
    regions = lax.all_to_all(sliced, "group", 0, 0, tiled=True)
    picked = call(
        pick_kernel, jax.ShapeDtypeStruct((16, 128, 128), BF), [VMEM], "pick_regions"
    )(regions)
    mine = lax.all_to_all(picked, "group", 0, 0, tiled=True)
    omega, damping = omega.reshape(1, 128), damping.reshape(1, 128)
    message = jax.ShapeDtypeStruct((BLOCKS, 16, 128), BF)
    fanned = call(fan_kernel, (message,) * 6, [VMEM] * 3, "fan_out")(mine, omega, damping)
    got = [[shift(fanned[3 * half + n], half, d) for n, d in enumerate(ORDER)] for half in range(2)]
    terms = []
    for half in range(2):
        block = jax.ShapeDtypeStruct((32, 2048), BF)
        made = call(
            functools.partial(product_kernel, half),
            (block,) * 4,
            [VMEM] * 6 + [SMEM],
            "products_%d" % half,
            flops=2 * 256 * 1024 * 1024,
        )(mine, omega, damping, *got[half], speeds)
        terms += [made[0]] + [shift(made[d], 1 - half, d) for d in ORDER]
    return call(
        sum_kernel, jax.ShapeDtypeStruct((32, 1, 4, 2, 512), F32), [VMEM] * 8, "sum_terms"
    )(*terms)


def solution(mesh):
    in_specs = (P(None, "group", None, "mode"), P("group", None), P("mode"), P("mode"), P())
    out_specs = P("mode", "group", None, None, None)
    return jax.shard_map(shards, mesh=mesh, in_specs=in_specs, out_specs=out_specs, check_vma=False)
```

time: 89.3 us -> 77.5 us (0.87)
  the two profiles are of different devices: /device:TPU:6 before, /device:TPU:1 now
where the time goes in v2:
time: 77.5 us; the launch traced here: 77.3 us
  blocking collectives  42.9 us (55%)
  starting transfers between devices  21.2 us (27%)
  waiting for transfers between devices  6.21 us (8%)
  Pallas kernels  4.67 us (6%)
  local copies, waits for them, and re-layouts  2.28 us (3%)
    all_to_all x1, blocking collectives, shards(): regions = lax.all_to_all(sliced, 'group', 0, 0, tiled=True)  22.8 us
    ppermute x12, starting transfers between devices, shift(): return lax.ppermute(value, 'mode', perm)  21.2 us
    all_to_all x1, blocking collectives, shards(): mine = lax.all_to_all(picked, 'group', 0, 0, tiled=True)  20.1 us
    ppermute x12, waiting for transfers between devices, shift(): return lax.ppermute(value, 'mode', perm)  6.21 us
    pallas_call x2, Pallas kernels, shards(): call(functools.partial(product_kernel, half), (block,) * 4, [VMEM] * 6 +...  2.77 us
    unnamed x10, local copies, waits for them, and re-layouts  2.28 us
  transfers between devices with their start and end apart: 12, of which 4 were waited for; matrix products, arithmetic and copies ran while one was open for 0% of the time, Pallas kernels for 4%

profile of v2, /device:TPU:1, one launch (start us, length us, event | category | flops | bytes accessed | tf_op | source)
XLA Modules:
  0.0 77.3 jit_solution(14338517114070338164)
XLA Ops:
  0.0 0.0 copy-start
  0.0 0.9 %copy-done = bf16[2,1,512,128]{3,2,1,0:T(8,128)(2,1)S(1)} copy-done((bf16[2,1,512,128]{3,2,1,0:T(8,128)(2,1)S(1)}, bf16[2,1,512,128]{3,2,1,0:T(8,128)(2,1)}, u32[]{:S(2)}) %copy-start) | copy-done | bytes 262168
  1.0 0.0 copy-start.1
  1.0 0.7 copy-done.1
  1.6 0.6 slice_rows.1
  2.2 22.8 %all_to_all.10.all_ref = bf16[16,80,128]{2,1,0:T(8,128)(2,1)S(1)} all-to-all(bf16[16,80,128]{2,1,0:T(8,128)(2,1)S(1)} %slice_rows.1), channel_id=1, replica_groups=mesh['group'=16,'mode'=16] {'group'}, dimensions={0} | all-to-all | bytes 655360 | tf_op jit(solution)/shard_map/all_to_all | solution.py:167
  25.0 0.1 pick_regions.1
  25.1 20.1 %all_to_all.11.mine_ref = bf16[16,128,128]{2,1,0:T(8,128)(2,1)S(1)} all-to-all(bf16[16,128,128]{2,1,0:T(8,128)(2,1)S(1)} %pick_regions.1), channel_id=1, replica_groups=mesh['group'=16,'mode'=16] {'group'}, dimensions={0} | all-to-all | bytes 1048576 | tf_op jit(solution)/shard_map/all_to_all | solution.py:171
  45.2 0.0 copy-start.2
  45.2 0.0 copy-start.3
  45.2 0.7 copy-done.2
  45.9 0.0 copy-done.3
  45.9 0.1 fan_out.1
  46.0 3.0 %collective-permute-start = (bf16[49,16,128]{2,1,0:T(8,128)(2,1)S(1)}, bf16[49,16,128]{2,1,0:T(8,128)(2,1)S(1)}, u32[]{:S(2)}, u32[]{:S(2)}) collective-permute-start(bf16[49,16,128]{2,1,0:T(8,128)(2,1)S(1)} %get-tuple-element.19), channel_id=1, source_target_pairs={{0,8},{1,9},{2,10},{3,11},{4,12},{5,13},{6,14},{7,15},{8,0},{9,1},... | collective-permute-start | bytes 602120 | tf_op jit(solution)/shard_map/ppermute | solution.py:160
  49.0 0.4 collective-permute-start.1
  49.4 2.3 %collective-permute-start.2 = (bf16[49,16,128]{2,1,0:T(8,128)(2,1)S(1)}, bf16[49,16,128]{2,1,0:T(8,128)(2,1)S(1)}, u32[]{:S(2)}, u32[]{:S(2)}) collective-permute-start(bf16[49,16,128]{2,1,0:T(8,128)(2,1)S(1)} %get-tuple-element.21), channel_id=1, source_target_pairs={{0,12},{1,13},{2,14},{3,15},{4,0},{5,1},{6,2},{7,3},{8,4},{9,5},{1... | collective-permute-start | bytes 602120 | tf_op jit(solution)/shard_map/ppermute | solution.py:160
  51.7 2.7 %collective-permute-start.6 = (bf16[49,16,128]{2,1,0:T(8,128)(2,1)S(1)}, bf16[49,16,128]{2,1,0:T(8,128)(2,1)S(1)}, u32[]{:S(2)}, u32[]{:S(2)}) collective-permute-start(bf16[49,16,128]{2,1,0:T(8,128)(2,1)S(1)} %get-tuple-element.26), channel_id=1, source_target_pairs={{0,2},{1,3},{2,0},{3,1},{4,6},{5,7},{6,4},{7,5},{8,10},{9,11},{10,... | collective-permute-start | bytes 602120 | tf_op jit(solution)/shard_map/ppermute | solution.py:160
  54.4 0.0 copy-start.4
  54.4 0.3 collective-permute-start.7
  54.7 0.0 collective-permute-done.one_ref
  54.7 2.4 %collective-permute-start.8 = (bf16[49,16,128]{2,1,0:T(8,128)(2,1)S(1)}, bf16[49,16,128]{2,1,0:T(8,128)(2,1)S(1)}, u32[]{:S(2)}, u32[]{:S(2)}) collective-permute-start(bf16[49,16,128]{2,1,0:T(8,128)(2,1)S(1)} %get-tuple-element.28), channel_id=1, source_target_pairs={{0,3},{1,0},{2,1},{3,2},{4,7},{5,4},{6,5},{7,6},{8,11},{9,8},{10,9... | collective-permute-start | bytes 602120 | tf_op jit(solution)/shard_map/ppermute | solution.py:160
  57.1 1.1 %collective-permute-done.1.two_ref = bf16[49,16,128]{2,1,0:T(8,128)(2,1)S(1)} collective-permute-done((bf16[49,16,128]{2,1,0:T(8,128)(2,1)S(1)}, bf16[49,16,128]{2,1,0:T(8,128)(2,1)S(1)}, u32[]{:S(2)}, u32[]{:S(2)}) %collective-permute-start.1) | collective-permute-done | bytes 200736 | tf_op jit(solution)/shard_map/ppermute | solution.py:160
  58.2 0.3 collective-permute-done.2.three_ref
  58.5 0.0 copy-done.4
  58.5 1.4 %products_0.1 = (bf16[32,2048]{1,0:T(8,128)(2,1)S(1)}, bf16[32,2048]{1,0:T(8,128)(2,1)S(1)}, bf16[32,2048]{1,0:T(8,128)(2,1)S(1)}, bf16[32,2048]{1,0:T(8,128)(2,1)S(1)}) custom-call(bf16[16,128,128]{2,1,0:T(8,128)(2,1)S(1)} %all_to_all.11.mine_ref, f32[1,128]{1,0:T(1,128)S(1)} %bitcast.3, f32[1,128]{1,0:T(1,128)S(1)} %bitcast.6, ...), custom_call_target="tpu_custom_call" | custom-call | flops 536870912 | bytes 1048576 | tf_op jit(solution)/shard_map/products_0/pallas_call | solution.py:179
  59.9 2.8 %collective-permute-start.3 = (bf16[32,2048]{1,0:T(8,128)(2,1)S(1)}, bf16[32,2048]{1,0:T(8,128)(2,1)S(1)}, u32[]{:S(2)}, u32[]{:S(2)}) collective-permute-start(bf16[32,2048]{1,0:T(8,128)(2,1)S(1)} %get-tuple-element.23), channel_id=1, source_target_pairs={{0,2},{1,3},{2,0},{3,1},{4,6},{5,7},{6,4},{7,5},{8,10},{9,11},{10,... | collective-permute-start | bytes 393224 | tf_op jit(solution)/shard_map/ppermute | solution.py:160
  62.7 0.3 collective-permute-start.4
  63.0 0.0 collective-permute-done.6.one_ref
  63.1 2.4 %collective-permute-start.5 = (bf16[32,2048]{1,0:T(8,128)(2,1)S(1)}, bf16[32,2048]{1,0:T(8,128)(2,1)S(1)}, u32[]{:S(2)}, u32[]{:S(2)}) collective-permute-start(bf16[32,2048]{1,0:T(8,128)(2,1)S(1)} %get-tuple-element.25), channel_id=1, source_target_pairs={{0,3},{1,0},{2,1},{3,2},{4,7},{5,4},{6,5},{7,6},{8,11},{9,8},{10,9... | collective-permute-start | bytes 393224 | tf_op jit(solution)/shard_map/ppermute | solution.py:160
  65.4 0.0 collective-permute-done.7.two_ref
  65.4 0.0 collective-permute-done.8.three_ref
  65.4 1.4 %products_1.1 = (bf16[32,2048]{1,0:T(8,128)(2,1)S(1)}, bf16[32,2048]{1,0:T(8,128)(2,1)S(1)}, bf16[32,2048]{1,0:T(8,128)(2,1)S(1)}, bf16[32,2048]{1,0:T(8,128)(2,1)S(1)}) custom-call(bf16[16,128,128]{2,1,0:T(8,128)(2,1)S(1)} %all_to_all.11.mine_ref, f32[1,128]{1,0:T(1,128)S(1)} %bitcast.4, f32[1,128]{1,0:T(1,128)S(1)} %bitcast.7, ...), custom_call_target="tpu_custom_call" | custom-call | flops 536870912 | bytes 1048576 | tf_op jit(solution)/shard_map/products_1/pallas_call | solution.py:179
  66.8 1.9 %collective-permute-start.9 = (bf16[32,2048]{1,0:T(8,128)(2,1)S(1)}, bf16[32,2048]{1,0:T(8,128)(2,1)S(1)}, u32[]{:S(2)}, u32[]{:S(2)}) collective-permute-start(bf16[32,2048]{1,0:T(8,128)(2,1)S(1)} %get-tuple-element.30), channel_id=1, source_target_pairs={{0,8},{1,9},{2,10},{3,11},{4,12},{5,13},{6,14},{7,15},{8,0},{9,1},... | collective-permute-start | bytes 393224 | tf_op jit(solution)/shard_map/ppermute | solution.py:160
  68.7 1.1 %collective-permute-start.10 = (bf16[32,2048]{1,0:T(8,128)(2,1)S(1)}, bf16[32,2048]{1,0:T(8,128)(2,1)S(1)}, u32[]{:S(2)}, u32[]{:S(2)}) collective-permute-start(bf16[32,2048]{1,0:T(8,128)(2,1)S(1)} %get-tuple-element.31), channel_id=1, source_target_pairs={{0,4},{1,5},{2,6},{3,7},{4,8},{5,9},{6,10},{7,11},{8,12},{9,13},{1... | collective-permute-start | bytes 393224 | tf_op jit(solution)/shard_map/ppermute | solution.py:160
  69.9 0.0 collective-permute-done.3.refs_1_
  69.9 1.5 %collective-permute-start.11 = (bf16[32,2048]{1,0:T(8,128)(2,1)S(1)}, bf16[32,2048]{1,0:T(8,128)(2,1)S(1)}, u32[]{:S(2)}, u32[]{:S(2)}) collective-permute-start(bf16[32,2048]{1,0:T(8,128)(2,1)S(1)} %get-tuple-element.32), channel_id=1, source_target_pairs={{0,12},{1,13},{2,14},{3,15},{4,0},{5,1},{6,2},{7,3},{8,4},{9,5},{1... | collective-permute-start | bytes 393224 | tf_op jit(solution)/shard_map/ppermute | solution.py:160
  71.4 0.0 collective-permute-done.4.refs_2_
  71.4 0.0 collective-permute-done.5.refs_3_
  71.4 1.2 %collective-permute-done.9.refs_5_ = bf16[32,2048]{1,0:T(8,128)(2,1)S(1)} collective-permute-done((bf16[32,2048]{1,0:T(8,128)(2,1)S(1)}, bf16[32,2048]{1,0:T(8,128)(2,1)S(1)}, u32[]{:S(2)}, u32[]{:S(2)}) %collective-permute-start.9) | collective-permute-done | bytes 131104 | tf_op jit(solution)/shard_map/ppermute | solution.py:160
  72.6 3.6 %collective-permute-done.10.refs_6_ = bf16[32,2048]{1,0:T(8,128)(2,1)S(1)} collective-permute-done((bf16[32,2048]{1,0:T(8,128)(2,1)S(1)}, bf16[32,2048]{1,0:T(8,128)(2,1)S(1)}, u32[]{:S(2)}, u32[]{:S(2)}) %collective-permute-start.10) | collective-permute-done | bytes 131104 | tf_op jit(solution)/shard_map/ppermute | solution.py:160
  76.2 0.0 collective-permute-done.11.refs_7_
  76.2 1.1 %sum_terms.1 = f32[32,1,4,2,512]{4,3,2,1,0:T(2,128)} custom-call(bf16[32,2048]{1,0:T(8,128)(2,1)S(1)} %get-tuple-element.22.refs_0_, bf16[32,2048]{1,0:T(8,128)(2,1)S(1)} %collective-permute-done.3.refs_1_, bf16[32,2048]{1,0:T(8,128)(2,1)S(1)} %collective-permute-done.4.refs_2_, bf16[32,2048]{1,0:T(8,128)(2,1)S(1)} %collective-permute-done.5.refs_3_, ...), custom_call_target="tpu_custom_call" | custom-call | bytes 1048576 | tf_op jit(solution)/shard_map/sum_terms/pallas_call | solution.py:187
Async XLA Ops:
  0.0 0.9 %copy-start = (bf16[2,1,512,128]{3,2,1,0:T(8,128)(2,1)S(1)}, bf16[2,1,512,128]{3,2,1,0:T(8,128)(2,1)}, u32[]{:S(2)}) copy-start(bf16[2,1,512,128]{3,2,1,0:T(8,128)(2,1)} %shapes_ref.1) | copy-start | bytes 786436
  1.0 0.7 copy-start.1
  45.2 0.7 copy-start.2
  45.2 0.7 copy-start.3
  46.0 8.7 %collective-permute-start = (bf16[49,16,128]{2,1,0:T(8,128)(2,1)S(1)}, bf16[49,16,128]{2,1,0:T(8,128)(2,1)S(1)}, u32[]{:S(2)}, u32[]{:S(2)}) collective-permute-start(bf16[49,16,128]{2,1,0:T(8,128)(2,1)S(1)} %get-tuple-element.19), channel_id=1, source_target_pairs={{0,8},{1,9},{2,10},{3,11},{4,12},{5,13},{6,14},{7,15},{8,0},{9,1},... | collective-permute-start | bytes 602120 | tf_op jit(solution)/shard_map/ppermute | solution.py:160
  49.0 9.2 %collective-permute-start.1 = (bf16[49,16,128]{2,1,0:T(8,128)(2,1)S(1)}, bf16[49,16,128]{2,1,0:T(8,128)(2,1)S(1)}, u32[]{:S(2)}, u32[]{:S(2)}) collective-permute-start(bf16[49,16,128]{2,1,0:T(8,128)(2,1)S(1)} %get-tuple-element.20), channel_id=1, source_target_pairs={{0,4},{1,5},{2,6},{3,7},{4,8},{5,9},{6,10},{7,11},{8,12},{9,13},{1... | collective-permute-start | bytes 602120 | tf_op jit(solution)/shard_map/ppermute | solution.py:160
  49.4 9.1 %collective-permute-start.2 = (bf16[49,16,128]{2,1,0:T(8,128)(2,1)S(1)}, bf16[49,16,128]{2,1,0:T(8,128)(2,1)S(1)}, u32[]{:S(2)}, u32[]{:S(2)}) collective-permute-start(bf16[49,16,128]{2,1,0:T(8,128)(2,1)S(1)} %get-tuple-element.21), channel_id=1, source_target_pairs={{0,12},{1,13},{2,14},{3,15},{4,0},{5,1},{6,2},{7,3},{8,4},{9,5},{1... | collective-permute-start | bytes 602120 | tf_op jit(solution)/shard_map/ppermute | solution.py:160
  51.7 11.4 %collective-permute-start.6 = (bf16[49,16,128]{2,1,0:T(8,128)(2,1)S(1)}, bf16[49,16,128]{2,1,0:T(8,128)(2,1)S(1)}, u32[]{:S(2)}, u32[]{:S(2)}) collective-permute-start(bf16[49,16,128]{2,1,0:T(8,128)(2,1)S(1)} %get-tuple-element.26), channel_id=1, source_target_pairs={{0,2},{1,3},{2,0},{3,1},{4,6},{5,7},{6,4},{7,5},{8,10},{9,11},{10,... | collective-permute-start | bytes 602120 | tf_op jit(solution)/shard_map/ppermute | solution.py:160
  54.4 4.1 %copy-start.4 = (f32[4]{0:T(128)S(1)}, f32[4]{0:T(128)}, u32[]{:S(2)}) copy-start(f32[4]{0:T(128)} %speeds_ref.3) | copy-start | bytes 52
  54.4 11.0 %collective-permute-start.7 = (bf16[49,16,128]{2,1,0:T(8,128)(2,1)S(1)}, bf16[49,16,128]{2,1,0:T(8,128)(2,1)S(1)}, u32[]{:S(2)}, u32[]{:S(2)}) collective-permute-start(bf16[49,16,128]{2,1,0:T(8,128)(2,1)S(1)} %get-tuple-element.27), channel_id=1, source_target_pairs={{0,1},{1,2},{2,3},{3,0},{4,5},{5,6},{6,7},{7,4},{8,9},{9,10},{10,1... | collective-permute-start | bytes 602120 | tf_op jit(solution)/shard_map/ppermute | solution.py:160
  54.7 10.7 %collective-permute-start.8 = (bf16[49,16,128]{2,1,0:T(8,128)(2,1)S(1)}, bf16[49,16,128]{2,1,0:T(8,128)(2,1)S(1)}, u32[]{:S(2)}, u32[]{:S(2)}) collective-permute-start(bf16[49,16,128]{2,1,0:T(8,128)(2,1)S(1)} %get-tuple-element.28), channel_id=1, source_target_pairs={{0,3},{1,0},{2,1},{3,2},{4,7},{5,4},{6,5},{7,6},{8,11},{9,8},{10,9... | collective-permute-start | bytes 602120 | tf_op jit(solution)/shard_map/ppermute | solution.py:160
  59.9 10.0 %collective-permute-start.3 = (bf16[32,2048]{1,0:T(8,128)(2,1)S(1)}, bf16[32,2048]{1,0:T(8,128)(2,1)S(1)}, u32[]{:S(2)}, u32[]{:S(2)}) collective-permute-start(bf16[32,2048]{1,0:T(8,128)(2,1)S(1)} %get-tuple-element.23), channel_id=1, source_target_pairs={{0,2},{1,3},{2,0},{3,1},{4,6},{5,7},{6,4},{7,5},{8,10},{9,11},{10,... | collective-permute-start | bytes 393224 | tf_op jit(solution)/shard_map/ppermute | solution.py:160
  62.7 8.7 %collective-permute-start.4 = (bf16[32,2048]{1,0:T(8,128)(2,1)S(1)}, bf16[32,2048]{1,0:T(8,128)(2,1)S(1)}, u32[]{:S(2)}, u32[]{:S(2)}) collective-permute-start(bf16[32,2048]{1,0:T(8,128)(2,1)S(1)} %get-tuple-element.24), channel_id=1, source_target_pairs={{0,1},{1,2},{2,3},{3,0},{4,5},{5,6},{6,7},{7,4},{8,9},{9,10},{10,1... | collective-permute-start | bytes 393224 | tf_op jit(solution)/shard_map/ppermute | solution.py:160
  63.1 8.3 %collective-permute-start.5 = (bf16[32,2048]{1,0:T(8,128)(2,1)S(1)}, bf16[32,2048]{1,0:T(8,128)(2,1)S(1)}, u32[]{:S(2)}, u32[]{:S(2)}) collective-permute-start(bf16[32,2048]{1,0:T(8,128)(2,1)S(1)} %get-tuple-element.25), channel_id=1, source_target_pairs={{0,3},{1,0},{2,1},{3,2},{4,7},{5,4},{6,5},{7,6},{8,11},{9,8},{10,9... | collective-permute-start | bytes 393224 | tf_op jit(solution)/shard_map/ppermute | solution.py:160
  66.8 5.7 %collective-permute-start.9 = (bf16[32,2048]{1,0:T(8,128)(2,1)S(1)}, bf16[32,2048]{1,0:T(8,128)(2,1)S(1)}, u32[]{:S(2)}, u32[]{:S(2)}) collective-permute-start(bf16[32,2048]{1,0:T(8,128)(2,1)S(1)} %get-tuple-element.30), channel_id=1, source_target_pairs={{0,8},{1,9},{2,10},{3,11},{4,12},{5,13},{6,14},{7,15},{8,0},{9,1},... | collective-permute-start | bytes 393224 | tf_op jit(solution)/shard_map/ppermute | solution.py:160
  68.7 7.5 %collective-permute-start.10 = (bf16[32,2048]{1,0:T(8,128)(2,1)S(1)}, bf16[32,2048]{1,0:T(8,128)(2,1)S(1)}, u32[]{:S(2)}, u32[]{:S(2)}) collective-permute-start(bf16[32,2048]{1,0:T(8,128)(2,1)S(1)} %get-tuple-element.31), channel_id=1, source_target_pairs={{0,4},{1,5},{2,6},{3,7},{4,8},{5,9},{6,10},{7,11},{8,12},{9,13},{1... | collective-permute-start | bytes 393224 | tf_op jit(solution)/shard_map/ppermute | solution.py:160
  69.9 6.3 %collective-permute-start.11 = (bf16[32,2048]{1,0:T(8,128)(2,1)S(1)}, bf16[32,2048]{1,0:T(8,128)(2,1)S(1)}, u32[]{:S(2)}, u32[]{:S(2)}) collective-permute-start(bf16[32,2048]{1,0:T(8,128)(2,1)S(1)} %get-tuple-element.32), channel_id=1, source_target_pairs={{0,12},{1,13},{2,14},{3,15},{4,0},{5,1},{6,2},{7,3},{8,4},{9,5},{1... | collective-permute-start | bytes 393224 | tf_op jit(solution)/shard_map/ppermute | solution.py:160

commit v3 on v1

v3 whole, which is shorter than its diff:
```python
import jax
import jax.numpy as jnp
from jax import lax
from jax.experimental import pallas as pl
from jax.experimental.pallas import tpu as pltpu
from jax.sharding import PartitionSpec as P

BF = jnp.bfloat16
F32 = jnp.float32
VMEM = pl.BlockSpec(memory_space=pltpu.VMEM)
SMEM = pl.BlockSpec(memory_space=pltpu.SMEM)
PARAMS = pltpu.CompilerParams(vmem_limit_bytes=40 * 1024 * 1024)
EXCITE, RESPONSE, TABLE, ROWS = 0, 1024, 1280, 1296


def call(kernel, out_shape, in_specs, name, flops=0, size=1 << 20):
    many = isinstance(out_shape, tuple)
    return pl.pallas_call(
        kernel,
        out_shape=out_shape,
        in_specs=in_specs,
        out_specs=tuple(VMEM for _ in out_shape) if many else VMEM,
        compiler_params=PARAMS,
        cost_estimate=pl.CostEstimate(flops=flops, bytes_accessed=size, transcendentals=0),
        name=name,
    )


def partner(at, shifted):
    odd = at % 2
    return (at + 1 - 2 * (odd ^ shifted)) % 4


def peer(y, x, d, shifted):
    return (partner(y, shifted) if d & 2 else y), (partner(x, shifted) if d & 1 else x)


def slice_kernel(shapes_ref, pairs_ref, out_ref):
    rows = lax.broadcasted_iota(jnp.int32, (16, 128), 0)
    pair = jnp.where(rows < 8, pairs_ref[0, 0], pairs_ref[0, 1])
    pair = pair.astype(F32).astype(BF)
    for i in range(16):
        out_ref[i, 0:32, :] = shapes_ref[0, 0, 32 * i : 32 * i + 32, :]
        out_ref[i, 32:64, :] = shapes_ref[1, 0, 32 * i : 32 * i + 32, :]
        out_ref[i, 64:80, :] = pair


def pick_kernel(all_ref, out_ref):
    for g in range(16):
        pair = all_ref[g, 64:80, :].astype(F32)
        response = pair[0, 0].astype(jnp.int32)
        excite = pair[8, 0].astype(jnp.int32)
        out_ref[g, 0:64, :] = all_ref[response, 0:64, :]
        out_ref[g, 64:128, :] = all_ref[excite, 0:64, :]


def split3(x):
    first = x.astype(BF)
    rest = x - first.astype(F32)
    second = rest.astype(BF)
    third = (rest - second.astype(F32)).astype(BF)
    return first.astype(F32), second.astype(F32), third.astype(F32)


def fan_kernel(mine_ref, omega_ref, damping_ref, *out_refs):
    me = lax.axis_index("mode")
    core = lax.axis_index("group") % 2
    pieces = split3(omega_ref[...]) + split3(damping_ref[...])
    rows = lax.broadcasted_iota(jnp.int32, (16, 128), 0)
    table = jnp.zeros((16, 128), F32)
    for n, piece in enumerate(pieces):
        table = jnp.where(rows == n, piece, table)
    table = table.astype(BF)
    for d, out_ref in enumerate(out_refs):
        y, x = peer(me // 4, me % 4, d, core)
        for i in range(16):
            at = EXCITE + 32 * i
            out_ref[at : at + 32, :] = mine_ref[i, 64:96, :]
            out_ref[at + 512 : at + 544, :] = mine_ref[i, 96:128, :]
        for e in range(4):
            owner_y, owner_x = peer(y, x, e, 1 - core)
            owner = 4 * owner_y + owner_x
            at = RESPONSE + 32 * e
            out_ref[at : at + 32, :] = mine_ref[owner, 0:32, :]
            out_ref[at + 128 : at + 160, :] = mine_ref[owner, 32:64, :]
        out_ref[TABLE:ROWS, :] = table


def product_kernel(*refs):
    parts, speeds_ref, out_refs = refs[:4], refs[4], refs[5:]
    left, excite, weights = [], [], []
    for ref in parts:
        res_re = ref[RESPONSE : RESPONSE + 128, :]
        res_im = ref[RESPONSE + 128 : RESPONSE + 256, :]
        left.append(jnp.concatenate([res_re, res_im], axis=0))
        left.append(jnp.concatenate([-res_im, res_re], axis=0))
        table = ref[TABLE:ROWS, :].astype(F32)
        weights.append((table[0:1] + table[1:2] + table[2:3], table[3:4] + table[4:5] + table[5:6]))
    left = jnp.concatenate(left, axis=1)
    for s in range(4):
        speed = speeds_ref[s]
        right = []
        for ref, (omega, damping) in zip(parts, weights):
            ere = ref[EXCITE : EXCITE + 512, :].astype(F32)
            eim = ref[EXCITE + 512 : EXCITE + 1024, :].astype(F32)
            a = omega * omega - speed * speed
            b = 2.0 * damping * omega * speed
            denom = a * a + b * b
            wre = a / denom
            wim = -b / denom
            right.append((wre * ere - wim * eim).astype(BF))
            right.append((wre * eim + wim * ere).astype(BF))
        right = jnp.concatenate(right, axis=1)
        both = lax.dot_general(
            left, right, (((1,), (1,)), ((), ())), preferred_element_type=F32
        )
        for c in range(2):
            at = (2 * s + c) * 512
            for e in range(4):
                row = 128 * c + 32 * e
                out_refs[e][:, at : at + 512] = both[row : row + 32].astype(BF)


def sum_kernel(*refs):
    terms, out_ref = refs[:4], refs[4]
    for s in range(4):
        for c in range(2):
            at = (2 * s + c) * 512
            total = terms[0][:, at : at + 512].astype(F32)
            for ref in terms[1:]:
                total = total + ref[:, at : at + 512].astype(F32)
            out_ref[:, 0, s, c, :] = total


def exchange(value, d, flip):
    perm = []
    for g in range(16):
        for m in range(16):
            y, x = peer(m // 4, m % 4, d, (g % 2) ^ flip)
            perm.append((16 * g + m, 16 * g + 4 * y + x))
    return lax.ppermute(value, ("group", "mode"), perm)


def shards(shapes, pairs, omega, damping, speeds):
    sliced = call(
        slice_kernel, jax.ShapeDtypeStruct((16, 80, 128), BF), [VMEM, SMEM], "slice_rows"
    )(shapes, pairs)
    regions = lax.all_to_all(sliced, "group", 0, 0, tiled=True)
    picked = call(
        pick_kernel, jax.ShapeDtypeStruct((16, 128, 128), BF), [VMEM], "pick_regions"
    )(regions)
    mine = lax.all_to_all(picked, "group", 0, 0, tiled=True)
    omega, damping = omega.reshape(1, 128), damping.reshape(1, 128)
    message = jax.ShapeDtypeStruct((ROWS, 128), BF)
    fanned = call(fan_kernel, (message,) * 4, [VMEM] * 3, "fan_out")(mine, omega, damping)
    parts = [fanned[0]] + [exchange(fanned[d], d, 0) for d in (3, 1, 2)]
    block = jax.ShapeDtypeStruct((32, 4096), BF)
    made = call(
        product_kernel, (block,) * 4, [VMEM] * 4 + [SMEM], "products", flops=1 << 30
    )(*parts, speeds)
    terms = [made[0]] + [exchange(made[e], e, 1) for e in (3, 1, 2)]
    return call(
        sum_kernel, jax.ShapeDtypeStruct((32, 1, 4, 2, 512), F32), [VMEM] * 4, "sum_terms"
    )(*terms)


def solution(mesh):
    in_specs = (P(None, "group", None, "mode"), P("group", None), P("mode"), P("mode"), P())
    out_specs = P("mode", "group", None, None, None)
    return jax.shard_map(shards, mesh=mesh, in_specs=in_specs, out_specs=out_specs, check_vma=False)
```

time: 89.3 us -> 72.6 us (0.81); the launches traced: 87.7 us -> 72 us
  blocking collectives: 81.5 us -> 40.2 us
  waiting for transfers between devices: 0 us -> 15.4 us
  starting transfers between devices: 0 us -> 9.57 us
    all_to_all x2 -> x0, blocking collectives: 41.3 us -> none  [the longest x1 23.4 us: shards(): lax.all_to_all(fanned, 'mode', 0, 0, tiled=True, axis_index_groups=along_y)]
    ppermute x0 -> x6, waiting for transfers between devices: none -> 15.4 us  [exchange(): return lax.ppermute(value, ('group', 'mode'), perm)]
    ppermute x0 -> x6, starting transfers between devices: none -> 9.57 us  [exchange(): return lax.ppermute(value, ('group', 'mode'), perm)]
  transfers between devices with their start and end apart: 0 -> 6, of which waited for: 0 -> 5; matrix products, arithmetic and copies ran while one was open for 0% -> 0% of each run, Pallas kernels for 0% -> 0%
where the time goes in v3:
time: 72.6 us; the launch traced here: 72 us
  blocking collectives  40.2 us (55%)
  waiting for transfers between devices  15.4 us (21%)
  starting transfers between devices  9.57 us (13%)
  Pallas kernels  4.52 us (6%)
  local copies, waits for them, and re-layouts  2.28 us (3%)
    all_to_all x1, blocking collectives, shards(): regions = lax.all_to_all(sliced, 'group', 0, 0, tiled=True)  20.8 us
    all_to_all x1, blocking collectives, shards(): mine = lax.all_to_all(picked, 'group', 0, 0, tiled=True)  19.4 us
    ppermute x6, waiting for transfers between devices, exchange(): return lax.ppermute(value, ('group', 'mode'), perm)  15.4 us
    ppermute x6, starting transfers between devices, exchange(): return lax.ppermute(value, ('group', 'mode'), perm)  9.57 us
    pallas_call x1, Pallas kernels, shards(): call(product_kernel, (block,) * 4, [VMEM] * 4 + [SMEM], 'products', flops...  2.66 us
    unnamed x10, local copies, waits for them, and re-layouts  2.28 us
  transfers between devices with their start and end apart: 6, of which 5 were waited for; matrix products, arithmetic and copies ran while one was open for 0% of the time, Pallas kernels for 0%

profile of v3, /device:TPU:6, one launch (start us, length us, event | category | flops | bytes accessed | tf_op | source)
XLA Modules:
  0.0 72.0 jit_solution(6532730643415675075)
XLA Ops:
  0.0 0.0 copy-start
  0.0 0.9 %copy-done = bf16[2,1,512,128]{3,2,1,0:T(8,128)(2,1)S(1)} copy-done((bf16[2,1,512,128]{3,2,1,0:T(8,128)(2,1)S(1)}, bf16[2,1,512,128]{3,2,1,0:T(8,128)(2,1)}, u32[]{:S(2)}) %copy-start) | copy-done | bytes 262168
  1.0 0.0 copy-start.1
  1.0 0.7 copy-done.1
  1.6 0.6 slice_rows.1
  2.2 20.8 %all_to_all.10.all_ref = bf16[16,80,128]{2,1,0:T(8,128)(2,1)S(1)} all-to-all(bf16[16,80,128]{2,1,0:T(8,128)(2,1)S(1)} %slice_rows.1), channel_id=1, replica_groups=mesh['group'=16,'mode'=16] {'group'}, dimensions={0} | all-to-all | bytes 655360 | tf_op jit(solution)/shard_map/all_to_all | solution.py:148
  22.9 0.1 pick_regions.1
  23.1 19.4 %all_to_all.11.mine_ref = bf16[16,128,128]{2,1,0:T(8,128)(2,1)S(1)} all-to-all(bf16[16,128,128]{2,1,0:T(8,128)(2,1)S(1)} %pick_regions.1), channel_id=1, replica_groups=mesh['group'=16,'mode'=16] {'group'}, dimensions={0} | all-to-all | bytes 1048576 | tf_op jit(solution)/shard_map/all_to_all | solution.py:152
  42.5 0.0 copy-start.2
  42.5 0.0 copy-start.3
  42.5 0.7 copy-done.2
  43.2 0.0 copy-done.3
  43.2 0.2 fan_out.1
  43.3 1.9 %collective-permute-start = (bf16[1296,128]{1,0:T(8,128)(2,1)S(1)}, bf16[1296,128]{1,0:T(8,128)(2,1)S(1)}, u32[]{:S(2)}, u32[]{:S(2)}) collective-permute-start(bf16[1296,128]{1,0:T(8,128)(2,1)S(1)} %get-tuple-element.14), channel_id=1, source_target_pairs={{0,5},{1,4},{2,7},{3,6},{4,1},{5,0},{6,3},{7,2},{8,13},{9,12},{10,... | collective-permute-start | bytes 995336 | tf_op jit(solution)/shard_map/ppermute | solution.py:141
  45.3 1.2 %collective-permute-start.1 = (bf16[1296,128]{1,0:T(8,128)(2,1)S(1)}, bf16[1296,128]{1,0:T(8,128)(2,1)S(1)}, u32[]{:S(2)}, u32[]{:S(2)}) collective-permute-start(bf16[1296,128]{1,0:T(8,128)(2,1)S(1)} %get-tuple-element.15), channel_id=1, source_target_pairs={{0,1},{1,0},{2,3},{3,2},{4,5},{5,4},{6,7},{7,6},{8,9},{9,8},{10,11... | collective-permute-start | bytes 995336 | tf_op jit(solution)/shard_map/ppermute | solution.py:141
  46.5 0.0 copy-start.4
  46.5 0.4 collective-permute-start.2
  46.9 4.6 %collective-permute-done.refs_1_ = bf16[1296,128]{1,0:T(8,128)(2,1)S(1)} collective-permute-done((bf16[1296,128]{1,0:T(8,128)(2,1)S(1)}, bf16[1296,128]{1,0:T(8,128)(2,1)S(1)}, u32[]{:S(2)}, u32[]{:S(2)}) %collective-permute-start) | collective-permute-done | bytes 331808 | tf_op jit(solution)/shard_map/ppermute | solution.py:141
  51.6 3.6 %collective-permute-done.1.refs_2_ = bf16[1296,128]{1,0:T(8,128)(2,1)S(1)} collective-permute-done((bf16[1296,128]{1,0:T(8,128)(2,1)S(1)}, bf16[1296,128]{1,0:T(8,128)(2,1)S(1)}, u32[]{:S(2)}, u32[]{:S(2)}) %collective-permute-start.1) | collective-permute-done | bytes 331808 | tf_op jit(solution)/shard_map/ppermute | solution.py:141
  55.2 0.0 collective-permute-done.2.refs_3_
  55.2 0.0 copy-done.4
  55.2 2.7 %products.1 = (bf16[32,4096]{1,0:T(8,128)(2,1)S(1)}, bf16[32,4096]{1,0:T(8,128)(2,1)S(1)}, bf16[32,4096]{1,0:T(8,128)(2,1)S(1)}, bf16[32,4096]{1,0:T(8,128)(2,1)S(1)}) custom-call(bf16[1296,128]{1,0:T(8,128)(2,1)S(1)} %get-tuple-element.13.refs_0_, bf16[1296,128]{1,0:T(8,128)(2,1)S(1)} %collective-permute-done.refs_1_, ...), custom_call_target="tpu_custom_call" | custom-call | flops 1073741824 | bytes 1048576 | tf_op jit(solution)/shard_map/products/pallas_call | solution.py:158
  57.8 2.9 %collective-permute-start.3 = (bf16[32,4096]{1,0:T(8,128)(2,1)S(1)}, bf16[32,4096]{1,0:T(8,128)(2,1)S(1)}, u32[]{:S(2)}, u32[]{:S(2)}) collective-permute-start(bf16[32,4096]{1,0:T(8,128)(2,1)S(1)} %get-tuple-element.18), channel_id=1, source_target_pairs={{0,15},{1,14},{2,13},{3,12},{4,11},{5,10},{6,9},{7,8},{8,7},{9,6},... | collective-permute-start | bytes 786440 | tf_op jit(solution)/shard_map/ppermute | solution.py:141
  60.7 2.7 %collective-permute-start.4 = (bf16[32,4096]{1,0:T(8,128)(2,1)S(1)}, bf16[32,4096]{1,0:T(8,128)(2,1)S(1)}, u32[]{:S(2)}, u32[]{:S(2)}) collective-permute-start(bf16[32,4096]{1,0:T(8,128)(2,1)S(1)} %get-tuple-element.19), channel_id=1, source_target_pairs={{0,3},{1,2},{2,1},{3,0},{4,7},{5,6},{6,5},{7,4},{8,11},{9,10},{10,... | collective-permute-start | bytes 786440 | tf_op jit(solution)/shard_map/ppermute | solution.py:141
  63.4 0.4 collective-permute-start.5
  63.8 3.8 %collective-permute-done.3.refs_1_ = bf16[32,4096]{1,0:T(8,128)(2,1)S(1)} collective-permute-done((bf16[32,4096]{1,0:T(8,128)(2,1)S(1)}, bf16[32,4096]{1,0:T(8,128)(2,1)S(1)}, u32[]{:S(2)}, u32[]{:S(2)}) %collective-permute-start.3) | collective-permute-done | bytes 262176 | tf_op jit(solution)/shard_map/ppermute | solution.py:141
  67.6 3.0 %collective-permute-done.4.refs_2_ = bf16[32,4096]{1,0:T(8,128)(2,1)S(1)} collective-permute-done((bf16[32,4096]{1,0:T(8,128)(2,1)S(1)}, bf16[32,4096]{1,0:T(8,128)(2,1)S(1)}, u32[]{:S(2)}, u32[]{:S(2)}) %collective-permute-start.4) | collective-permute-done | bytes 262176 | tf_op jit(solution)/shard_map/ppermute | solution.py:141
  70.6 0.4 collective-permute-done.5.refs_3_
  71.0 1.0 %sum_terms.1 = f32[32,1,4,2,512]{4,3,2,1,0:T(2,128)} custom-call(bf16[32,4096]{1,0:T(8,128)(2,1)S(1)} %get-tuple-element.17.refs_0_, bf16[32,4096]{1,0:T(8,128)(2,1)S(1)} %collective-permute-done.3.refs_1_, bf16[32,4096]{1,0:T(8,128)(2,1)S(1)} %collective-permute-done.4.refs_2_, bf16[32,4096]{1,0:T(8,128)(2,1)S(1)} %collective-permute-done.5.refs_3_), custom_call_target="tpu_custom_call" | custom-call | bytes 1048576 | tf_op jit(solution)/shard_map/sum_terms/pallas_call | solution.py:162
Async XLA Ops:
  0.0 0.9 %copy-start = (bf16[2,1,512,128]{3,2,1,0:T(8,128)(2,1)S(1)}, bf16[2,1,512,128]{3,2,1,0:T(8,128)(2,1)}, u32[]{:S(2)}) copy-start(bf16[2,1,512,128]{3,2,1,0:T(8,128)(2,1)} %shapes_ref.1) | copy-start | bytes 786436
  1.0 0.7 copy-start.1
  42.5 0.7 copy-start.2
  42.5 0.7 copy-start.3
  43.3 8.2 %collective-permute-start = (bf16[1296,128]{1,0:T(8,128)(2,1)S(1)}, bf16[1296,128]{1,0:T(8,128)(2,1)S(1)}, u32[]{:S(2)}, u32[]{:S(2)}) collective-permute-start(bf16[1296,128]{1,0:T(8,128)(2,1)S(1)} %get-tuple-element.14), channel_id=1, source_target_pairs={{0,5},{1,4},{2,7},{3,6},{4,1},{5,0},{6,3},{7,2},{8,13},{9,12},{10,... | collective-permute-start | bytes 995336 | tf_op jit(solution)/shard_map/ppermute | solution.py:141
  45.3 9.9 %collective-permute-start.1 = (bf16[1296,128]{1,0:T(8,128)(2,1)S(1)}, bf16[1296,128]{1,0:T(8,128)(2,1)S(1)}, u32[]{:S(2)}, u32[]{:S(2)}) collective-permute-start(bf16[1296,128]{1,0:T(8,128)(2,1)S(1)} %get-tuple-element.15), channel_id=1, source_target_pairs={{0,1},{1,0},{2,3},{3,2},{4,5},{5,4},{6,7},{7,6},{8,9},{9,8},{10,11... | collective-permute-start | bytes 995336 | tf_op jit(solution)/shard_map/ppermute | solution.py:141
  46.5 8.7 %copy-start.4 = (f32[4]{0:T(128)S(1)}, f32[4]{0:T(128)}, u32[]{:S(2)}) copy-start(f32[4]{0:T(128)} %refs_4_.1) | copy-start | bytes 52
  46.5 8.7 %collective-permute-start.2 = (bf16[1296,128]{1,0:T(8,128)(2,1)S(1)}, bf16[1296,128]{1,0:T(8,128)(2,1)S(1)}, u32[]{:S(2)}, u32[]{:S(2)}) collective-permute-start(bf16[1296,128]{1,0:T(8,128)(2,1)S(1)} %get-tuple-element.16), channel_id=1, source_target_pairs={{0,4},{1,5},{2,6},{3,7},{4,0},{5,1},{6,2},{7,3},{8,12},{9,13},{10,... | collective-permute-start | bytes 995336 | tf_op jit(solution)/shard_map/ppermute | solution.py:141
  57.8 9.8 %collective-permute-start.3 = (bf16[32,4096]{1,0:T(8,128)(2,1)S(1)}, bf16[32,4096]{1,0:T(8,128)(2,1)S(1)}, u32[]{:S(2)}, u32[]{:S(2)}) collective-permute-start(bf16[32,4096]{1,0:T(8,128)(2,1)S(1)} %get-tuple-element.18), channel_id=1, source_target_pairs={{0,15},{1,14},{2,13},{3,12},{4,11},{5,10},{6,9},{7,8},{8,7},{9,6},... | collective-permute-start | bytes 786440 | tf_op jit(solution)/shard_map/ppermute | solution.py:141
  60.7 9.9 %collective-permute-start.4 = (bf16[32,4096]{1,0:T(8,128)(2,1)S(1)}, bf16[32,4096]{1,0:T(8,128)(2,1)S(1)}, u32[]{:S(2)}, u32[]{:S(2)}) collective-permute-start(bf16[32,4096]{1,0:T(8,128)(2,1)S(1)} %get-tuple-element.19), channel_id=1, source_target_pairs={{0,3},{1,2},{2,1},{3,0},{4,7},{5,6},{6,5},{7,4},{8,11},{9,10},{10,... | collective-permute-start | bytes 786440 | tf_op jit(solution)/shard_map/ppermute | solution.py:141
  63.4 7.6 %collective-permute-start.5 = (bf16[32,4096]{1,0:T(8,128)(2,1)S(1)}, bf16[32,4096]{1,0:T(8,128)(2,1)S(1)}, u32[]{:S(2)}, u32[]{:S(2)}) collective-permute-start(bf16[32,4096]{1,0:T(8,128)(2,1)S(1)} %get-tuple-element.20), channel_id=1, source_target_pairs={{0,12},{1,13},{2,14},{3,15},{4,8},{5,9},{6,10},{7,11},{8,4},{9,5},... | collective-permute-start | bytes 786440 | tf_op jit(solution)/shard_map/ppermute | solution.py:141

commit v4 on v3

v4 whole, which is shorter than its diff:
```python
import jax
import jax.numpy as jnp
from jax import lax
from jax.experimental import pallas as pl
from jax.experimental.pallas import tpu as pltpu
from jax.sharding import PartitionSpec as P

BF = jnp.bfloat16
F32 = jnp.float32
VMEM = pl.BlockSpec(memory_space=pltpu.VMEM)
SMEM = pl.BlockSpec(memory_space=pltpu.SMEM)
HBM = pl.BlockSpec(memory_space=pltpu.HBM)
PARAMS = pltpu.CompilerParams(vmem_limit_bytes=40 * 1024 * 1024)
EXCITE, RESPONSE, TABLE, ROWS = 0, 1024, 1280, 1296


def call(kernel, out_shape, in_specs, name, flops=0, size=1 << 20, scratch=(), aliases=None, params=PARAMS, out_spec=VMEM):
    many = isinstance(out_shape, tuple)
    return pl.pallas_call(
        kernel,
        out_shape=out_shape,
        in_specs=in_specs,
        out_specs=tuple(out_spec for _ in out_shape) if many else out_spec,
        scratch_shapes=list(scratch),
        input_output_aliases=aliases or {},
        compiler_params=params,
        cost_estimate=pl.CostEstimate(flops=flops, bytes_accessed=size, transcendentals=0),
        name=name,
    )


def partner(at, shifted):
    odd = at % 2
    return (at + 1 - 2 * (odd ^ shifted)) % 4


def peer(y, x, d, shifted):
    return (partner(y, shifted) if d & 2 else y), (partner(x, shifted) if d & 1 else x)


def locate(region, me):
    core = me % 2
    below = (me // 2 - region // 2) % 8
    steps = jnp.where(core == 0, below, (8 - below) % 8)
    same = region % 2 == core
    slot = jnp.where(same, steps, jnp.where(steps == 0, 8, 4 + steps))
    return jnp.where(slot < 8, jnp.where(steps > 4, 8, slot), 8)


def prepare_kernel(shapes_ref, omega_ref, damping_ref, own_ref, table_ref):
    own_ref[...] = shapes_ref[:, 0]
    pieces = split3(omega_ref[...]) + split3(damping_ref[...])
    rows = lax.broadcasted_iota(jnp.int32, (16, 128), 0)
    table = jnp.zeros((16, 128), F32)
    for n, piece in enumerate(pieces):
        table = jnp.where(rows == n, piece, table)
    table_ref[...] = table.astype(BF)


def pick_kernel(pair_ref, *refs):
    regions, out_ref = refs[:8], refs[8]
    me = lax.axis_index("group")
    for n in range(2):
        slot = locate(pair_ref[0, n], me)
        for k, ref in enumerate(regions):

            @pl.when(slot == k)
            def _(ref=ref):
                out_ref[n] = ref[...]


def split3(x):
    first = x.astype(BF)
    rest = x - first.astype(F32)
    second = rest.astype(BF)
    third = (rest - second.astype(F32)).astype(BF)
    return first.astype(F32), second.astype(F32), third.astype(F32)


def fan_kernel(pair_ref, table_ref, *refs):
    regions, other_ref, out_refs, picked_ref = refs[:8], refs[8], refs[9:13], refs[13]
    me = lax.axis_index("group")
    for n in range(2):
        slot = locate(pair_ref[0, n], me)
        for k, ref in enumerate(regions):

            @pl.when(slot == k)
            def _(ref=ref):
                picked_ref[n] = ref[...]

        @pl.when(slot == 8)
        def _():
            picked_ref[n] = other_ref[n]

    core = me % 2
    at_mode = lax.axis_index("mode")
    for d, out_ref in enumerate(out_refs):
        y, x = peer(at_mode // 4, at_mode % 4, d, core)
        out_ref[EXCITE : EXCITE + 512, :] = picked_ref[1, 0]
        out_ref[EXCITE + 512 : EXCITE + 1024, :] = picked_ref[1, 1]
        for e in range(4):
            owner_y, owner_x = peer(y, x, e, 1 - core)
            owned = pl.ds(pl.multiple_of(32 * (4 * owner_y + owner_x), 32), 32)
            at = RESPONSE + 32 * e
            out_ref[at : at + 32, :] = picked_ref[0, 0, owned, :]
            out_ref[at + 128 : at + 160, :] = picked_ref[0, 1, owned, :]
        out_ref[TABLE:ROWS, :] = table_ref[...]


def share(parts, speeds_ref):
    left, modes = [], []
    for ref in parts:
        res_re = ref[RESPONSE : RESPONSE + 128, :]
        res_im = ref[RESPONSE + 128 : RESPONSE + 256, :]
        left.append(jnp.concatenate([res_re, res_im], axis=0))
        left.append(jnp.concatenate([-res_im, res_re], axis=0))
        table = ref[TABLE:ROWS, :].astype(F32)
        modes.append((table[0:1] + table[1:2] + table[2:3], table[3:4] + table[4:5] + table[5:6]))
    left = jnp.concatenate(left, axis=1)
    for s in range(4):
        speed = speeds_ref[s]
        right = []
        for ref, (omega, damping) in zip(parts, modes):
            ere = ref[EXCITE : EXCITE + 512, :].astype(F32)
            eim = ref[EXCITE + 512 : EXCITE + 1024, :].astype(F32)
            a = omega * omega - speed * speed
            b = 2.0 * damping * omega * speed
            denom = a * a + b * b
            wre = a / denom
            wim = -b / denom
            right.append((wre * ere - wim * eim).astype(BF))
            right.append((wre * eim + wim * ere).astype(BF))
        right = jnp.concatenate(right, axis=1)
        yield s, lax.dot_general(
            left, right, (((1,), (1,)), ((), ())), preferred_element_type=F32
        )


def first_kernel(part_ref, speeds_ref, out_ref):
    for s, both in share([part_ref], speeds_ref):
        out_ref[s] = both


def next_kernel(total_ref, part_ref, speeds_ref, out_ref):
    for s, both in share([part_ref], speeds_ref):
        out_ref[s] = total_ref[s] + both


def last_kernel(total_ref, part_ref, other_ref, speeds_ref, own_ref, *out_refs):
    for s, both in share([part_ref, other_ref], speeds_ref):
        both = total_ref[s] + both
        for c in range(2):
            at = (2 * s + c) * 512
            own_ref[:, at : at + 512] = both[128 * c : 128 * c + 32]
            for e in range(1, 4):
                row = 128 * c + 32 * e
                out_refs[e - 1][:, at : at + 512] = both[row : row + 32].astype(BF)


def sum_kernel(*refs):
    terms, out_ref = refs[:4], refs[4]
    for s in range(4):
        for c in range(2):
            at = (2 * s + c) * 512
            total = terms[0][:, at : at + 512]
            for ref in terms[1:]:
                total = total + ref[:, at : at + 512].astype(F32)
            out_ref[:, 0, s, c, :] = total


def exchange(value, d, flip):
    perm = []
    for g in range(16):
        for m in range(16):
            y, x = peer(m // 4, m % 4, d, (g % 2) ^ flip)
            perm.append((16 * g + m, 16 * g + 4 * y + x))
    return lax.ppermute(value, ("group", "mode"), perm)


def along_z(value, crossing=False):
    perm = []
    for g in range(16):
        core = g % 2 ^ crossing
        perm.append((g, 2 * ((g // 2 + 1 - 2 * core) % 8) + core))
    return lax.ppermute(value, "group", perm)


def swap_cores(value):
    return lax.ppermute(value, "group", [(g, g ^ 1) for g in range(16)])


def shards(shapes, pairs, omega, damping, speeds):
    a1 = along_z(shapes.reshape(2, 512, 128))
    own, table = call(
        prepare_kernel,
        (jax.ShapeDtypeStruct((2, 512, 128), BF), jax.ShapeDtypeStruct((16, 128), BF)),
        [VMEM] * 3,
        "prepare",
    )(shapes, omega.reshape(1, 128), damping.reshape(1, 128))
    b1 = along_z(own, crossing=True)
    a1, other_pair = lax.optimization_barrier((a1, swap_cores(pairs)))
    a2 = along_z(a1)
    b2 = along_z(b1)
    a3 = along_z(a2)
    b3 = along_z(b2)
    a4 = along_z(a3)
    regions = (own, a1, a2, a3, a4, b1, b2, b3)
    other = jax.ShapeDtypeStruct((2, 2, 512, 128), BF)
    wanted = call(pick_kernel, other, [SMEM] + [VMEM] * 8, "pick_regions")(other_pair, *regions)
    message = jax.ShapeDtypeStruct((ROWS, 128), BF)
    fanned = call(
        fan_kernel,
        (message,) * 4,
        [SMEM] + [VMEM] * 10,
        "fan_out",
        scratch=[pltpu.VMEM((2, 2, 512, 128), BF)],
    )(pairs, table, *regions, swap_cores(wanted))
    parts = [fanned[0]] + [exchange(fanned[d], d, 0) for d in (3, 1, 2)]
    sums = jax.ShapeDtypeStruct((4, 256, 512), F32)
    total = call(first_kernel, sums, [VMEM, SMEM], "product_0", flops=1 << 28)(parts[0], speeds)
    total = call(
        next_kernel, sums, [VMEM, VMEM, SMEM], "product_1", flops=1 << 28, aliases={0: 0}
    )(total, parts[1], speeds)
    block = jax.ShapeDtypeStruct((32, 4096), BF)
    made = call(
        last_kernel,
        (jax.ShapeDtypeStruct((32, 4096), F32), block, block, block),
        [VMEM, VMEM, VMEM, SMEM],
        "product_2",
        flops=1 << 29,
    )(total, parts[2], parts[3], speeds)
    terms = [made[0]] + [exchange(made[e], e, 1) for e in (3, 1, 2)]
    return call(
        sum_kernel, jax.ShapeDtypeStruct((32, 1, 4, 2, 512), F32), [VMEM] * 4, "sum_terms"
    )(*terms)


def solution(mesh):
    in_specs = (P(None, "group", None, "mode"), P("group", None), P("mode"), P("mode"), P())
    out_specs = P("mode", "group", None, None, None)
    return jax.shard_map(shards, mesh=mesh, in_specs=in_specs, out_specs=out_specs, check_vma=False)
```

time: 72.6 us -> 64.7 us (0.89)
  blocking collectives: 40.2 us -> 0 us
  waiting for transfers between devices: 15.4 us -> 38.7 us
  starting transfers between devices: 9.57 us -> 16.6 us
  Pallas kernels: 4.52 us -> 6.87 us
    all_to_all x2 -> x0, blocking collectives: 40.2 us -> none  [the longest x1 20.8 us: shards(): regions = lax.all_to_all(sliced, 'group', 0, 0, tiled=True)]
    ppermute x0 -> x9, waiting for transfers between devices: none -> 25.8 us  [the longest x7 23.9 us: along_z(): return lax.ppermute(value, 'group', perm)]
    ppermute x0 -> x9, starting transfers between devices: none -> 7.03 us  [the longest x2 3.59 us: swap_cores(): return lax.ppermute(value, 'group', [(g, g ^ 1) for g in range(16)])]
    ppermute x6, waiting for transfers between devices: 15.4 us -> 12.9 us  [exchange(): return lax.ppermute(value, ('group', 'mode'), perm)]
    pallas_call x4 -> x6, Pallas kernels: 3.51 us -> 5.86 us  [the longest x1 1.74 us: shards(): call(last_kernel, (jax.ShapeDtypeStruct((32, 4096), F32), block, block, b...]
  transfers between devices with their start and end apart: 6 -> 15, of which waited for: 5 -> 13; matrix products, arithmetic and copies ran while one was open for 0% -> 0% of each run, Pallas kernels for 0% -> 4%
where the time goes in v4:
time: 64.7 us; the launch traced here: 64.5 us
  waiting for transfers between devices  38.7 us (60%)
  starting transfers between devices  16.6 us (26%)
  Pallas kernels  6.87 us (11%)
  local copies, waits for them, and re-layouts  2.27 us (4%)
    ppermute x7, waiting for transfers between devices, along_z(): return lax.ppermute(value, 'group', perm)  23.9 us
    ppermute x6, waiting for transfers between devices, exchange(): return lax.ppermute(value, ('group', 'mode'), perm)  12.9 us
    ppermute x6, starting transfers between devices, exchange(): return lax.ppermute(value, ('group', 'mode'), perm)  9.57 us
    ppermute x2, starting transfers between devices, swap_cores(): return lax.ppermute(value, 'group', [(g, g ^ 1) for g in range(16)])  3.59 us
    ppermute x7, starting transfers between devices, along_z(): return lax.ppermute(value, 'group', perm)  3.44 us
    unnamed x10, local copies, waits for them, and re-layouts  2.27 us
    ppermute x2, waiting for transfers between devices, swap_cores(): return lax.ppermute(value, 'group', [(g, g ^ 1) for g in range(16)])  1.9 us
    pallas_call x1, Pallas kernels, shards(): call(last_kernel, (jax.ShapeDtypeStruct((32, 4096), F32), block, block, b...  1.74 us
  transfers between devices with their start and end apart: 15, of which 13 were waited for; matrix products, arithmetic and copies ran while one was open for 0% of the time, Pallas kernels for 4%

profile of v4, /device:TPU:6, one launch (start us, length us, event | category | flops | bytes accessed | tf_op | source)
XLA Modules:
  0.0 64.5 jit_solution(5736787209160279008)
XLA Ops:
  0.0 0.0 copy-start.4
  0.0 1.9 %collective-permute-start = (bf16[2,512,128]{2,1,0:T(8,128)(2,1)}, bf16[2,512,128]{2,1,0:T(8,128)(2,1)S(1)}, u32[]{:S(2)}, u32[]{:S(2)}) collective-permute-start(bf16[2,512,128]{2,1,0:T(8,128)(2,1)} %bitcast.3), channel_id=1, source_target_pairs={{0,32},{16,240},{32,64},{48,16},{64,96},{80,48},{96,128},{112,80},... | collective-permute-start | bytes 786440 | tf_op jit(solution)/shard_map/ppermute | solution.py:185
  1.9 3.5 %collective-permute-start.1 = (s32[1,2]{1,0:T(1,128)}, s32[1,2]{1,0:T(1,128)S(1)}, u32[]{:S(2)}, u32[]{:S(2)}) collective-permute-start(s32[1,2]{1,0:T(1,128)} %pair_ref.1), channel_id=1, source_target_pairs={{0,16},{16,0},{32,48},{48,32},{64,80},{80,64},{96,112},{112,96},{1... | collective-permute-start | bytes 32 | tf_op jit(solution)/shard_map/ppermute | solution.py:189
  5.4 0.0 copy-start
  5.4 0.9 %copy-done = bf16[2,1,512,128]{3,2,1,0:T(8,128)(2,1)S(1)} copy-done((bf16[2,1,512,128]{3,2,1,0:T(8,128)(2,1)S(1)}, bf16[2,1,512,128]{3,2,1,0:T(8,128)(2,1)}, u32[]{:S(2)}) %copy-start) | copy-done | bytes 262168
  6.4 0.0 copy-start.2
  6.4 0.7 %copy-done.2 = f32[128]{0:T(128)S(1)} copy-done((f32[128]{0:T(128)S(1)}, f32[128]{0:T(128)}, u32[]{:S(2)}) %copy-start.2) | copy-done | bytes 536
  7.0 0.0 copy-start.3
  7.0 0.7 %copy-done.3 = f32[128]{0:T(128)S(1)} copy-done((f32[128]{0:T(128)S(1)}, f32[128]{0:T(128)}, u32[]{:S(2)}) %copy-start.3) | copy-done | bytes 536
  7.7 0.0 copy-start.1
  7.7 0.7 %collective-permute-start.5 = (bf16[2,512,128]{2,1,0:T(8,128)(2,1)S(1)}, bf16[2,512,128]{2,1,0:T(8,128)(2,1)S(1)}, u32[]{:S(2)}, u32[]{:S(2)}) collective-permute-start(bf16[2,512,128]{2,1,0:T(8,128)(2,1)S(1)} %get-tuple-element.18.refs_0_), channel_id=1, source_target_pairs={{0,240},{16,32},{32,16},{48,64},{64,48},{80,96},{96,80},{112,128},... | collective-permute-start | bytes 786440 | tf_op jit(solution)/shard_map/ppermute | solution.py:185
  8.5 0.0 collective-permute-done.1.pair_ref
  8.5 2.0 %collective-permute-done.refs_1_ = bf16[2,512,128]{2,1,0:T(8,128)(2,1)S(1)} collective-permute-done((bf16[2,512,128]{2,1,0:T(8,128)(2,1)}, bf16[2,512,128]{2,1,0:T(8,128)(2,1)S(1)}, u32[]{:S(2)}, u32[]{:S(2)}) %collective-permute-start) | collective-permute-done | bytes 262176 | tf_op jit(solution)/shard_map/ppermute | solution.py:185
  10.4 0.0 collective-permute-start.2
  10.4 4.4 %collective-permute-done.5.refs_5_ = bf16[2,512,128]{2,1,0:T(8,128)(2,1)S(1)} collective-permute-done((bf16[2,512,128]{2,1,0:T(8,128)(2,1)S(1)}, bf16[2,512,128]{2,1,0:T(8,128)(2,1)S(1)}, u32[]{:S(2)}, u32[]{:S(2)}) %collective-permute-start.5) | collective-permute-done | bytes 262176 | tf_op jit(solution)/shard_map/ppermute | solution.py:185
  14.8 0.8 %collective-permute-start.6 = (bf16[2,512,128]{2,1,0:T(8,128)(2,1)S(1)}, bf16[2,512,128]{2,1,0:T(8,128)(2,1)S(1)}, u32[]{:S(2)}, u32[]{:S(2)}) collective-permute-start(bf16[2,512,128]{2,1,0:T(8,128)(2,1)S(1)} %collective-permute-done.5.refs_5_), channel_id=1, source_target_pairs={{0,32},{16,240},{32,64},{48,16},{64,96},{80,48},{96,128},{112,80},... | collective-permute-start | bytes 786440 | tf_op jit(solution)/shard_map/ppermute | solution.py:185
  15.6 2.4 %collective-permute-done.2.refs_2_ = bf16[2,512,128]{2,1,0:T(8,128)(2,1)S(1)} collective-permute-done((bf16[2,512,128]{2,1,0:T(8,128)(2,1)S(1)}, bf16[2,512,128]{2,1,0:T(8,128)(2,1)S(1)}, u32[]{:S(2)}, u32[]{:S(2)}) %collective-permute-start.2) | collective-permute-done | bytes 262176 | tf_op jit(solution)/shard_map/ppermute | solution.py:185
  18.0 0.0 collective-permute-start.3
  18.0 4.4 %collective-permute-done.6.refs_6_ = bf16[2,512,128]{2,1,0:T(8,128)(2,1)S(1)} collective-permute-done((bf16[2,512,128]{2,1,0:T(8,128)(2,1)S(1)}, bf16[2,512,128]{2,1,0:T(8,128)(2,1)S(1)}, u32[]{:S(2)}, u32[]{:S(2)}) %collective-permute-start.6) | collective-permute-done | bytes 262176 | tf_op jit(solution)/shard_map/ppermute | solution.py:185
  22.4 0.0 collective-permute-start.7
  22.4 3.2 %collective-permute-done.3.refs_3_ = bf16[2,512,128]{2,1,0:T(8,128)(2,1)S(1)} collective-permute-done((bf16[2,512,128]{2,1,0:T(8,128)(2,1)S(1)}, bf16[2,512,128]{2,1,0:T(8,128)(2,1)S(1)}, u32[]{:S(2)}, u32[]{:S(2)}) %collective-permute-start.3) | collective-permute-done | bytes 262176 | tf_op jit(solution)/shard_map/ppermute | solution.py:185
  25.6 0.0 collective-permute-start.4
  25.6 4.4 %collective-permute-done.7.refs_7_ = bf16[2,512,128]{2,1,0:T(8,128)(2,1)S(1)} collective-permute-done((bf16[2,512,128]{2,1,0:T(8,128)(2,1)S(1)}, bf16[2,512,128]{2,1,0:T(8,128)(2,1)S(1)}, u32[]{:S(2)}, u32[]{:S(2)}) %collective-permute-start.7) | collective-permute-done | bytes 262176 | tf_op jit(solution)/shard_map/ppermute | solution.py:185
  30.0 3.2 %collective-permute-done.4.refs_4_ = bf16[2,512,128]{2,1,0:T(8,128)(2,1)S(1)} collective-permute-done((bf16[2,512,128]{2,1,0:T(8,128)(2,1)S(1)}, bf16[2,512,128]{2,1,0:T(8,128)(2,1)S(1)}, u32[]{:S(2)}, u32[]{:S(2)}) %collective-permute-start.4) | collective-permute-done | bytes 262176 | tf_op jit(solution)/shard_map/ppermute | solution.py:185
  33.2 0.7 %pick_regions.1 = bf16[2,2,512,128]{3,2,1,0:T(8,128)(2,1)S(1)} custom-call(s32[1,2]{1,0:T(1,128)S(1)} %collective-permute-done.1.pair_ref, bf16[2,512,128]{2,1,0:T(8,128)(2,1)S(1)} %get-tuple-element.18.refs_0_, bf16[2,512,128]{2,1,0:T(8,128)(2,1)S(1)} %collective-permute-done.refs_1_, bf16[2,512,128]{2,1,0:T(8,128)(2,1)S(1)} %collective-permute-done.2.refs_2_, ...), custom_call_target="tpu_custom_call" | custom-call | bytes 1048576 | tf_op jit(solution)/shard_map/pick_regions/pallas_call | solution.py:209
  33.9 0.1 collective-permute-start.8
  34.0 1.9 %collective-permute-done.8.refs_8_ = bf16[2,2,512,128]{3,2,1,0:T(8,128)(2,1)S(1)} collective-permute-done((bf16[2,2,512,128]{3,2,1,0:T(8,128)(2,1)S(1)}, bf16[2,2,512,128]{3,2,1,0:T(8,128)(2,1)S(1)}, u32[]{:S(2)}, u32[]{:S(2)}) %collective-permute-start.8) | collective-permute-done | bytes 524320 | tf_op jit(solution)/shard_map/ppermute | solution.py:189
  35.9 0.0 copy-done.4
  35.9 0.9 %fan_out.1 = (bf16[1296,128]{1,0:T(8,128)(2,1)S(1)}, bf16[1296,128]{1,0:T(8,128)(2,1)S(1)}, bf16[1296,128]{1,0:T(8,128)(2,1)S(1)}, bf16[1296,128]{1,0:T(8,128)(2,1)S(1)}) custom-call(s32[1,2]{1,0:T(1,128)S(1)} %copy-done.4, bf16[16,128]{1,0:T(8,128)(2,1)S(1)} %get-tuple-element.17.table_ref, bf16[2,512,128]{2,1,0:T(8,128)(2,1)S(1)} %get-tuple-element.18.refs_0_, ...), custom_call_target="tpu_custom_call" | custom-call | bytes 1048576 | tf_op jit(solution)/shard_map/fan_out/pallas_call | solution.py:211
  36.8 1.9 %collective-permute-start.9 = (bf16[1296,128]{1,0:T(8,128)(2,1)S(1)}, bf16[1296,128]{1,0:T(8,128)(2,1)S(1)}, u32[]{:S(2)}, u32[]{:S(2)}) collective-permute-start(bf16[1296,128]{1,0:T(8,128)(2,1)S(1)} %get-tuple-element.22), channel_id=1, source_target_pairs={{0,5},{1,4},{2,7},{3,6},{4,1},{5,0},{6,3},{7,2},{8,13},{9,12},{10,... | collective-permute-start | bytes 995336 | tf_op jit(solution)/shard_map/ppermute | solution.py:177
  38.7 1.2 %collective-permute-start.10 = (bf16[1296,128]{1,0:T(8,128)(2,1)S(1)}, bf16[1296,128]{1,0:T(8,128)(2,1)S(1)}, u32[]{:S(2)}, u32[]{:S(2)}) collective-permute-start(bf16[1296,128]{1,0:T(8,128)(2,1)S(1)} %get-tuple-element.23), channel_id=1, source_target_pairs={{0,1},{1,0},{2,3},{3,2},{4,5},{5,4},{6,7},{7,6},{8,9},{9,8},{10,11... | collective-permute-start | bytes 995336 | tf_op jit(solution)/shard_map/ppermute | solution.py:177
  39.9 0.4 collective-permute-start.11
  40.3 0.0 copy-done.1
  40.3 1.2 %product_0.1.total_ref = f32[4,256,512]{2,1,0:T(8,128)S(1)} custom-call(bf16[1296,128]{1,0:T(8,128)(2,1)S(1)} %get-tuple-element.21.part_ref, f32[4]{0:T(128)S(1)} %copy-done.1), custom_call_target="tpu_custom_call" | custom-call | flops 268435456 | bytes 1048576 | tf_op jit(solution)/shard_map/product_0/pallas_call | solution.py:220
  41.5 3.4 %collective-permute-done.9.part_ref = bf16[1296,128]{1,0:T(8,128)(2,1)S(1)} collective-permute-done((bf16[1296,128]{1,0:T(8,128)(2,1)S(1)}, bf16[1296,128]{1,0:T(8,128)(2,1)S(1)}, u32[]{:S(2)}, u32[]{:S(2)}) %collective-permute-start.9) | collective-permute-done | bytes 331808 | tf_op jit(solution)/shard_map/ppermute | solution.py:177
  45.0 1.3 %product_1.1.total_ref = f32[4,256,512]{2,1,0:T(8,128)S(1)} custom-call(f32[4,256,512]{2,1,0:T(8,128)S(1)} %product_0.1.total_ref, bf16[1296,128]{1,0:T(8,128)(2,1)S(1)} %collective-permute-done.9.part_ref, f32[4]{0:T(128)S(1)} %copy-done.1), custom_call_target="tpu_custom_call", output_to_operand_aliasing={{}: (0, {})} | custom-call | flops 268435456 | bytes 1048576 | tf_op jit(solution)/shard_map/product_1/pallas_call | solution.py:221
  46.3 2.3 %collective-permute-done.10.part_ref = bf16[1296,128]{1,0:T(8,128)(2,1)S(1)} collective-permute-done((bf16[1296,128]{1,0:T(8,128)(2,1)S(1)}, bf16[1296,128]{1,0:T(8,128)(2,1)S(1)}, u32[]{:S(2)}, u32[]{:S(2)}) %collective-permute-start.10) | collective-permute-done | bytes 331808 | tf_op jit(solution)/shard_map/ppermute | solution.py:177
  48.6 0.0 collective-permute-done.11.other_ref
  48.6 1.7 %product_2.1 = (f32[32,4096]{1,0:T(8,128)S(1)}, bf16[32,4096]{1,0:T(8,128)(2,1)S(1)}, bf16[32,4096]{1,0:T(8,128)(2,1)S(1)}, bf16[32,4096]{1,0:T(8,128)(2,1)S(1)}) custom-call(f32[4,256,512]{2,1,0:T(8,128)S(1)} %product_1.1.total_ref, bf16[1296,128]{1,0:T(8,128)(2,1)S(1)} %collective-permute-done.10.part_ref, ...), custom_call_target="tpu_custom_call" | custom-call | flops 536870912 | bytes 1048576 | tf_op jit(solution)/shard_map/product_2/pallas_call | solution.py:225
  50.3 2.9 %collective-permute-start.12 = (bf16[32,4096]{1,0:T(8,128)(2,1)S(1)}, bf16[32,4096]{1,0:T(8,128)(2,1)S(1)}, u32[]{:S(2)}, u32[]{:S(2)}) collective-permute-start(bf16[32,4096]{1,0:T(8,128)(2,1)S(1)} %get-tuple-element.26), channel_id=1, source_target_pairs={{0,15},{1,14},{2,13},{3,12},{4,11},{5,10},{6,9},{7,8},{8,7},{9,6},... | collective-permute-start | bytes 786440 | tf_op jit(solution)/shard_map/ppermute | solution.py:177
  53.2 2.8 %collective-permute-start.13 = (bf16[32,4096]{1,0:T(8,128)(2,1)S(1)}, bf16[32,4096]{1,0:T(8,128)(2,1)S(1)}, u32[]{:S(2)}, u32[]{:S(2)}) collective-permute-start(bf16[32,4096]{1,0:T(8,128)(2,1)S(1)} %get-tuple-element.27), channel_id=1, source_target_pairs={{0,3},{1,2},{2,1},{3,0},{4,7},{5,6},{6,5},{7,4},{8,11},{9,10},{10,... | collective-permute-start | bytes 786440 | tf_op jit(solution)/shard_map/ppermute | solution.py:177
  55.9 0.4 collective-permute-start.14
  56.3 3.8 %collective-permute-done.12.refs_1_ = bf16[32,4096]{1,0:T(8,128)(2,1)S(1)} collective-permute-done((bf16[32,4096]{1,0:T(8,128)(2,1)S(1)}, bf16[32,4096]{1,0:T(8,128)(2,1)S(1)}, u32[]{:S(2)}, u32[]{:S(2)}) %collective-permute-start.12) | collective-permute-done | bytes 262176 | tf_op jit(solution)/shard_map/ppermute | solution.py:177
  60.1 3.0 %collective-permute-done.13.refs_2_ = bf16[32,4096]{1,0:T(8,128)(2,1)S(1)} collective-permute-done((bf16[32,4096]{1,0:T(8,128)(2,1)S(1)}, bf16[32,4096]{1,0:T(8,128)(2,1)S(1)}, u32[]{:S(2)}, u32[]{:S(2)}) %collective-permute-start.13) | collective-permute-done | bytes 262176 | tf_op jit(solution)/shard_map/ppermute | solution.py:177
  63.1 0.4 collective-permute-done.14.refs_3_
  63.5 1.0 %sum_terms.1 = f32[32,1,4,2,512]{4,3,2,1,0:T(2,128)} custom-call(f32[32,4096]{1,0:T(8,128)S(1)} %get-tuple-element.25.refs_0_, bf16[32,4096]{1,0:T(8,128)(2,1)S(1)} %collective-permute-done.12.refs_1_, bf16[32,4096]{1,0:T(8,128)(2,1)S(1)} %collective-permute-done.13.refs_2_, bf16[32,4096]{1,0:T(8,128)(2,1)S(1)} %collective-permute-done.14.refs_3_), custom_call_target="tpu_custom_call" | custom-call | bytes 1048576 | tf_op jit(solution)/shard_map/sum_terms/pallas_call | solution.py:233
  (1 shorter events, 0.0 us)
Async XLA Ops:
  0.0 35.9 %copy-start.4 = (s32[1,2]{1,0:T(1,128)S(1)}, s32[1,2]{1,0:T(1,128)}, u32[]{:S(2)}) copy-start(s32[1,2]{1,0:T(1,128)} %pair_ref.1) | copy-start | bytes 28
  0.0 10.4 %collective-permute-start = (bf16[2,512,128]{2,1,0:T(8,128)(2,1)}, bf16[2,512,128]{2,1,0:T(8,128)(2,1)S(1)}, u32[]{:S(2)}, u32[]{:S(2)}) collective-permute-start(bf16[2,512,128]{2,1,0:T(8,128)(2,1)} %bitcast.3), channel_id=1, source_target_pairs={{0,32},{16,240},{32,64},{48,16},{64,96},{80,48},{96,128},{112,80},... | collective-permute-start | bytes 786440 | tf_op jit(solution)/shard_map/ppermute | solution.py:185
  1.9 6.5 %collective-permute-start.1 = (s32[1,2]{1,0:T(1,128)}, s32[1,2]{1,0:T(1,128)S(1)}, u32[]{:S(2)}, u32[]{:S(2)}) collective-permute-start(s32[1,2]{1,0:T(1,128)} %pair_ref.1), channel_id=1, source_target_pairs={{0,16},{16,0},{32,48},{48,32},{64,80},{80,64},{96,112},{112,96},{1... | collective-permute-start | bytes 32 | tf_op jit(solution)/shard_map/ppermute | solution.py:189
  5.4 0.9 %copy-start = (bf16[2,1,512,128]{3,2,1,0:T(8,128)(2,1)S(1)}, bf16[2,1,512,128]{3,2,1,0:T(8,128)(2,1)}, u32[]{:S(2)}) copy-start(bf16[2,1,512,128]{3,2,1,0:T(8,128)(2,1)} %shapes_ref.1) | copy-start | bytes 786436
  6.4 0.7 %copy-start.2 = (f32[128]{0:T(128)S(1)}, f32[128]{0:T(128)}, u32[]{:S(2)}) copy-start(f32[128]{0:T(128)} %param.7) | copy-start | bytes 1540
  7.0 0.7 %copy-start.3 = (f32[128]{0:T(128)S(1)}, f32[128]{0:T(128)}, u32[]{:S(2)}) copy-start(f32[128]{0:T(128)} %param.8) | copy-start | bytes 1540
  7.7 32.6 %copy-start.1 = (f32[4]{0:T(128)S(1)}, f32[4]{0:T(128)}, u32[]{:S(2)}) copy-start(f32[4]{0:T(128)} %speeds_ref.5) | copy-start | bytes 52
  7.7 7.1 %collective-permute-start.5 = (bf16[2,512,128]{2,1,0:T(8,128)(2,1)S(1)}, bf16[2,512,128]{2,1,0:T(8,128)(2,1)S(1)}, u32[]{:S(2)}, u32[]{:S(2)}) collective-permute-start(bf16[2,512,128]{2,1,0:T(8,128)(2,1)S(1)} %get-tuple-element.18.refs_0_), channel_id=1, source_target_pairs={{0,240},{16,32},{32,16},{48,64},{64,48},{80,96},{96,80},{112,128},... | collective-permute-start | bytes 786440 | tf_op jit(solution)/shard_map/ppermute | solution.py:185
  10.4 7.6 %collective-permute-start.2 = (bf16[2,512,128]{2,1,0:T(8,128)(2,1)S(1)}, bf16[2,512,128]{2,1,0:T(8,128)(2,1)S(1)}, u32[]{:S(2)}, u32[]{:S(2)}) collective-permute-start(bf16[2,512,128]{2,1,0:T(8,128)(2,1)S(1)} %collective-permute-done.refs_1_), channel_id=1, source_target_pairs={{0,32},{16,240},{32,64},{48,16},{64,96},{80,48},{96,128},{112,80},... | collective-permute-start | bytes 786440 | tf_op jit(solution)/shard_map/ppermute | solution.py:185
  14.8 7.6 %collective-permute-start.6 = (bf16[2,512,128]{2,1,0:T(8,128)(2,1)S(1)}, bf16[2,512,128]{2,1,0:T(8,128)(2,1)S(1)}, u32[]{:S(2)}, u32[]{:S(2)}) collective-permute-start(bf16[2,512,128]{2,1,0:T(8,128)(2,1)S(1)} %collective-permute-done.5.refs_5_), channel_id=1, source_target_pairs={{0,32},{16,240},{32,64},{48,16},{64,96},{80,48},{96,128},{112,80},... | collective-permute-start | bytes 786440 | tf_op jit(solution)/shard_map/ppermute | solution.py:185
  18.0 7.6 %collective-permute-start.3 = (bf16[2,512,128]{2,1,0:T(8,128)(2,1)S(1)}, bf16[2,512,128]{2,1,0:T(8,128)(2,1)S(1)}, u32[]{:S(2)}, u32[]{:S(2)}) collective-permute-start(bf16[2,512,128]{2,1,0:T(8,128)(2,1)S(1)} %collective-permute-done.2.refs_2_), channel_id=1, source_target_pairs={{0,32},{16,240},{32,64},{48,16},{64,96},{80,48},{96,128},{112,80},... | collective-permute-start | bytes 786440 | tf_op jit(solution)/shard_map/ppermute | solution.py:185
  22.4 7.6 %collective-permute-start.7 = (bf16[2,512,128]{2,1,0:T(8,128)(2,1)S(1)}, bf16[2,512,128]{2,1,0:T(8,128)(2,1)S(1)}, u32[]{:S(2)}, u32[]{:S(2)}) collective-permute-start(bf16[2,512,128]{2,1,0:T(8,128)(2,1)S(1)} %collective-permute-done.6.refs_6_), channel_id=1, source_target_pairs={{0,32},{16,240},{32,64},{48,16},{64,96},{80,48},{96,128},{112,80},... | collective-permute-start | bytes 786440 | tf_op jit(solution)/shard_map/ppermute | solution.py:185
  25.6 7.6 %collective-permute-start.4 = (bf16[2,512,128]{2,1,0:T(8,128)(2,1)S(1)}, bf16[2,512,128]{2,1,0:T(8,128)(2,1)S(1)}, u32[]{:S(2)}, u32[]{:S(2)}) collective-permute-start(bf16[2,512,128]{2,1,0:T(8,128)(2,1)S(1)} %collective-permute-done.3.refs_3_), channel_id=1, source_target_pairs={{0,32},{16,240},{32,64},{48,16},{64,96},{80,48},{96,128},{112,80},... | collective-permute-start | bytes 786440 | tf_op jit(solution)/shard_map/ppermute | solution.py:185
  33.9 2.0 %collective-permute-start.8 = (bf16[2,2,512,128]{3,2,1,0:T(8,128)(2,1)S(1)}, bf16[2,2,512,128]{3,2,1,0:T(8,128)(2,1)S(1)}, u32[]{:S(2)}, u32[]{:S(2)}) collective-permute-start(bf16[2,2,512,128]{3,2,1,0:T(8,128)(2,1)S(1)} %pick_regions.1), channel_id=1, source_target_pairs={{0,16},{16,0},{32,48},{48,32},{64,80},{80,64},{96,112},{112,96},{1... | collective-permute-start | bytes 1572872 | tf_op jit(solution)/shard_map/ppermute | solution.py:189
  36.8 8.2 %collective-permute-start.9 = (bf16[1296,128]{1,0:T(8,128)(2,1)S(1)}, bf16[1296,128]{1,0:T(8,128)(2,1)S(1)}, u32[]{:S(2)}, u32[]{:S(2)}) collective-permute-start(bf16[1296,128]{1,0:T(8,128)(2,1)S(1)} %get-tuple-element.22), channel_id=1, source_target_pairs={{0,5},{1,4},{2,7},{3,6},{4,1},{5,0},{6,3},{7,2},{8,13},{9,12},{10,... | collective-permute-start | bytes 995336 | tf_op jit(solution)/shard_map/ppermute | solution.py:177
  38.7 9.9 %collective-permute-start.10 = (bf16[1296,128]{1,0:T(8,128)(2,1)S(1)}, bf16[1296,128]{1,0:T(8,128)(2,1)S(1)}, u32[]{:S(2)}, u32[]{:S(2)}) collective-permute-start(bf16[1296,128]{1,0:T(8,128)(2,1)S(1)} %get-tuple-element.23), channel_id=1, source_target_pairs={{0,1},{1,0},{2,3},{3,2},{4,5},{5,4},{6,7},{7,6},{8,9},{9,8},{10,11... | collective-permute-start | bytes 995336 | tf_op jit(solution)/shard_map/ppermute | solution.py:177
  39.9 8.7 %collective-permute-start.11 = (bf16[1296,128]{1,0:T(8,128)(2,1)S(1)}, bf16[1296,128]{1,0:T(8,128)(2,1)S(1)}, u32[]{:S(2)}, u32[]{:S(2)}) collective-permute-start(bf16[1296,128]{1,0:T(8,128)(2,1)S(1)} %get-tuple-element.24), channel_id=1, source_target_pairs={{0,4},{1,5},{2,6},{3,7},{4,0},{5,1},{6,2},{7,3},{8,12},{9,13},{10,... | collective-permute-start | bytes 995336 | tf_op jit(solution)/shard_map/ppermute | solution.py:177
  50.3 9.8 %collective-permute-start.12 = (bf16[32,4096]{1,0:T(8,128)(2,1)S(1)}, bf16[32,4096]{1,0:T(8,128)(2,1)S(1)}, u32[]{:S(2)}, u32[]{:S(2)}) collective-permute-start(bf16[32,4096]{1,0:T(8,128)(2,1)S(1)} %get-tuple-element.26), channel_id=1, source_target_pairs={{0,15},{1,14},{2,13},{3,12},{4,11},{5,10},{6,9},{7,8},{8,7},{9,6},... | collective-permute-start | bytes 786440 | tf_op jit(solution)/shard_map/ppermute | solution.py:177
  53.2 9.9 %collective-permute-start.13 = (bf16[32,4096]{1,0:T(8,128)(2,1)S(1)}, bf16[32,4096]{1,0:T(8,128)(2,1)S(1)}, u32[]{:S(2)}, u32[]{:S(2)}) collective-permute-start(bf16[32,4096]{1,0:T(8,128)(2,1)S(1)} %get-tuple-element.27), channel_id=1, source_target_pairs={{0,3},{1,2},{2,1},{3,0},{4,7},{5,6},{6,5},{7,4},{8,11},{9,10},{10,... | collective-permute-start | bytes 786440 | tf_op jit(solution)/shard_map/ppermute | solution.py:177
  55.9 7.6 %collective-permute-start.14 = (bf16[32,4096]{1,0:T(8,128)(2,1)S(1)}, bf16[32,4096]{1,0:T(8,128)(2,1)S(1)}, u32[]{:S(2)}, u32[]{:S(2)}) collective-permute-start(bf16[32,4096]{1,0:T(8,128)(2,1)S(1)} %get-tuple-element.28), channel_id=1, source_target_pairs={{0,12},{1,13},{2,14},{3,15},{4,8},{5,9},{6,10},{7,11},{8,4},{9,5},... | collective-permute-start | bytes 786440 | tf_op jit(solution)/shard_map/ppermute | solution.py:177

commit v5 on v4

--- a/solution.py
+++ b/solution.py
@@ -43,11 +43,33 @@
     below = (me // 2 - region // 2) % 8
     steps = jnp.where(core == 0, below, (8 - below) % 8)
     same = region % 2 == core
-    slot = jnp.where(same, steps, jnp.where(steps == 0, 8, 4 + steps))
-    return jnp.where(slot < 8, jnp.where(steps > 4, 8, slot), 8)
-
-
-def prepare_kernel(shapes_ref, omega_ref, damping_ref, own_ref, table_ref):
+    near = jnp.where(same, steps, jnp.where(steps == 0, 8, 3 + steps))
+    far = jnp.where(steps > 4, 8, jnp.where(same, 7, 9))
+    return jnp.where(steps < 4, near, far)
+
+
+def pick_kernel(pair_ref, *refs):
+    regions, out_ref = refs[:7], refs[7]
+    me = lax.axis_index("group")
+    pair = pair_ref[...]
+    for n in range(2):
+        slot = locate(pair[0, n], me)
+        for k, ref in enumerate(regions):
+
+            @pl.when(slot == k)
+            def _(ref=ref):
+                out_ref[n] = ref[...]
+
+
+def split3(x):
+    first = x.astype(BF)
+    rest = x - first.astype(F32)
+    second = rest.astype(BF)
+    third = (rest - second.astype(F32)).astype(BF)
+    return first.astype(F32), second.astype(F32), third.astype(F32)
+
+
+def prepare_kernel(shapes_ref, omega_ref, damping_ref, speeds_ref, own_ref, table_ref, speed_rows_ref):
     own_ref[...] = shapes_ref[:, 0]
     pieces = split3(omega_ref[...]) + split3(damping_ref[...])
     rows = lax.broadcasted_iota(jnp.int32, (16, 128), 0)
@@ -55,42 +77,24 @@
     for n, piece in enumerate(pieces):
         table = jnp.where(rows == n, piece, table)
     table_ref[...] = table.astype(BF)
-
-
-def pick_kernel(pair_ref, *refs):
-    regions, out_ref = refs[:8], refs[8]
+    rows = lax.broadcasted_iota(jnp.int32, (8, 128), 0)
+    speeds = jnp.zeros((8, 128), F32)
+    for s in range(4):
+        speeds = jnp.where(rows == s, speeds_ref[s], speeds)
+    speed_rows_ref[...] = speeds
+
+
+def fan_kernel(pair_ref, table_ref, *refs):
+    regions, other_ref, far_ref, out_refs, picked_ref = refs[:8], refs[8], refs[9], refs[10:14], refs[14]
     me = lax.axis_index("group")
+    pair = pair_ref[...]
     for n in range(2):
-        slot = locate(pair_ref[0, n], me)
-        for k, ref in enumerate(regions):
-
-            @pl.when(slot == k)
-            def _(ref=ref):
-                out_ref[n] = ref[...]
-
-
-def split3(x):
-    first = x.astype(BF)
-    rest = x - first.astype(F32)
-    second = rest.astype(BF)
-    third = (rest - second.astype(F32)).astype(BF)
-    return first.astype(F32), second.astype(F32), third.astype(F32)
-
-
-def fan_kernel(pair_ref, table_ref, *refs):
-    regions, other_ref, out_refs, picked_ref = refs[:8], refs[8], refs[9:13], refs[13]
-    me = lax.axis_index("group")
-    for n in range(2):
-        slot = locate(pair_ref[0, n], me)
-        for k, ref in enumerate(regions):
+        slot = locate(pair[0, n], me)
+        for k, ref in enumerate(regions + (other_ref.at[n], far_ref)):
 
             @pl.when(slot == k)
             def _(ref=ref):
                 picked_ref[n] = ref[...]
-
-        @pl.when(slot == 8)
-        def _():
-            picked_ref[n] = other_ref[n]
 
     core = me % 2
     at_mode = lax.axis_index("mode")
@@ -118,7 +122,7 @@
         modes.append((table[0:1] + table[1:2] + table[2:3], table[3:4] + table[4:5] + table[5:6]))
     left = jnp.concatenate(left, axis=1)
     for s in range(4):
-        speed = speeds_ref[s]
+        speed = speeds_ref[s : s + 1, :]
         right = []
         for ref, (omega, damping) in zip(parts, modes):
             ere = ref[EXCITE : EXCITE + 512, :].astype(F32)
@@ -191,12 +195,16 @@
 
 def shards(shapes, pairs, omega, damping, speeds):
     a1 = along_z(shapes.reshape(2, 512, 128))
-    own, table = call(
+    own, table, speed_rows = call(
         prepare_kernel,
-        (jax.ShapeDtypeStruct((2, 512, 128), BF), jax.ShapeDtypeStruct((16, 128), BF)),
-        [VMEM] * 3,
+        (
+            jax.ShapeDtypeStruct((2, 512, 128), BF),
+            jax.ShapeDtypeStruct((16, 128), BF),
+            jax.ShapeDtypeStruct((8, 128), F32),
+        ),
+        [VMEM] * 3 + [SMEM],
         "prepare",
-    )(shapes, omega.reshape(1, 128), damping.reshape(1, 128))
+    )(shapes, omega.reshape(1, 128), damping.reshape(1, 128), speeds)
     b1 = along_z(own, crossing=True)
     a1, other_pair = lax.optimization_barrier((a1, swap_cores(pairs)))
     a2 = along_z(a1)
@@ -204,31 +212,31 @@
     a3 = along_z(a2)
     b3 = along_z(b2)
     a4 = along_z(a3)
-    regions = (own, a1, a2, a3, a4, b1, b2, b3)
+    regions = (own, a1, a2, a3, b1, b2, b3)
     other = jax.ShapeDtypeStruct((2, 2, 512, 128), BF)
-    wanted = call(pick_kernel, other, [SMEM] + [VMEM] * 8, "pick_regions")(other_pair, *regions)
+    wanted = call(pick_kernel, other, [VMEM] * 8, "pick_regions")(other_pair, *regions)
     message = jax.ShapeDtypeStruct((ROWS, 128), BF)
     fanned = call(
         fan_kernel,
         (message,) * 4,
-        [SMEM] + [VMEM] * 10,
+        [VMEM] * 12,
         "fan_out",
         scratch=[pltpu.VMEM((2, 2, 512, 128), BF)],
-    )(pairs, table, *regions, swap_cores(wanted))
+    )(pairs, table, *regions, a4, swap_cores(wanted), swap_cores(a4))
     parts = [fanned[0]] + [exchange(fanned[d], d, 0) for d in (3, 1, 2)]
     sums = jax.ShapeDtypeStruct((4, 256, 512), F32)
-    total = call(first_kernel, sums, [VMEM, SMEM], "product_0", flops=1 << 28)(parts[0], speeds)
+    total = call(first_kernel, sums, [VMEM] * 2, "product_0", flops=1 << 28)(parts[0], speed_rows)
     total = call(
-        next_kernel, sums, [VMEM, VMEM, SMEM], "product_1", flops=1 << 28, aliases={0: 0}
-    )(total, parts[1], speeds)
+        next_kernel, sums, [VMEM] * 3, "product_1", flops=1 << 28, aliases={0: 0}
+    )(total, parts[1], speed_rows)
     block = jax.ShapeDtypeStruct((32, 4096), BF)
     made = call(
         last_kernel,
         (jax.ShapeDtypeStruct((32, 4096), F32), block, block, block),
-        [VMEM, VMEM, VMEM, SMEM],
+        [VMEM] * 4,
         "product_2",
         flops=1 << 29,
-    )(total, parts[2], parts[3], speeds)
+    )(total, parts[2], parts[3], speed_rows)
     terms = [made[0]] + [exchange(made[e], e, 1) for e in (3, 1, 2)]
     return call(
         sum_kernel, jax.ShapeDtypeStruct((32, 1, 4, 2, 512), F32), [VMEM] * 4, "sum_terms"

time: 64.7 us -> 63.1 us (0.975)
  Pallas kernels: 6.87 us -> 4.95 us
  waiting for transfers between devices: 38.7 us -> 36.9 us
  starting transfers between devices: 16.6 us -> 18.1 us
  local copies, waits for them, and re-layouts: 2.27 us -> 2.95 us
    ppermute x7, starting transfers between devices: 3.44 us -> 8.4 us  [along_z(): return lax.ppermute(value, 'group', perm)]
    ppermute x7, waiting for transfers between devices: 23.9 us -> 20.1 us  [along_z(): return lax.ppermute(value, 'group', perm)]
    ppermute x2 -> x3, starting transfers between devices: 3.59 us -> 0.1 us  [swap_cores(): return lax.ppermute(value, 'group', [(g, g ^ 1) for g in range(16)])]
    pallas_call x4, Pallas kernels: 4.09 us -> 2.14 us  [the longest x1 0.76 us: shards(): call(next_kernel, sums, [VMEM] * 3, 'product_1', flops=1 << 28, aliases={...]
    ppermute x6, waiting for transfers between devices: 12.9 us -> 14 us  [exchange(): return lax.ppermute(value, ('group', 'mode'), perm)]
    ppermute x2 -> x3, waiting for transfers between devices: 1.9 us -> 2.79 us  [swap_cores(): return lax.ppermute(value, 'group', [(g, g ^ 1) for g in range(16)])]
    unnamed x10, local copies, waits for them, and re-layouts: 2.27 us -> 2.95 us
  transfers between devices with their start and end apart: 15 -> 16, of which waited for: 13 -> 13; matrix products, arithmetic and copies ran while one was open for 0% -> 0% of each run, Pallas kernels for 4% -> 4%
where the time goes in v5:
time: 63.1 us; the launch traced here: 62.9 us
  waiting for transfers between devices  36.9 us (58%)
  starting transfers between devices  18.1 us (29%)
  Pallas kernels  4.95 us (8%)
  local copies, waits for them, and re-layouts  2.95 us (5%)
    ppermute x7, waiting for transfers between devices, along_z(): return lax.ppermute(value, 'group', perm)  20.1 us
    ppermute x6, waiting for transfers between devices, exchange(): return lax.ppermute(value, ('group', 'mode'), perm)  14 us
    ppermute x6, starting transfers between devices, exchange(): return lax.ppermute(value, ('group', 'mode'), perm)  9.57 us
    ppermute x7, starting transfers between devices, along_z(): return lax.ppermute(value, 'group', perm)  8.4 us
    unnamed x10, local copies, waits for them, and re-layouts  2.95 us
    ppermute x3, waiting for transfers between devices, swap_cores(): return lax.ppermute(value, 'group', [(g, g ^ 1) for g in range(16)])  2.79 us
  transfers between devices with their start and end apart: 16, of which 13 were waited for; matrix products, arithmetic and copies ran while one was open for 0% of the time, Pallas kernels for 4%

profile of v5, /device:TPU:6, one launch (start us, length us, event | category | flops | bytes accessed | tf_op | source)
XLA Modules:
  0.0 62.9 jit_solution(17071768675957995479)
XLA Ops:
  0.0 0.0 copy-start.4
  0.0 1.9 %collective-permute-start = (bf16[2,512,128]{2,1,0:T(8,128)(2,1)}, bf16[2,512,128]{2,1,0:T(8,128)(2,1)S(1)}, u32[]{:S(2)}, u32[]{:S(2)}) collective-permute-start(bf16[2,512,128]{2,1,0:T(8,128)(2,1)} %bitcast.3), channel_id=1, source_target_pairs={{0,32},{16,240},{32,64},{48,16},{64,96},{80,48},{96,128},{112,80},... | collective-permute-start | bytes 786440 | tf_op jit(solution)/shard_map/ppermute | solution.py:189
  1.9 0.0 copy-start
  1.9 1.0 %copy-done = bf16[2,1,512,128]{3,2,1,0:T(8,128)(2,1)S(1)} copy-done((bf16[2,1,512,128]{3,2,1,0:T(8,128)(2,1)S(1)}, bf16[2,1,512,128]{3,2,1,0:T(8,128)(2,1)}, u32[]{:S(2)}) %copy-start) | copy-done | bytes 262168
  2.9 0.0 copy-start.1
  2.9 0.7 %copy-done.1 = f32[128]{0:T(128)S(1)} copy-done((f32[128]{0:T(128)S(1)}, f32[128]{0:T(128)}, u32[]{:S(2)}) %copy-start.1) | copy-done | bytes 536
  3.6 0.0 copy-start.2
  3.6 0.7 %copy-done.2 = f32[128]{0:T(128)S(1)} copy-done((f32[128]{0:T(128)S(1)}, f32[128]{0:T(128)}, u32[]{:S(2)}) %copy-start.2) | copy-done | bytes 536
  4.2 0.7 %copy-done.3 = f32[4]{0:T(128)S(1)} copy-done((f32[4]{0:T(128)S(1)}, f32[4]{0:T(128)}, u32[]{:S(2)}) %copy-start.3) | copy-done | bytes 40
  4.9 0.6 prepare.1
  5.4 4.2 %collective-permute-start.4 = (bf16[2,512,128]{2,1,0:T(8,128)(2,1)S(1)}, bf16[2,512,128]{2,1,0:T(8,128)(2,1)S(1)}, u32[]{:S(2)}, u32[]{:S(2)}) collective-permute-start(bf16[2,512,128]{2,1,0:T(8,128)(2,1)S(1)} %get-tuple-element.19.refs_0_), channel_id=1, source_target_pairs={{0,240},{16,32},{32,16},{48,64},{64,48},{80,96},{96,80},{112,128},... | collective-permute-start | bytes 786440 | tf_op jit(solution)/shard_map/ppermute | solution.py:189
  9.6 0.0 collective-permute-start.1
  9.6 1.3 %collective-permute-done.1.pair_ref = s32[1,2]{1,0:T(1,128)S(1)} collective-permute-done((s32[1,2]{1,0:T(1,128)}, s32[1,2]{1,0:T(1,128)S(1)}, u32[]{:S(2)}, u32[]{:S(2)}) %collective-permute-start.1) | collective-permute-done | bytes 40 | tf_op jit(solution)/shard_map/ppermute | solution.py:193
  10.9 0.0 collective-permute-done.refs_1_
  10.9 1.0 %collective-permute-start.2 = (bf16[2,512,128]{2,1,0:T(8,128)(2,1)S(1)}, bf16[2,512,128]{2,1,0:T(8,128)(2,1)S(1)}, u32[]{:S(2)}, u32[]{:S(2)}) collective-permute-start(bf16[2,512,128]{2,1,0:T(8,128)(2,1)S(1)} %collective-permute-done.refs_1_), channel_id=1, source_target_pairs={{0,32},{16,240},{32,64},{48,16},{64,96},{80,48},{96,128},{112,80},... | collective-permute-start | bytes 786440 | tf_op jit(solution)/shard_map/ppermute | solution.py:189
  11.9 2.6 %collective-permute-done.4.refs_4_ = bf16[2,512,128]{2,1,0:T(8,128)(2,1)S(1)} collective-permute-done((bf16[2,512,128]{2,1,0:T(8,128)(2,1)S(1)}, bf16[2,512,128]{2,1,0:T(8,128)(2,1)S(1)}, u32[]{:S(2)}, u32[]{:S(2)}) %collective-permute-start.4) | collective-permute-done | bytes 262176 | tf_op jit(solution)/shard_map/ppermute | solution.py:189
  14.5 1.2 %collective-permute-start.5 = (bf16[2,512,128]{2,1,0:T(8,128)(2,1)S(1)}, bf16[2,512,128]{2,1,0:T(8,128)(2,1)S(1)}, u32[]{:S(2)}, u32[]{:S(2)}) collective-permute-start(bf16[2,512,128]{2,1,0:T(8,128)(2,1)S(1)} %collective-permute-done.4.refs_4_), channel_id=1, source_target_pairs={{0,32},{16,240},{32,64},{48,16},{64,96},{80,48},{96,128},{112,80},... | collective-permute-start | bytes 786440 | tf_op jit(solution)/shard_map/ppermute | solution.py:189
  15.8 2.7 %collective-permute-done.2.refs_2_ = bf16[2,512,128]{2,1,0:T(8,128)(2,1)S(1)} collective-permute-done((bf16[2,512,128]{2,1,0:T(8,128)(2,1)S(1)}, bf16[2,512,128]{2,1,0:T(8,128)(2,1)S(1)}, u32[]{:S(2)}, u32[]{:S(2)}) %collective-permute-start.2) | collective-permute-done | bytes 262176 | tf_op jit(solution)/shard_map/ppermute | solution.py:189
  18.5 0.0 collective-permute-start.3
  18.5 3.6 %collective-permute-done.5.refs_5_ = bf16[2,512,128]{2,1,0:T(8,128)(2,1)S(1)} collective-permute-done((bf16[2,512,128]{2,1,0:T(8,128)(2,1)S(1)}, bf16[2,512,128]{2,1,0:T(8,128)(2,1)S(1)}, u32[]{:S(2)}, u32[]{:S(2)}) %collective-permute-start.5) | collective-permute-done | bytes 262176 | tf_op jit(solution)/shard_map/ppermute | solution.py:189
  22.1 0.0 collective-permute-start.6
  22.2 3.9 %collective-permute-done.3.refs_3_ = bf16[2,512,128]{2,1,0:T(8,128)(2,1)S(1)} collective-permute-done((bf16[2,512,128]{2,1,0:T(8,128)(2,1)S(1)}, bf16[2,512,128]{2,1,0:T(8,128)(2,1)S(1)}, u32[]{:S(2)}, u32[]{:S(2)}) %collective-permute-start.3) | collective-permute-done | bytes 262176 | tf_op jit(solution)/shard_map/ppermute | solution.py:189
  26.1 0.0 collective-permute-start.7
  26.1 3.6 %collective-permute-done.6.refs_6_ = bf16[2,512,128]{2,1,0:T(8,128)(2,1)S(1)} collective-permute-done((bf16[2,512,128]{2,1,0:T(8,128)(2,1)S(1)}, bf16[2,512,128]{2,1,0:T(8,128)(2,1)S(1)}, u32[]{:S(2)}, u32[]{:S(2)}) %collective-permute-start.6) | collective-permute-done | bytes 262176 | tf_op jit(solution)/shard_map/ppermute | solution.py:189
  29.7 0.3 pick_regions.1
  30.0 0.1 collective-permute-start.8
  30.1 3.6 %collective-permute-done.7.refs_7_ = bf16[2,512,128]{2,1,0:T(8,128)(2,1)S(1)} collective-permute-done((bf16[2,512,128]{2,1,0:T(8,128)(2,1)S(1)}, bf16[2,512,128]{2,1,0:T(8,128)(2,1)S(1)}, u32[]{:S(2)}, u32[]{:S(2)}) %collective-permute-start.7) | collective-permute-done | bytes 262176 | tf_op jit(solution)/shard_map/ppermute | solution.py:189
  33.7 0.0 collective-permute-start.9
  33.7 1.5 %collective-permute-done.9.refs_9_ = bf16[2,512,128]{2,1,0:T(8,128)(2,1)S(1)} collective-permute-done((bf16[2,512,128]{2,1,0:T(8,128)(2,1)S(1)}, bf16[2,512,128]{2,1,0:T(8,128)(2,1)S(1)}, u32[]{:S(2)}, u32[]{:S(2)}) %collective-permute-start.9) | collective-permute-done | bytes 262176 | tf_op jit(solution)/shard_map/ppermute | solution.py:193
  35.2 0.0 collective-permute-done.8.refs_8_
  35.2 0.0 copy-done.4
  35.2 0.5 fan_out.1
  35.7 1.9 %collective-permute-start.10 = (bf16[1296,128]{1,0:T(8,128)(2,1)S(1)}, bf16[1296,128]{1,0:T(8,128)(2,1)S(1)}, u32[]{:S(2)}, u32[]{:S(2)}) collective-permute-start(bf16[1296,128]{1,0:T(8,128)(2,1)S(1)} %get-tuple-element.24), channel_id=1, source_target_pairs={{0,5},{1,4},{2,7},{3,6},{4,1},{5,0},{6,3},{7,2},{8,13},{9,12},{10,... | collective-permute-start | bytes 995336 | tf_op jit(solution)/shard_map/ppermute | solution.py:181
  37.6 1.2 %collective-permute-start.11 = (bf16[1296,128]{1,0:T(8,128)(2,1)S(1)}, bf16[1296,128]{1,0:T(8,128)(2,1)S(1)}, u32[]{:S(2)}, u32[]{:S(2)}) collective-permute-start(bf16[1296,128]{1,0:T(8,128)(2,1)S(1)} %get-tuple-element.25), channel_id=1, source_target_pairs={{0,1},{1,0},{2,3},{3,2},{4,5},{5,4},{6,7},{7,6},{8,9},{9,8},{10,11... | collective-permute-start | bytes 995336 | tf_op jit(solution)/shard_map/ppermute | solution.py:181
  38.8 0.4 collective-permute-start.12
  39.3 0.7 %product_0.1.total_ref = f32[4,256,512]{2,1,0:T(8,128)S(1)} custom-call(bf16[1296,128]{1,0:T(8,128)(2,1)S(1)} %get-tuple-element.22.part_ref, f32[8,128]{1,0:T(8,128)S(1)} %get-tuple-element.23.speeds_ref), custom_call_target="tpu_custom_call" | custom-call | flops 268435456 | bytes 1048576 | tf_op jit(solution)/shard_map/product_0/pallas_call | solution.py:228
  39.9 4.0 %collective-permute-done.10.part_ref = bf16[1296,128]{1,0:T(8,128)(2,1)S(1)} collective-permute-done((bf16[1296,128]{1,0:T(8,128)(2,1)S(1)}, bf16[1296,128]{1,0:T(8,128)(2,1)S(1)}, u32[]{:S(2)}, u32[]{:S(2)}) %collective-permute-start.10) | collective-permute-done | bytes 331808 | tf_op jit(solution)/shard_map/ppermute | solution.py:181
  43.9 0.8 %product_1.1.total_ref = f32[4,256,512]{2,1,0:T(8,128)S(1)} custom-call(f32[4,256,512]{2,1,0:T(8,128)S(1)} %product_0.1.total_ref, bf16[1296,128]{1,0:T(8,128)(2,1)S(1)} %collective-permute-done.10.part_ref, f32[8,128]{1,0:T(8,128)S(1)} %get-tuple-element.23.speeds_ref), custom_call_target="tpu_custom_call", output_to_operand_aliasing={{}: (0, {})} | custom-call | flops 268435456 | bytes 1048576 | tf_op jit(solution)/shard_map/product_1/pallas_call | solution.py:229
  44.7 2.8 %collective-permute-done.11.part_ref = bf16[1296,128]{1,0:T(8,128)(2,1)S(1)} collective-permute-done((bf16[1296,128]{1,0:T(8,128)(2,1)S(1)}, bf16[1296,128]{1,0:T(8,128)(2,1)S(1)}, u32[]{:S(2)}, u32[]{:S(2)}) %collective-permute-start.11) | collective-permute-done | bytes 331808 | tf_op jit(solution)/shard_map/ppermute | solution.py:181
  47.5 0.0 collective-permute-done.12.other_ref
  47.5 1.2 %product_2.1 = (f32[32,4096]{1,0:T(8,128)S(1)}, bf16[32,4096]{1,0:T(8,128)(2,1)S(1)}, bf16[32,4096]{1,0:T(8,128)(2,1)S(1)}, bf16[32,4096]{1,0:T(8,128)(2,1)S(1)}) custom-call(f32[4,256,512]{2,1,0:T(8,128)S(1)} %product_1.1.total_ref, bf16[1296,128]{1,0:T(8,128)(2,1)S(1)} %collective-permute-done.11.part_ref, ...), custom_call_target="tpu_custom_call" | custom-call | flops 536870912 | bytes 1048576 | tf_op jit(solution)/shard_map/product_2/pallas_call | solution.py:233
  48.7 2.8 %collective-permute-start.13 = (bf16[32,4096]{1,0:T(8,128)(2,1)S(1)}, bf16[32,4096]{1,0:T(8,128)(2,1)S(1)}, u32[]{:S(2)}, u32[]{:S(2)}) collective-permute-start(bf16[32,4096]{1,0:T(8,128)(2,1)S(1)} %get-tuple-element.28), channel_id=1, source_target_pairs={{0,15},{1,14},{2,13},{3,12},{4,11},{5,10},{6,9},{7,8},{8,7},{9,6},... | collective-permute-start | bytes 786440 | tf_op jit(solution)/shard_map/ppermute | solution.py:181
  51.6 2.8 %collective-permute-start.14 = (bf16[32,4096]{1,0:T(8,128)(2,1)S(1)}, bf16[32,4096]{1,0:T(8,128)(2,1)S(1)}, u32[]{:S(2)}, u32[]{:S(2)}) collective-permute-start(bf16[32,4096]{1,0:T(8,128)(2,1)S(1)} %get-tuple-element.29), channel_id=1, source_target_pairs={{0,3},{1,2},{2,1},{3,0},{4,7},{5,6},{6,5},{7,4},{8,11},{9,10},{10,... | collective-permute-start | bytes 786440 | tf_op jit(solution)/shard_map/ppermute | solution.py:181
  54.4 0.4 collective-permute-start.15
  54.7 3.8 %collective-permute-done.13.refs_1_ = bf16[32,4096]{1,0:T(8,128)(2,1)S(1)} collective-permute-done((bf16[32,4096]{1,0:T(8,128)(2,1)S(1)}, bf16[32,4096]{1,0:T(8,128)(2,1)S(1)}, u32[]{:S(2)}, u32[]{:S(2)}) %collective-permute-start.13) | collective-permute-done | bytes 262176 | tf_op jit(solution)/shard_map/ppermute | solution.py:181
  58.5 3.0 %collective-permute-done.14.refs_2_ = bf16[32,4096]{1,0:T(8,128)(2,1)S(1)} collective-permute-done((bf16[32,4096]{1,0:T(8,128)(2,1)S(1)}, bf16[32,4096]{1,0:T(8,128)(2,1)S(1)}, u32[]{:S(2)}, u32[]{:S(2)}) %collective-permute-start.14) | collective-permute-done | bytes 262176 | tf_op jit(solution)/shard_map/ppermute | solution.py:181
  61.5 0.4 collective-permute-done.15.refs_3_
  61.9 1.0 %sum_terms.1 = f32[32,1,4,2,512]{4,3,2,1,0:T(2,128)} custom-call(f32[32,4096]{1,0:T(8,128)S(1)} %get-tuple-element.27.refs_0_, bf16[32,4096]{1,0:T(8,128)(2,1)S(1)} %collective-permute-done.13.refs_1_, bf16[32,4096]{1,0:T(8,128)(2,1)S(1)} %collective-permute-done.14.refs_2_, bf16[32,4096]{1,0:T(8,128)(2,1)S(1)} %collective-permute-done.15.refs_3_), custom_call_target="tpu_custom_call" | custom-call | bytes 1048576 | tf_op jit(solution)/shard_map/sum_terms/pallas_call | solution.py:241
  (1 shorter events, 0.0 us)
Async XLA Ops:
  0.0 35.2 %copy-start.4 = (s32[1,2]{1,0:T(1,128)S(1)}, s32[1,2]{1,0:T(1,128)}, u32[]{:S(2)}) copy-start(s32[1,2]{1,0:T(1,128)} %pair_ref.1) | copy-start | bytes 28
  0.0 10.9 %collective-permute-start = (bf16[2,512,128]{2,1,0:T(8,128)(2,1)}, bf16[2,512,128]{2,1,0:T(8,128)(2,1)S(1)}, u32[]{:S(2)}, u32[]{:S(2)}) collective-permute-start(bf16[2,512,128]{2,1,0:T(8,128)(2,1)} %bitcast.3), channel_id=1, source_target_pairs={{0,32},{16,240},{32,64},{48,16},{64,96},{80,48},{96,128},{112,80},... | collective-permute-start | bytes 786440 | tf_op jit(solution)/shard_map/ppermute | solution.py:189
  1.9 1.0 %copy-start = (bf16[2,1,512,128]{3,2,1,0:T(8,128)(2,1)S(1)}, bf16[2,1,512,128]{3,2,1,0:T(8,128)(2,1)}, u32[]{:S(2)}) copy-start(bf16[2,1,512,128]{3,2,1,0:T(8,128)(2,1)} %shapes_ref.1) | copy-start | bytes 786436
  2.9 0.7 %copy-start.1 = (f32[128]{0:T(128)S(1)}, f32[128]{0:T(128)}, u32[]{:S(2)}) copy-start(f32[128]{0:T(128)} %param.7) | copy-start | bytes 1540
  3.6 0.7 %copy-start.2 = (f32[128]{0:T(128)S(1)}, f32[128]{0:T(128)}, u32[]{:S(2)}) copy-start(f32[128]{0:T(128)} %param.8) | copy-start | bytes 1540
  4.2 0.7 %copy-start.3 = (f32[4]{0:T(128)S(1)}, f32[4]{0:T(128)}, u32[]{:S(2)}) copy-start(f32[4]{0:T(128)} %speeds_ref.1) | copy-start | bytes 52
  5.4 9.1 %collective-permute-start.4 = (bf16[2,512,128]{2,1,0:T(8,128)(2,1)S(1)}, bf16[2,512,128]{2,1,0:T(8,128)(2,1)S(1)}, u32[]{:S(2)}, u32[]{:S(2)}) collective-permute-start(bf16[2,512,128]{2,1,0:T(8,128)(2,1)S(1)} %get-tuple-element.19.refs_0_), channel_id=1, source_target_pairs={{0,240},{16,32},{32,16},{48,64},{64,48},{80,96},{96,80},{112,128},... | collective-permute-start | bytes 786440 | tf_op jit(solution)/shard_map/ppermute | solution.py:189
  9.6 1.3 %collective-permute-start.1 = (s32[1,2]{1,0:T(1,128)}, s32[1,2]{1,0:T(1,128)S(1)}, u32[]{:S(2)}, u32[]{:S(2)}) collective-permute-start(s32[1,2]{1,0:T(1,128)} %pair_ref.1), channel_id=1, source_target_pairs={{0,16},{16,0},{32,48},{48,32},{64,80},{80,64},{96,112},{112,96},{1... | collective-permute-start | bytes 32 | tf_op jit(solution)/shard_map/ppermute | solution.py:193
  10.9 7.6 %collective-permute-start.2 = (bf16[2,512,128]{2,1,0:T(8,128)(2,1)S(1)}, bf16[2,512,128]{2,1,0:T(8,128)(2,1)S(1)}, u32[]{:S(2)}, u32[]{:S(2)}) collective-permute-start(bf16[2,512,128]{2,1,0:T(8,128)(2,1)S(1)} %collective-permute-done.refs_1_), channel_id=1, source_target_pairs={{0,32},{16,240},{32,64},{48,16},{64,96},{80,48},{96,128},{112,80},... | collective-permute-start | bytes 786440 | tf_op jit(solution)/shard_map/ppermute | solution.py:189
  14.5 7.6 %collective-permute-start.5 = (bf16[2,512,128]{2,1,0:T(8,128)(2,1)S(1)}, bf16[2,512,128]{2,1,0:T(8,128)(2,1)S(1)}, u32[]{:S(2)}, u32[]{:S(2)}) collective-permute-start(bf16[2,512,128]{2,1,0:T(8,128)(2,1)S(1)} %collective-permute-done.4.refs_4_), channel_id=1, source_target_pairs={{0,32},{16,240},{32,64},{48,16},{64,96},{80,48},{96,128},{112,80},... | collective-permute-start | bytes 786440 | tf_op jit(solution)/shard_map/ppermute | solution.py:189
  18.5 7.6 %collective-permute-start.3 = (bf16[2,512,128]{2,1,0:T(8,128)(2,1)S(1)}, bf16[2,512,128]{2,1,0:T(8,128)(2,1)S(1)}, u32[]{:S(2)}, u32[]{:S(2)}) collective-permute-start(bf16[2,512,128]{2,1,0:T(8,128)(2,1)S(1)} %collective-permute-done.2.refs_2_), channel_id=1, source_target_pairs={{0,32},{16,240},{32,64},{48,16},{64,96},{80,48},{96,128},{112,80},... | collective-permute-start | bytes 786440 | tf_op jit(solution)/shard_map/ppermute | solution.py:189
  22.1 7.6 %collective-permute-start.6 = (bf16[2,512,128]{2,1,0:T(8,128)(2,1)S(1)}, bf16[2,512,128]{2,1,0:T(8,128)(2,1)S(1)}, u32[]{:S(2)}, u32[]{:S(2)}) collective-permute-start(bf16[2,512,128]{2,1,0:T(8,128)(2,1)S(1)} %collective-permute-done.5.refs_5_), channel_id=1, source_target_pairs={{0,32},{16,240},{32,64},{48,16},{64,96},{80,48},{96,128},{112,80},... | collective-permute-start | bytes 786440 | tf_op jit(solution)/shard_map/ppermute | solution.py:189
  26.1 7.6 %collective-permute-start.7 = (bf16[2,512,128]{2,1,0:T(8,128)(2,1)S(1)}, bf16[2,512,128]{2,1,0:T(8,128)(2,1)S(1)}, u32[]{:S(2)}, u32[]{:S(2)}) collective-permute-start(bf16[2,512,128]{2,1,0:T(8,128)(2,1)S(1)} %collective-permute-done.3.refs_3_), channel_id=1, source_target_pairs={{0,32},{16,240},{32,64},{48,16},{64,96},{80,48},{96,128},{112,80},... | collective-permute-start | bytes 786440 | tf_op jit(solution)/shard_map/ppermute | solution.py:189
  30.0 5.2 %collective-permute-start.8 = (bf16[2,2,512,128]{3,2,1,0:T(8,128)(2,1)S(1)}, bf16[2,2,512,128]{3,2,1,0:T(8,128)(2,1)S(1)}, u32[]{:S(2)}, u32[]{:S(2)}) collective-permute-start(bf16[2,2,512,128]{3,2,1,0:T(8,128)(2,1)S(1)} %pick_regions.1), channel_id=1, source_target_pairs={{0,16},{16,0},{32,48},{48,32},{64,80},{80,64},{96,112},{112,96},{1... | collective-permute-start | bytes 1572872 | tf_op jit(solution)/shard_map/ppermute | solution.py:193
  33.7 1.5 %collective-permute-start.9 = (bf16[2,512,128]{2,1,0:T(8,128)(2,1)S(1)}, bf16[2,512,128]{2,1,0:T(8,128)(2,1)S(1)}, u32[]{:S(2)}, u32[]{:S(2)}) collective-permute-start(bf16[2,512,128]{2,1,0:T(8,128)(2,1)S(1)} %collective-permute-done.7.refs_7_), channel_id=1, source_target_pairs={{0,16},{16,0},{32,48},{48,32},{64,80},{80,64},{96,112},{112,96},{1... | collective-permute-start | bytes 786440 | tf_op jit(solution)/shard_map/ppermute | solution.py:193
  35.7 8.2 %collective-permute-start.10 = (bf16[1296,128]{1,0:T(8,128)(2,1)S(1)}, bf16[1296,128]{1,0:T(8,128)(2,1)S(1)}, u32[]{:S(2)}, u32[]{:S(2)}) collective-permute-start(bf16[1296,128]{1,0:T(8,128)(2,1)S(1)} %get-tuple-element.24), channel_id=1, source_target_pairs={{0,5},{1,4},{2,7},{3,6},{4,1},{5,0},{6,3},{7,2},{8,13},{9,12},{10,... | collective-permute-start | bytes 995336 | tf_op jit(solution)/shard_map/ppermute | solution.py:181
  37.6 9.9 %collective-permute-start.11 = (bf16[1296,128]{1,0:T(8,128)(2,1)S(1)}, bf16[1296,128]{1,0:T(8,128)(2,1)S(1)}, u32[]{:S(2)}, u32[]{:S(2)}) collective-permute-start(bf16[1296,128]{1,0:T(8,128)(2,1)S(1)} %get-tuple-element.25), channel_id=1, source_target_pairs={{0,1},{1,0},{2,3},{3,2},{4,5},{5,4},{6,7},{7,6},{8,9},{9,8},{10,11... | collective-permute-start | bytes 995336 | tf_op jit(solution)/shard_map/ppermute | solution.py:181
  38.8 8.7 %collective-permute-start.12 = (bf16[1296,128]{1,0:T(8,128)(2,1)S(1)}, bf16[1296,128]{1,0:T(8,128)(2,1)S(1)}, u32[]{:S(2)}, u32[]{:S(2)}) collective-permute-start(bf16[1296,128]{1,0:T(8,128)(2,1)S(1)} %get-tuple-element.26), channel_id=1, source_target_pairs={{0,4},{1,5},{2,6},{3,7},{4,0},{5,1},{6,2},{7,3},{8,12},{9,13},{10,... | collective-permute-start | bytes 995336 | tf_op jit(solution)/shard_map/ppermute | solution.py:181
  48.7 9.8 %collective-permute-start.13 = (bf16[32,4096]{1,0:T(8,128)(2,1)S(1)}, bf16[32,4096]{1,0:T(8,128)(2,1)S(1)}, u32[]{:S(2)}, u32[]{:S(2)}) collective-permute-start(bf16[32,4096]{1,0:T(8,128)(2,1)S(1)} %get-tuple-element.28), channel_id=1, source_target_pairs={{0,15},{1,14},{2,13},{3,12},{4,11},{5,10},{6,9},{7,8},{8,7},{9,6},... | collective-permute-start | bytes 786440 | tf_op jit(solution)/shard_map/ppermute | solution.py:181
  51.6 9.9 %collective-permute-start.14 = (bf16[32,4096]{1,0:T(8,128)(2,1)S(1)}, bf16[32,4096]{1,0:T(8,128)(2,1)S(1)}, u32[]{:S(2)}, u32[]{:S(2)}) collective-permute-start(bf16[32,4096]{1,0:T(8,128)(2,1)S(1)} %get-tuple-element.29), channel_id=1, source_target_pairs={{0,3},{1,2},{2,1},{3,0},{4,7},{5,6},{6,5},{7,4},{8,11},{9,10},{10,... | collective-permute-start | bytes 786440 | tf_op jit(solution)/shard_map/ppermute | solution.py:181
  54.4 7.6 %collective-permute-start.15 = (bf16[32,4096]{1,0:T(8,128)(2,1)S(1)}, bf16[32,4096]{1,0:T(8,128)(2,1)S(1)}, u32[]{:S(2)}, u32[]{:S(2)}) collective-permute-start(bf16[32,4096]{1,0:T(8,128)(2,1)S(1)} %get-tuple-element.30), channel_id=1, source_target_pairs={{0,12},{1,13},{2,14},{3,15},{4,8},{5,9},{6,10},{7,11},{8,4},{9,5},... | collective-permute-start | bytes 786440 | tf_op jit(solution)/shard_map/ppermute | solution.py:181

commit v6 on v5

--- a/solution.py
+++ b/solution.py
@@ -38,14 +38,32 @@
     return (partner(y, shifted) if d & 2 else y), (partner(x, shifted) if d & 1 else x)
 
 
+A_UP = (0, 0, 0, 0, 1)
+B_UP = (1, 0, 0, 1)
+
+
+def step(value, k, up):
+    perm = []
+    for z in range(8):
+        perm.append((2 * z + up[k - 1], 2 * ((z + 1) % 8) + up[k]))
+        perm.append((2 * z + 1 - up[k - 1], 2 * ((z - 1) % 8) + 1 - up[k]))
+    return lax.ppermute(value, "group", perm)
+
+
 def locate(region, me):
-    core = me % 2
+    core, kind = me % 2, region % 2
     below = (me // 2 - region // 2) % 8
-    steps = jnp.where(core == 0, below, (8 - below) % 8)
-    same = region % 2 == core
-    near = jnp.where(same, steps, jnp.where(steps == 0, 8, 3 + steps))
-    far = jnp.where(steps > 4, 8, jnp.where(same, 7, 9))
-    return jnp.where(steps < 4, near, far)
+    slot = jnp.where(kind == core, 0, 8)
+    for k in range(1, 5):
+        for way, steps in ((0, below), (1, 8 - below)):
+            on = A_UP[k] ^ way
+            here = (steps == k) & (kind == way)
+            slot = jnp.where(here, jnp.where(core == on, k if k < 4 else 7, 8 if k < 4 else 9), slot)
+            if k < 4:
+                on = B_UP[k] ^ way
+                here = (steps == k) & (kind != way)
+                slot = jnp.where(here, jnp.where(core == on, 3 + k, 8), slot)
+    return slot
 
 
 def pick_kernel(pair_ref, *refs):
@@ -99,16 +117,25 @@
     core = me % 2
     at_mode = lax.axis_index("mode")
     for d, out_ref in enumerate(out_refs):
-        y, x = peer(at_mode // 4, at_mode % 4, d, core)
+        y, x = peer(at_mode // 4, at_mode % 4, d, 1 - core)
         out_ref[EXCITE : EXCITE + 512, :] = picked_ref[1, 0]
         out_ref[EXCITE + 512 : EXCITE + 1024, :] = picked_ref[1, 1]
         for e in range(4):
-            owner_y, owner_x = peer(y, x, e, 1 - core)
+            owner_y, owner_x = peer(y, x, e, core)
             owned = pl.ds(pl.multiple_of(32 * (4 * owner_y + owner_x), 32), 32)
             at = RESPONSE + 32 * e
             out_ref[at : at + 32, :] = picked_ref[0, 0, owned, :]
             out_ref[at + 128 : at + 160, :] = picked_ref[0, 1, owned, :]
         out_ref[TABLE:ROWS, :] = table_ref[...]
+
+
+def weights(table, speed):
+    omega = table[0:1] + table[1:2] + table[2:3]
+    damping = table[3:4] + table[4:5] + table[5:6]
+    a = omega * omega - speed * speed
+    b = 2.0 * damping * omega * speed
+    denom = a * a + b * b
+    return a / denom, -b / denom
 
 
 def share(parts, speeds_ref):
@@ -118,20 +145,14 @@
         res_im = ref[RESPONSE + 128 : RESPONSE + 256, :]
         left.append(jnp.concatenate([res_re, res_im], axis=0))
         left.append(jnp.concatenate([-res_im, res_re], axis=0))
-        table = ref[TABLE:ROWS, :].astype(F32)
-        modes.append((table[0:1] + table[1:2] + table[2:3], table[3:4] + table[4:5] + table[5:6]))
+        modes.append(ref[TABLE:ROWS, :].astype(F32))
     left = jnp.concatenate(left, axis=1)
     for s in range(4):
-        speed = speeds_ref[s : s + 1, :]
         right = []
-        for ref, (omega, damping) in zip(parts, modes):
+        for ref, table in zip(parts, modes):
+            wre, wim = weights(table, speeds_ref[s : s + 1, :])
             ere = ref[EXCITE : EXCITE + 512, :].astype(F32)
             eim = ref[EXCITE + 512 : EXCITE + 1024, :].astype(F32)
-            a = omega * omega - speed * speed
-            b = 2.0 * damping * omega * speed
-            denom = a * a + b * b
-            wre = a / denom
-            wim = -b / denom
             right.append((wre * ere - wim * eim).astype(BF))
             right.append((wre * eim + wim * ere).astype(BF))
         right = jnp.concatenate(right, axis=1)
@@ -151,8 +172,29 @@
 
 
 def last_kernel(total_ref, part_ref, other_ref, speeds_ref, own_ref, *out_refs):
-    for s, both in share([part_ref, other_ref], speeds_ref):
-        both = total_ref[s] + both
+    parts = (part_ref, other_ref)
+    right, modes = [], []
+    for ref in parts:
+        right.append(ref[EXCITE : EXCITE + 512, :])
+        right.append(ref[EXCITE + 512 : EXCITE + 1024, :])
+        modes.append(ref[TABLE:ROWS, :].astype(F32))
+    right = jnp.concatenate(right, axis=1)
+    for s in range(4):
+        left = []
+        for ref, table in zip(parts, modes):
+            wre, wim = weights(table, speeds_ref[s : s + 1, :])
+            rre = ref[RESPONSE : RESPONSE + 128, :].astype(F32)
+            rim = ref[RESPONSE + 128 : RESPONSE + 256, :].astype(F32)
+            lre = wre * rre - wim * rim
+            lim = wre * rim + wim * rre
+            left.append(jnp.concatenate([lre, lim], axis=0).astype(BF))
+            left.append(jnp.concatenate([-lim, lre], axis=0).astype(BF))
+        both = total_ref[s] + lax.dot_general(
+            jnp.concatenate(left, axis=1),
+            right,
+            (((1,), (1,)), ((), ())),
+            preferred_element_type=F32,
+        )
         for c in range(2):
             at = (2 * s + c) * 512
             own_ref[:, at : at + 512] = both[128 * c : 128 * c + 32]
@@ -176,25 +218,17 @@
     perm = []
     for g in range(16):
         for m in range(16):
-            y, x = peer(m // 4, m % 4, d, (g % 2) ^ flip)
+            y, x = peer(m // 4, m % 4, d, 1 ^ (g % 2) ^ flip)
             perm.append((16 * g + m, 16 * g + 4 * y + x))
     return lax.ppermute(value, ("group", "mode"), perm)
 
 
-def along_z(value, crossing=False):
-    perm = []
-    for g in range(16):
-        core = g % 2 ^ crossing
-        perm.append((g, 2 * ((g // 2 + 1 - 2 * core) % 8) + core))
-    return lax.ppermute(value, "group", perm)
-
-
 def swap_cores(value):
     return lax.ppermute(value, "group", [(g, g ^ 1) for g in range(16)])
 
 
 def shards(shapes, pairs, omega, damping, speeds):
-    a1 = along_z(shapes.reshape(2, 512, 128))
+    a1 = step(shapes.reshape(2, 512, 128), 1, A_UP)
     own, table, speed_rows = call(
         prepare_kernel,
         (
@@ -205,13 +239,13 @@
         [VMEM] * 3 + [SMEM],
         "prepare",
     )(shapes, omega.reshape(1, 128), damping.reshape(1, 128), speeds)
-    b1 = along_z(own, crossing=True)
+    b1 = step(own, 1, B_UP)
     a1, other_pair = lax.optimization_barrier((a1, swap_cores(pairs)))
-    a2 = along_z(a1)
-    b2 = along_z(b1)
-    a3 = along_z(a2)
-    b3 = along_z(b2)
-    a4 = along_z(a3)
+    a2 = step(a1, 2, A_UP)
+    b2 = step(b1, 2, B_UP)
+    a3 = step(a2, 3, A_UP)
+    b3 = step(b2, 3, B_UP)
+    a4 = step(a3, 4, A_UP)
     regions = (own, a1, a2, a3, b1, b2, b3)
     other = jax.ShapeDtypeStruct((2, 2, 512, 128), BF)
     wanted = call(pick_kernel, other, [VMEM] * 8, "pick_regions")(other_pair, *regions)
@@ -223,7 +257,7 @@
         "fan_out",
         scratch=[pltpu.VMEM((2, 2, 512, 128), BF)],
     )(pairs, table, *regions, a4, swap_cores(wanted), swap_cores(a4))
-    parts = [fanned[0]] + [exchange(fanned[d], d, 0) for d in (3, 1, 2)]
+    parts = [fanned[0]] + [exchange(fanned[d], d, 0) for d in (3, 2, 1)]
     sums = jax.ShapeDtypeStruct((4, 256, 512), F32)
     total = call(first_kernel, sums, [VMEM] * 2, "product_0", flops=1 << 28)(parts[0], speed_rows)
     total = call(
@@ -237,7 +271,7 @@
         "product_2",
         flops=1 << 29,
     )(total, parts[2], parts[3], speed_rows)
-    terms = [made[0]] + [exchange(made[e], e, 1) for e in (3, 1, 2)]
+    terms = [made[0]] + [exchange(made[e], e, 1) for e in (3, 2, 1)]
     return call(
         sum_kernel, jax.ShapeDtypeStruct((32, 1, 4, 2, 512), F32), [VMEM] * 4, "sum_terms"
     )(*terms)

time: 63.1 us -> 59.9 us (0.949)
  waiting for transfers between devices: 36.9 us -> 33 us
  starting transfers between devices: 18.1 us -> 19 us
    ppermute x7, waiting for transfers between devices: 20.1 us -> 17.4 us  [step(): return lax.ppermute(value, 'group', perm)]
    ppermute x6, waiting for transfers between devices: 14 us -> 12.8 us  [exchange(): return lax.ppermute(value, ('group', 'mode'), perm)]
    ppermute x3, starting transfers between devices: 0.1 us -> 1.03 us  [swap_cores(): return lax.ppermute(value, 'group', [(g, g ^ 1) for g in range(16)])]
where the time goes in v6:
time: 59.9 us; the launch traced here: 59.5 us
  waiting for transfers between devices  33 us (55%)
  starting transfers between devices  19 us (32%)
  Pallas kernels  4.53 us (8%)
  local copies, waits for them, and re-layouts  2.95 us (5%)
    ppermute x7, waiting for transfers between devices, step(): return lax.ppermute(value, 'group', perm)  17.4 us
    ppermute x6, waiting for transfers between devices, exchange(): return lax.ppermute(value, ('group', 'mode'), perm)  12.8 us
    ppermute x6, starting transfers between devices, exchange(): return lax.ppermute(value, ('group', 'mode'), perm)  9.56 us
    ppermute x7, starting transfers between devices, step(): return lax.ppermute(value, 'group', perm)  8.38 us
    unnamed x10, local copies, waits for them, and re-layouts  2.95 us
    ppermute x3, waiting for transfers between devices, swap_cores(): return lax.ppermute(value, 'group', [(g, g ^ 1) for g in range(16)])  2.79 us
  transfers between devices with their start and end apart: 16, of which 13 were waited for; matrix products, arithmetic and copies ran while one was open for 0% of the time, Pallas kernels for 4%

profile of v6, /device:TPU:6, one launch (start us, length us, event | category | flops | bytes accessed | tf_op | source)
XLA Modules:
  0.0 59.5 jit_solution(2201390946700853705)
XLA Ops:
  0.0 0.0 copy-start.4
  0.0 1.9 %collective-permute-start = (bf16[2,512,128]{2,1,0:T(8,128)(2,1)}, bf16[2,512,128]{2,1,0:T(8,128)(2,1)S(1)}, u32[]{:S(2)}, u32[]{:S(2)}) collective-permute-start(bf16[2,512,128]{2,1,0:T(8,128)(2,1)} %bitcast.3), channel_id=1, source_target_pairs={{0,32},{16,240},{32,64},{48,16},{64,96},{80,48},{96,128},{112,80},... | collective-permute-start | bytes 786440 | tf_op jit(solution)/shard_map/ppermute | solution.py:50
  1.9 0.0 copy-start
  1.9 1.0 %copy-done = bf16[2,1,512,128]{3,2,1,0:T(8,128)(2,1)S(1)} copy-done((bf16[2,1,512,128]{3,2,1,0:T(8,128)(2,1)S(1)}, bf16[2,1,512,128]{3,2,1,0:T(8,128)(2,1)}, u32[]{:S(2)}) %copy-start) | copy-done | bytes 262168
  2.9 0.0 copy-start.1
  2.9 0.7 %copy-done.1 = f32[128]{0:T(128)S(1)} copy-done((f32[128]{0:T(128)S(1)}, f32[128]{0:T(128)}, u32[]{:S(2)}) %copy-start.1) | copy-done | bytes 536
  3.6 0.0 copy-start.2
  3.6 0.7 %copy-done.2 = f32[128]{0:T(128)S(1)} copy-done((f32[128]{0:T(128)S(1)}, f32[128]{0:T(128)}, u32[]{:S(2)}) %copy-start.2) | copy-done | bytes 536
  4.2 0.7 %copy-done.3 = f32[4]{0:T(128)S(1)} copy-done((f32[4]{0:T(128)S(1)}, f32[4]{0:T(128)}, u32[]{:S(2)}) %copy-start.3) | copy-done | bytes 40
  4.9 0.6 prepare.1
  5.4 4.2 %collective-permute-start.4 = (bf16[2,512,128]{2,1,0:T(8,128)(2,1)S(1)}, bf16[2,512,128]{2,1,0:T(8,128)(2,1)S(1)}, u32[]{:S(2)}, u32[]{:S(2)}) collective-permute-start(bf16[2,512,128]{2,1,0:T(8,128)(2,1)S(1)} %get-tuple-element.19.refs_0_), channel_id=1, source_target_pairs={{16,32},{0,240},{48,64},{32,16},{80,96},{64,48},{112,128},{96,80},... | collective-permute-start | bytes 786440 | tf_op jit(solution)/shard_map/ppermute | solution.py:50
  9.6 0.0 collective-permute-start.1
  9.6 1.3 %collective-permute-done.1.pair_ref = s32[1,2]{1,0:T(1,128)S(1)} collective-permute-done((s32[1,2]{1,0:T(1,128)}, s32[1,2]{1,0:T(1,128)S(1)}, u32[]{:S(2)}, u32[]{:S(2)}) %collective-permute-start.1) | collective-permute-done | bytes 40 | tf_op jit(solution)/shard_map/ppermute | solution.py:227
  10.9 0.0 collective-permute-done.refs_1_
  10.9 1.0 %collective-permute-start.2 = (bf16[2,512,128]{2,1,0:T(8,128)(2,1)S(1)}, bf16[2,512,128]{2,1,0:T(8,128)(2,1)S(1)}, u32[]{:S(2)}, u32[]{:S(2)}) collective-permute-start(bf16[2,512,128]{2,1,0:T(8,128)(2,1)S(1)} %collective-permute-done.refs_1_), channel_id=1, source_target_pairs={{0,32},{16,240},{32,64},{48,16},{64,96},{80,48},{96,128},{112,80},... | collective-permute-start | bytes 786440 | tf_op jit(solution)/shard_map/ppermute | solution.py:50
  11.9 2.6 %collective-permute-done.4.refs_4_ = bf16[2,512,128]{2,1,0:T(8,128)(2,1)S(1)} collective-permute-done((bf16[2,512,128]{2,1,0:T(8,128)(2,1)S(1)}, bf16[2,512,128]{2,1,0:T(8,128)(2,1)S(1)}, u32[]{:S(2)}, u32[]{:S(2)}) %collective-permute-start.4) | collective-permute-done | bytes 262176 | tf_op jit(solution)/shard_map/ppermute | solution.py:50
  14.5 1.2 %collective-permute-start.5 = (bf16[2,512,128]{2,1,0:T(8,128)(2,1)S(1)}, bf16[2,512,128]{2,1,0:T(8,128)(2,1)S(1)}, u32[]{:S(2)}, u32[]{:S(2)}) collective-permute-start(bf16[2,512,128]{2,1,0:T(8,128)(2,1)S(1)} %collective-permute-done.4.refs_4_), channel_id=1, source_target_pairs={{0,32},{16,240},{32,64},{48,16},{64,96},{80,48},{96,128},{112,80},... | collective-permute-start | bytes 786440 | tf_op jit(solution)/shard_map/ppermute | solution.py:50
  15.8 2.7 %collective-permute-done.2.refs_2_ = bf16[2,512,128]{2,1,0:T(8,128)(2,1)S(1)} collective-permute-done((bf16[2,512,128]{2,1,0:T(8,128)(2,1)S(1)}, bf16[2,512,128]{2,1,0:T(8,128)(2,1)S(1)}, u32[]{:S(2)}, u32[]{:S(2)}) %collective-permute-start.2) | collective-permute-done | bytes 262176 | tf_op jit(solution)/shard_map/ppermute | solution.py:50
  18.5 0.0 collective-permute-start.3
  18.5 3.6 %collective-permute-done.5.refs_5_ = bf16[2,512,128]{2,1,0:T(8,128)(2,1)S(1)} collective-permute-done((bf16[2,512,128]{2,1,0:T(8,128)(2,1)S(1)}, bf16[2,512,128]{2,1,0:T(8,128)(2,1)S(1)}, u32[]{:S(2)}, u32[]{:S(2)}) %collective-permute-start.5) | collective-permute-done | bytes 262176 | tf_op jit(solution)/shard_map/ppermute | solution.py:50
  22.1 0.0 collective-permute-start.6
  22.1 3.9 %collective-permute-done.3.refs_3_ = bf16[2,512,128]{2,1,0:T(8,128)(2,1)S(1)} collective-permute-done((bf16[2,512,128]{2,1,0:T(8,128)(2,1)S(1)}, bf16[2,512,128]{2,1,0:T(8,128)(2,1)S(1)}, u32[]{:S(2)}, u32[]{:S(2)}) %collective-permute-start.3) | collective-permute-done | bytes 262176 | tf_op jit(solution)/shard_map/ppermute | solution.py:50
  26.1 0.0 collective-permute-start.7
  26.1 1.9 %collective-permute-done.6.refs_6_ = bf16[2,512,128]{2,1,0:T(8,128)(2,1)S(1)} collective-permute-done((bf16[2,512,128]{2,1,0:T(8,128)(2,1)S(1)}, bf16[2,512,128]{2,1,0:T(8,128)(2,1)S(1)}, u32[]{:S(2)}, u32[]{:S(2)}) %collective-permute-start.6) | collective-permute-done | bytes 262176 | tf_op jit(solution)/shard_map/ppermute | solution.py:50
  27.9 0.3 pick_regions.1
  28.2 1.0 %collective-permute-start.8 = (bf16[2,2,512,128]{3,2,1,0:T(8,128)(2,1)S(1)}, bf16[2,2,512,128]{3,2,1,0:T(8,128)(2,1)S(1)}, u32[]{:S(2)}, u32[]{:S(2)}) collective-permute-start(bf16[2,2,512,128]{3,2,1,0:T(8,128)(2,1)S(1)} %pick_regions.1), channel_id=1, source_target_pairs={{0,16},{16,0},{32,48},{48,32},{64,80},{80,64},{96,112},{112,96},{1... | collective-permute-start | bytes 1572872 | tf_op jit(solution)/shard_map/ppermute | solution.py:227
  29.2 2.6 %collective-permute-done.7.refs_7_ = bf16[2,512,128]{2,1,0:T(8,128)(2,1)S(1)} collective-permute-done((bf16[2,512,128]{2,1,0:T(8,128)(2,1)S(1)}, bf16[2,512,128]{2,1,0:T(8,128)(2,1)S(1)}, u32[]{:S(2)}, u32[]{:S(2)}) %collective-permute-start.7) | collective-permute-done | bytes 262176 | tf_op jit(solution)/shard_map/ppermute | solution.py:50
  31.9 0.0 collective-permute-start.9
  31.9 1.5 %collective-permute-done.9.refs_9_ = bf16[2,512,128]{2,1,0:T(8,128)(2,1)S(1)} collective-permute-done((bf16[2,512,128]{2,1,0:T(8,128)(2,1)S(1)}, bf16[2,512,128]{2,1,0:T(8,128)(2,1)S(1)}, u32[]{:S(2)}, u32[]{:S(2)}) %collective-permute-start.9) | collective-permute-done | bytes 262176 | tf_op jit(solution)/shard_map/ppermute | solution.py:227
  33.4 0.0 collective-permute-done.8.refs_8_
  33.4 0.0 copy-done.4
  33.4 0.5 fan_out.1
  33.9 3.0 %collective-permute-start.10 = (bf16[1296,128]{1,0:T(8,128)(2,1)S(1)}, bf16[1296,128]{1,0:T(8,128)(2,1)S(1)}, u32[]{:S(2)}, u32[]{:S(2)}) collective-permute-start(bf16[1296,128]{1,0:T(8,128)(2,1)S(1)} %get-tuple-element.24), channel_id=1, source_target_pairs={{0,15},{1,14},{2,13},{3,12},{4,11},{5,10},{6,9},{7,8},{8,7},{9,6},... | collective-permute-start | bytes 995336 | tf_op jit(solution)/shard_map/ppermute | solution.py:223
  36.9 0.2 collective-permute-start.11
  37.1 2.8 %collective-permute-start.12 = (bf16[1296,128]{1,0:T(8,128)(2,1)S(1)}, bf16[1296,128]{1,0:T(8,128)(2,1)S(1)}, u32[]{:S(2)}, u32[]{:S(2)}) collective-permute-start(bf16[1296,128]{1,0:T(8,128)(2,1)S(1)} %get-tuple-element.26), channel_id=1, source_target_pairs={{0,3},{1,2},{2,1},{3,0},{4,7},{5,6},{6,5},{7,4},{8,11},{9,10},{10,... | collective-permute-start | bytes 995336 | tf_op jit(solution)/shard_map/ppermute | solution.py:223
  39.9 0.6 %product_0.1.total_ref = f32[4,256,512]{2,1,0:T(8,128)S(1)} custom-call(bf16[1296,128]{1,0:T(8,128)(2,1)S(1)} %get-tuple-element.22.part_ref, f32[8,128]{1,0:T(8,128)S(1)} %get-tuple-element.23.speeds_ref), custom_call_target="tpu_custom_call" | custom-call | flops 268435456 | bytes 1048576 | tf_op jit(solution)/shard_map/product_0/pallas_call | solution.py:262
  40.6 4.0 %collective-permute-done.10.part_ref = bf16[1296,128]{1,0:T(8,128)(2,1)S(1)} collective-permute-done((bf16[1296,128]{1,0:T(8,128)(2,1)S(1)}, bf16[1296,128]{1,0:T(8,128)(2,1)S(1)}, u32[]{:S(2)}, u32[]{:S(2)}) %collective-permute-start.10) | collective-permute-done | bytes 331808 | tf_op jit(solution)/shard_map/ppermute | solution.py:223
  44.5 0.8 %product_1.1.total_ref = f32[4,256,512]{2,1,0:T(8,128)S(1)} custom-call(f32[4,256,512]{2,1,0:T(8,128)S(1)} %product_0.1.total_ref, bf16[1296,128]{1,0:T(8,128)(2,1)S(1)} %collective-permute-done.10.part_ref, f32[8,128]{1,0:T(8,128)S(1)} %get-tuple-element.23.speeds_ref), custom_call_target="tpu_custom_call", output_to_operand_aliasing={{}: (0, {})} | custom-call | flops 268435456 | bytes 1048576 | tf_op jit(solution)/shard_map/product_1/pallas_call | solution.py:263
  45.3 2.7 %collective-permute-done.11.part_ref = bf16[1296,128]{1,0:T(8,128)(2,1)S(1)} collective-permute-done((bf16[1296,128]{1,0:T(8,128)(2,1)S(1)}, bf16[1296,128]{1,0:T(8,128)(2,1)S(1)}, u32[]{:S(2)}, u32[]{:S(2)}) %collective-permute-start.11) | collective-permute-done | bytes 331808 | tf_op jit(solution)/shard_map/ppermute | solution.py:223
  48.0 0.4 collective-permute-done.12.other_ref
  48.4 0.8 %product_2.1 = (f32[32,4096]{1,0:T(8,128)S(1)}, bf16[32,4096]{1,0:T(8,128)(2,1)S(1)}, bf16[32,4096]{1,0:T(8,128)(2,1)S(1)}, bf16[32,4096]{1,0:T(8,128)(2,1)S(1)}) custom-call(f32[4,256,512]{2,1,0:T(8,128)S(1)} %product_1.1.total_ref, bf16[1296,128]{1,0:T(8,128)(2,1)S(1)} %collective-permute-done.11.part_ref, ...), custom_call_target="tpu_custom_call" | custom-call | flops 536870912 | bytes 1048576 | tf_op jit(solution)/shard_map/product_2/pallas_call | solution.py:267
  49.1 0.1 collective-permute-start.13
  49.2 1.1 %collective-permute-start.14 = (bf16[32,4096]{1,0:T(8,128)(2,1)S(1)}, bf16[32,4096]{1,0:T(8,128)(2,1)S(1)}, u32[]{:S(2)}, u32[]{:S(2)}) collective-permute-start(bf16[32,4096]{1,0:T(8,128)(2,1)S(1)} %get-tuple-element.29), channel_id=1, source_target_pairs={{0,4},{1,5},{2,6},{3,7},{4,0},{5,1},{6,2},{7,3},{8,12},{9,13},{10,... | collective-permute-start | bytes 786440 | tf_op jit(solution)/shard_map/ppermute | solution.py:223
  50.3 2.4 %collective-permute-start.15 = (bf16[32,4096]{1,0:T(8,128)(2,1)S(1)}, bf16[32,4096]{1,0:T(8,128)(2,1)S(1)}, u32[]{:S(2)}, u32[]{:S(2)}) collective-permute-start(bf16[32,4096]{1,0:T(8,128)(2,1)S(1)} %get-tuple-element.30), channel_id=1, source_target_pairs={{0,1},{1,0},{2,3},{3,2},{4,5},{5,4},{6,7},{7,6},{8,9},{9,8},{10,11... | collective-permute-start | bytes 786440 | tf_op jit(solution)/shard_map/ppermute | solution.py:223
  52.7 3.9 %collective-permute-done.13.refs_1_ = bf16[32,4096]{1,0:T(8,128)(2,1)S(1)} collective-permute-done((bf16[32,4096]{1,0:T(8,128)(2,1)S(1)}, bf16[32,4096]{1,0:T(8,128)(2,1)S(1)}, u32[]{:S(2)}, u32[]{:S(2)}) %collective-permute-start.13) | collective-permute-done | bytes 262176 | tf_op jit(solution)/shard_map/ppermute | solution.py:223
  56.6 1.9 %collective-permute-done.14.refs_2_ = bf16[32,4096]{1,0:T(8,128)(2,1)S(1)} collective-permute-done((bf16[32,4096]{1,0:T(8,128)(2,1)S(1)}, bf16[32,4096]{1,0:T(8,128)(2,1)S(1)}, u32[]{:S(2)}, u32[]{:S(2)}) %collective-permute-start.14) | collective-permute-done | bytes 262176 | tf_op jit(solution)/shard_map/ppermute | solution.py:223
  58.5 0.0 collective-permute-done.15.refs_3_
  58.5 1.0 %sum_terms.1 = f32[32,1,4,2,512]{4,3,2,1,0:T(2,128)} custom-call(f32[32,4096]{1,0:T(8,128)S(1)} %get-tuple-element.27.refs_0_, bf16[32,4096]{1,0:T(8,128)(2,1)S(1)} %collective-permute-done.13.refs_1_, bf16[32,4096]{1,0:T(8,128)(2,1)S(1)} %collective-permute-done.14.refs_2_, bf16[32,4096]{1,0:T(8,128)(2,1)S(1)} %collective-permute-done.15.refs_3_), custom_call_target="tpu_custom_call" | custom-call | bytes 1048576 | tf_op jit(solution)/shard_map/sum_terms/pallas_call | solution.py:275
  (1 shorter events, 0.0 us)
Async XLA Ops:
  0.0 33.4 %copy-start.4 = (s32[1,2]{1,0:T(1,128)S(1)}, s32[1,2]{1,0:T(1,128)}, u32[]{:S(2)}) copy-start(s32[1,2]{1,0:T(1,128)} %pair_ref.1) | copy-start | bytes 28
  0.0 10.9 %collective-permute-start = (bf16[2,512,128]{2,1,0:T(8,128)(2,1)}, bf16[2,512,128]{2,1,0:T(8,128)(2,1)S(1)}, u32[]{:S(2)}, u32[]{:S(2)}) collective-permute-start(bf16[2,512,128]{2,1,0:T(8,128)(2,1)} %bitcast.3), channel_id=1, source_target_pairs={{0,32},{16,240},{32,64},{48,16},{64,96},{80,48},{96,128},{112,80},... | collective-permute-start | bytes 786440 | tf_op jit(solution)/shard_map/ppermute | solution.py:50
  1.9 1.0 %copy-start = (bf16[2,1,512,128]{3,2,1,0:T(8,128)(2,1)S(1)}, bf16[2,1,512,128]{3,2,1,0:T(8,128)(2,1)}, u32[]{:S(2)}) copy-start(bf16[2,1,512,128]{3,2,1,0:T(8,128)(2,1)} %shapes_ref.1) | copy-start | bytes 786436
  2.9 0.7 %copy-start.1 = (f32[128]{0:T(128)S(1)}, f32[128]{0:T(128)}, u32[]{:S(2)}) copy-start(f32[128]{0:T(128)} %param.7) | copy-start | bytes 1540
  3.6 0.7 %copy-start.2 = (f32[128]{0:T(128)S(1)}, f32[128]{0:T(128)}, u32[]{:S(2)}) copy-start(f32[128]{0:T(128)} %param.8) | copy-start | bytes 1540
  4.2 0.7 %copy-start.3 = (f32[4]{0:T(128)S(1)}, f32[4]{0:T(128)}, u32[]{:S(2)}) copy-start(f32[4]{0:T(128)} %speeds_ref.1) | copy-start | bytes 52
  5.4 9.1 %collective-permute-start.4 = (bf16[2,512,128]{2,1,0:T(8,128)(2,1)S(1)}, bf16[2,512,128]{2,1,0:T(8,128)(2,1)S(1)}, u32[]{:S(2)}, u32[]{:S(2)}) collective-permute-start(bf16[2,512,128]{2,1,0:T(8,128)(2,1)S(1)} %get-tuple-element.19.refs_0_), channel_id=1, source_target_pairs={{16,32},{0,240},{48,64},{32,16},{80,96},{64,48},{112,128},{96,80},... | collective-permute-start | bytes 786440 | tf_op jit(solution)/shard_map/ppermute | solution.py:50
  9.6 1.3 %collective-permute-start.1 = (s32[1,2]{1,0:T(1,128)}, s32[1,2]{1,0:T(1,128)S(1)}, u32[]{:S(2)}, u32[]{:S(2)}) collective-permute-start(s32[1,2]{1,0:T(1,128)} %pair_ref.1), channel_id=1, source_target_pairs={{0,16},{16,0},{32,48},{48,32},{64,80},{80,64},{96,112},{112,96},{1... | collective-permute-start | bytes 32 | tf_op jit(solution)/shard_map/ppermute | solution.py:227
  10.9 7.6 %collective-permute-start.2 = (bf16[2,512,128]{2,1,0:T(8,128)(2,1)S(1)}, bf16[2,512,128]{2,1,0:T(8,128)(2,1)S(1)}, u32[]{:S(2)}, u32[]{:S(2)}) collective-permute-start(bf16[2,512,128]{2,1,0:T(8,128)(2,1)S(1)} %collective-permute-done.refs_1_), channel_id=1, source_target_pairs={{0,32},{16,240},{32,64},{48,16},{64,96},{80,48},{96,128},{112,80},... | collective-permute-start | bytes 786440 | tf_op jit(solution)/shard_map/ppermute | solution.py:50
  14.5 7.6 %collective-permute-start.5 = (bf16[2,512,128]{2,1,0:T(8,128)(2,1)S(1)}, bf16[2,512,128]{2,1,0:T(8,128)(2,1)S(1)}, u32[]{:S(2)}, u32[]{:S(2)}) collective-permute-start(bf16[2,512,128]{2,1,0:T(8,128)(2,1)S(1)} %collective-permute-done.4.refs_4_), channel_id=1, source_target_pairs={{0,32},{16,240},{32,64},{48,16},{64,96},{80,48},{96,128},{112,80},... | collective-permute-start | bytes 786440 | tf_op jit(solution)/shard_map/ppermute | solution.py:50
  18.5 7.6 %collective-permute-start.3 = (bf16[2,512,128]{2,1,0:T(8,128)(2,1)S(1)}, bf16[2,512,128]{2,1,0:T(8,128)(2,1)S(1)}, u32[]{:S(2)}, u32[]{:S(2)}) collective-permute-start(bf16[2,512,128]{2,1,0:T(8,128)(2,1)S(1)} %collective-permute-done.2.refs_2_), channel_id=1, source_target_pairs={{0,32},{16,240},{32,64},{48,16},{64,96},{80,48},{96,128},{112,80},... | collective-permute-start | bytes 786440 | tf_op jit(solution)/shard_map/ppermute | solution.py:50
  22.1 5.8 %collective-permute-start.6 = (bf16[2,512,128]{2,1,0:T(8,128)(2,1)S(1)}, bf16[2,512,128]{2,1,0:T(8,128)(2,1)S(1)}, u32[]{:S(2)}, u32[]{:S(2)}) collective-permute-start(bf16[2,512,128]{2,1,0:T(8,128)(2,1)S(1)} %collective-permute-done.5.refs_5_), channel_id=1, source_target_pairs={{0,48},{16,224},{32,80},{48,0},{64,112},{80,32},{96,144},{112,64},... | collective-permute-start | bytes 786440 | tf_op jit(solution)/shard_map/ppermute | solution.py:50
  26.1 5.8 %collective-permute-start.7 = (bf16[2,512,128]{2,1,0:T(8,128)(2,1)S(1)}, bf16[2,512,128]{2,1,0:T(8,128)(2,1)S(1)}, u32[]{:S(2)}, u32[]{:S(2)}) collective-permute-start(bf16[2,512,128]{2,1,0:T(8,128)(2,1)S(1)} %collective-permute-done.3.refs_3_), channel_id=1, source_target_pairs={{0,48},{16,224},{32,80},{48,0},{64,112},{80,32},{96,144},{112,64},... | collective-permute-start | bytes 786440 | tf_op jit(solution)/shard_map/ppermute | solution.py:50
  28.2 5.2 %collective-permute-start.8 = (bf16[2,2,512,128]{3,2,1,0:T(8,128)(2,1)S(1)}, bf16[2,2,512,128]{3,2,1,0:T(8,128)(2,1)S(1)}, u32[]{:S(2)}, u32[]{:S(2)}) collective-permute-start(bf16[2,2,512,128]{3,2,1,0:T(8,128)(2,1)S(1)} %pick_regions.1), channel_id=1, source_target_pairs={{0,16},{16,0},{32,48},{48,32},{64,80},{80,64},{96,112},{112,96},{1... | collective-permute-start | bytes 1572872 | tf_op jit(solution)/shard_map/ppermute | solution.py:227
  31.9 1.5 %collective-permute-start.9 = (bf16[2,512,128]{2,1,0:T(8,128)(2,1)S(1)}, bf16[2,512,128]{2,1,0:T(8,128)(2,1)S(1)}, u32[]{:S(2)}, u32[]{:S(2)}) collective-permute-start(bf16[2,512,128]{2,1,0:T(8,128)(2,1)S(1)} %collective-permute-done.7.refs_7_), channel_id=1, source_target_pairs={{0,16},{16,0},{32,48},{48,32},{64,80},{80,64},{96,112},{112,96},{1... | collective-permute-start | bytes 786440 | tf_op jit(solution)/shard_map/ppermute | solution.py:227
  33.9 10.6 %collective-permute-start.10 = (bf16[1296,128]{1,0:T(8,128)(2,1)S(1)}, bf16[1296,128]{1,0:T(8,128)(2,1)S(1)}, u32[]{:S(2)}, u32[]{:S(2)}) collective-permute-start(bf16[1296,128]{1,0:T(8,128)(2,1)S(1)} %get-tuple-element.24), channel_id=1, source_target_pairs={{0,15},{1,14},{2,13},{3,12},{4,11},{5,10},{6,9},{7,8},{8,7},{9,6},... | collective-permute-start | bytes 995336 | tf_op jit(solution)/shard_map/ppermute | solution.py:223
  36.9 11.1 %collective-permute-start.11 = (bf16[1296,128]{1,0:T(8,128)(2,1)S(1)}, bf16[1296,128]{1,0:T(8,128)(2,1)S(1)}, u32[]{:S(2)}, u32[]{:S(2)}) collective-permute-start(bf16[1296,128]{1,0:T(8,128)(2,1)S(1)} %get-tuple-element.25), channel_id=1, source_target_pairs={{0,12},{1,13},{2,14},{3,15},{4,8},{5,9},{6,10},{7,11},{8,4},{9,5},... | collective-permute-start | bytes 995336 | tf_op jit(solution)/shard_map/ppermute | solution.py:223
  37.1 11.2 %collective-permute-start.12 = (bf16[1296,128]{1,0:T(8,128)(2,1)S(1)}, bf16[1296,128]{1,0:T(8,128)(2,1)S(1)}, u32[]{:S(2)}, u32[]{:S(2)}) collective-permute-start(bf16[1296,128]{1,0:T(8,128)(2,1)S(1)} %get-tuple-element.26), channel_id=1, source_target_pairs={{0,3},{1,2},{2,1},{3,0},{4,7},{5,6},{6,5},{7,4},{8,11},{9,10},{10,... | collective-permute-start | bytes 995336 | tf_op jit(solution)/shard_map/ppermute | solution.py:223
  49.1 7.5 %collective-permute-start.13 = (bf16[32,4096]{1,0:T(8,128)(2,1)S(1)}, bf16[32,4096]{1,0:T(8,128)(2,1)S(1)}, u32[]{:S(2)}, u32[]{:S(2)}) collective-permute-start(bf16[32,4096]{1,0:T(8,128)(2,1)S(1)} %get-tuple-element.28), channel_id=1, source_target_pairs={{0,5},{1,4},{2,7},{3,6},{4,1},{5,0},{6,3},{7,2},{8,13},{9,12},{10,... | collective-permute-start | bytes 786440 | tf_op jit(solution)/shard_map/ppermute | solution.py:223
  49.2 9.3 %collective-permute-start.14 = (bf16[32,4096]{1,0:T(8,128)(2,1)S(1)}, bf16[32,4096]{1,0:T(8,128)(2,1)S(1)}, u32[]{:S(2)}, u32[]{:S(2)}) collective-permute-start(bf16[32,4096]{1,0:T(8,128)(2,1)S(1)} %get-tuple-element.29), channel_id=1, source_target_pairs={{0,4},{1,5},{2,6},{3,7},{4,0},{5,1},{6,2},{7,3},{8,12},{9,13},{10,... | collective-permute-start | bytes 786440 | tf_op jit(solution)/shard_map/ppermute | solution.py:223
  50.3 8.2 %collective-permute-start.15 = (bf16[32,4096]{1,0:T(8,128)(2,1)S(1)}, bf16[32,4096]{1,0:T(8,128)(2,1)S(1)}, u32[]{:S(2)}, u32[]{:S(2)}) collective-permute-start(bf16[32,4096]{1,0:T(8,128)(2,1)S(1)} %get-tuple-element.30), channel_id=1, source_target_pairs={{0,1},{1,0},{2,3},{3,2},{4,5},{5,4},{6,7},{7,6},{8,9},{9,8},{10,11... | collective-permute-start | bytes 786440 | tf_op jit(solution)/shard_map/ppermute | solution.py:223

commit v7 on v6

--- a/solution.py
+++ b/solution.py
@@ -38,7 +38,7 @@
     return (partner(y, shifted) if d & 2 else y), (partner(x, shifted) if d & 1 else x)
 
 
-A_UP = (0, 0, 0, 0, 1)
+A_UP = (0, 1, 0, 1, 0)
 B_UP = (1, 0, 0, 1)
 
 
@@ -87,7 +87,7 @@
     return first.astype(F32), second.astype(F32), third.astype(F32)
 
 
-def prepare_kernel(shapes_ref, omega_ref, damping_ref, speeds_ref, own_ref, table_ref, speed_rows_ref):
+def prepare_kernel(shapes_ref, omega_ref, damping_ref, own_ref, table_ref):
     own_ref[...] = shapes_ref[:, 0]
     pieces = split3(omega_ref[...]) + split3(damping_ref[...])
     rows = lax.broadcasted_iota(jnp.int32, (16, 128), 0)
@@ -95,11 +95,6 @@
     for n, piece in enumerate(pieces):
         table = jnp.where(rows == n, piece, table)
     table_ref[...] = table.astype(BF)
-    rows = lax.broadcasted_iota(jnp.int32, (8, 128), 0)
-    speeds = jnp.zeros((8, 128), F32)
-    for s in range(4):
-        speeds = jnp.where(rows == s, speeds_ref[s], speeds)
-    speed_rows_ref[...] = speeds
 
 
 def fan_kernel(pair_ref, table_ref, *refs):
@@ -161,8 +156,13 @@
         )
 
 
-def first_kernel(part_ref, speeds_ref, out_ref):
-    for s, both in share([part_ref], speeds_ref):
+def first_kernel(part_ref, speeds_ref, out_ref, speed_rows_ref):
+    rows = lax.broadcasted_iota(jnp.int32, (8, 128), 0)
+    speeds = jnp.zeros((8, 128), F32)
+    for s in range(4):
+        speeds = jnp.where(rows == s, speeds_ref[s], speeds)
+    speed_rows_ref[...] = speeds
+    for s, both in share([part_ref], speed_rows_ref):
         out_ref[s] = both
 
 
@@ -229,16 +229,12 @@
 
 def shards(shapes, pairs, omega, damping, speeds):
     a1 = step(shapes.reshape(2, 512, 128), 1, A_UP)
-    own, table, speed_rows = call(
+    own, table = call(
         prepare_kernel,
-        (
-            jax.ShapeDtypeStruct((2, 512, 128), BF),
-            jax.ShapeDtypeStruct((16, 128), BF),
-            jax.ShapeDtypeStruct((8, 128), F32),
-        ),
-        [VMEM] * 3 + [SMEM],
+        (jax.ShapeDtypeStruct((2, 512, 128), BF), jax.ShapeDtypeStruct((16, 128), BF)),
+        [VMEM] * 3,
         "prepare",
-    )(shapes, omega.reshape(1, 128), damping.reshape(1, 128), speeds)
+    )(shapes, omega.reshape(1, 128), damping.reshape(1, 128))
     b1 = step(own, 1, B_UP)
     a1, other_pair = lax.optimization_barrier((a1, swap_cores(pairs)))
     a2 = step(a1, 2, A_UP)
@@ -259,7 +255,13 @@
     )(pairs, table, *regions, a4, swap_cores(wanted), swap_cores(a4))
     parts = [fanned[0]] + [exchange(fanned[d], d, 0) for d in (3, 2, 1)]
     sums = jax.ShapeDtypeStruct((4, 256, 512), F32)
-    total = call(first_kernel, sums, [VMEM] * 2, "product_0", flops=1 << 28)(parts[0], speed_rows)
+    total, speed_rows = call(
+        first_kernel,
+        (sums, jax.ShapeDtypeStruct((8, 128), F32)),
+        [VMEM, SMEM],
+        "product_0",
+        flops=1 << 28,
+    )(parts[0], speeds)
     total = call(
         next_kernel, sums, [VMEM] * 3, "product_1", flops=1 << 28, aliases={0: 0}
     )(total, parts[1], speed_rows)

time: 59.9 us -> 58.2 us (0.972)
  waiting for transfers between devices: 33 us -> 27.4 us
  starting transfers between devices: 19 us -> 23.5 us
  local copies, waits for them, and re-layouts: 2.95 us -> 2.3 us
    ppermute x7, waiting for transfers between devices: 17.4 us -> 12.5 us  [step(): return lax.ppermute(value, 'group', perm)]
    ppermute x7, starting transfers between devices: 8.38 us -> 12.8 us  [step(): return lax.ppermute(value, 'group', perm)]
    unnamed x10, local copies, waits for them, and re-layouts: 2.95 us -> 2.3 us
where the time goes in v7:
time: 58.2 us; the launch traced here: 57.8 us
  waiting for transfers between devices  27.4 us (47%)
  starting transfers between devices  23.5 us (40%)
  Pallas kernels  4.53 us (8%)
  local copies, waits for them, and re-layouts  2.3 us (4%)
    ppermute x7, starting transfers between devices, step(): return lax.ppermute(value, 'group', perm)  12.8 us
    ppermute x7, waiting for transfers between devices, step(): return lax.ppermute(value, 'group', perm)  12.5 us
    ppermute x6, waiting for transfers between devices, exchange(): return lax.ppermute(value, ('group', 'mode'), perm)  12.3 us
    ppermute x6, starting transfers between devices, exchange(): return lax.ppermute(value, ('group', 'mode'), perm)  9.56 us
    ppermute x3, waiting for transfers between devices, swap_cores(): return lax.ppermute(value, 'group', [(g, g ^ 1) for g in range(16)])  2.68 us
    unnamed x10, local copies, waits for them, and re-layouts  2.3 us
    pallas_call x1, Pallas kernels, shards(): call(first_kernel, (sums, jax.ShapeDtypeStruct((8, 128), F32)), [VMEM, SM...  1.19 us
  transfers between devices with their start and end apart: 16, of which 13 were waited for; matrix products, arithmetic and copies ran while one was open for 0% of the time, Pallas kernels for 4%

profile of v7, /device:TPU:6, one launch (start us, length us, event | category | flops | bytes accessed | tf_op | source)
XLA Modules:
  0.0 57.8 jit_solution(5309054900728880896)
XLA Ops:
  0.0 0.0 copy-start.3
  0.0 1.4 %collective-permute-start = (bf16[2,512,128]{2,1,0:T(8,128)(2,1)}, bf16[2,512,128]{2,1,0:T(8,128)(2,1)S(1)}, u32[]{:S(2)}, u32[]{:S(2)}) collective-permute-start(bf16[2,512,128]{2,1,0:T(8,128)(2,1)} %bitcast.3), channel_id=1, source_target_pairs={{0,48},{16,224},{32,80},{48,0},{64,112},{80,32},{96,144},{112,64},... | collective-permute-start | bytes 786440 | tf_op jit(solution)/shard_map/ppermute | solution.py:50
  1.4 0.0 copy-start
  1.4 1.0 %copy-done = bf16[2,1,512,128]{3,2,1,0:T(8,128)(2,1)S(1)} copy-done((bf16[2,1,512,128]{3,2,1,0:T(8,128)(2,1)S(1)}, bf16[2,1,512,128]{3,2,1,0:T(8,128)(2,1)}, u32[]{:S(2)}) %copy-start) | copy-done | bytes 262168
  2.3 0.0 copy-start.1
  2.3 0.7 %copy-done.1 = f32[128]{0:T(128)S(1)} copy-done((f32[128]{0:T(128)S(1)}, f32[128]{0:T(128)}, u32[]{:S(2)}) %copy-start.1) | copy-done | bytes 536
  3.0 0.0 copy-start.2
  3.0 0.7 %copy-done.2 = f32[128]{0:T(128)S(1)} copy-done((f32[128]{0:T(128)S(1)}, f32[128]{0:T(128)}, u32[]{:S(2)}) %copy-start.2) | copy-done | bytes 536
  3.7 0.0 copy-start.4
  3.7 5.3 %collective-permute-start.4 = (bf16[2,512,128]{2,1,0:T(8,128)(2,1)S(1)}, bf16[2,512,128]{2,1,0:T(8,128)(2,1)S(1)}, u32[]{:S(2)}, u32[]{:S(2)}) collective-permute-start(bf16[2,512,128]{2,1,0:T(8,128)(2,1)S(1)} %get-tuple-element.20.refs_0_), channel_id=1, source_target_pairs={{16,32},{0,240},{48,64},{32,16},{80,96},{64,48},{112,128},{96,80},... | collective-permute-start | bytes 786440 | tf_op jit(solution)/shard_map/ppermute | solution.py:50
  9.0 0.0 collective-permute-start.1
  9.0 1.3 %collective-permute-done.1.pair_ref = s32[1,2]{1,0:T(1,128)S(1)} collective-permute-done((s32[1,2]{1,0:T(1,128)}, s32[1,2]{1,0:T(1,128)S(1)}, u32[]{:S(2)}, u32[]{:S(2)}) %collective-permute-start.1) | collective-permute-done | bytes 40 | tf_op jit(solution)/shard_map/ppermute | solution.py:227
  10.3 0.0 collective-permute-done.refs_1_
  10.3 1.9 %collective-permute-start.2 = (bf16[2,512,128]{2,1,0:T(8,128)(2,1)S(1)}, bf16[2,512,128]{2,1,0:T(8,128)(2,1)S(1)}, u32[]{:S(2)}, u32[]{:S(2)}) collective-permute-start(bf16[2,512,128]{2,1,0:T(8,128)(2,1)S(1)} %collective-permute-done.refs_1_), channel_id=1, source_target_pairs={{16,32},{0,240},{48,64},{32,16},{80,96},{64,48},{112,128},{96,80},... | collective-permute-start | bytes 786440 | tf_op jit(solution)/shard_map/ppermute | solution.py:50
  12.1 1.1 %collective-permute-done.4.refs_4_ = bf16[2,512,128]{2,1,0:T(8,128)(2,1)S(1)} collective-permute-done((bf16[2,512,128]{2,1,0:T(8,128)(2,1)S(1)}, bf16[2,512,128]{2,1,0:T(8,128)(2,1)S(1)}, u32[]{:S(2)}, u32[]{:S(2)}) %collective-permute-start.4) | collective-permute-done | bytes 262176 | tf_op jit(solution)/shard_map/ppermute | solution.py:50
  13.2 0.9 %collective-permute-start.5 = (bf16[2,512,128]{2,1,0:T(8,128)(2,1)S(1)}, bf16[2,512,128]{2,1,0:T(8,128)(2,1)S(1)}, u32[]{:S(2)}, u32[]{:S(2)}) collective-permute-start(bf16[2,512,128]{2,1,0:T(8,128)(2,1)S(1)} %collective-permute-done.4.refs_4_), channel_id=1, source_target_pairs={{0,32},{16,240},{32,64},{48,16},{64,96},{80,48},{96,128},{112,80},... | collective-permute-start | bytes 786440 | tf_op jit(solution)/shard_map/ppermute | solution.py:50
  14.1 3.2 %collective-permute-done.2.refs_2_ = bf16[2,512,128]{2,1,0:T(8,128)(2,1)S(1)} collective-permute-done((bf16[2,512,128]{2,1,0:T(8,128)(2,1)S(1)}, bf16[2,512,128]{2,1,0:T(8,128)(2,1)S(1)}, u32[]{:S(2)}, u32[]{:S(2)}) %collective-permute-start.2) | collective-permute-done | bytes 262176 | tf_op jit(solution)/shard_map/ppermute | solution.py:50
  17.3 1.3 %collective-permute-start.3 = (bf16[2,512,128]{2,1,0:T(8,128)(2,1)S(1)}, bf16[2,512,128]{2,1,0:T(8,128)(2,1)S(1)}, u32[]{:S(2)}, u32[]{:S(2)}) collective-permute-start(bf16[2,512,128]{2,1,0:T(8,128)(2,1)S(1)} %collective-permute-done.2.refs_2_), channel_id=1, source_target_pairs={{0,48},{16,224},{32,80},{48,0},{64,112},{80,32},{96,144},{112,64},... | collective-permute-start | bytes 786440 | tf_op jit(solution)/shard_map/ppermute | solution.py:50
  18.6 2.3 %collective-permute-done.5.refs_5_ = bf16[2,512,128]{2,1,0:T(8,128)(2,1)S(1)} collective-permute-done((bf16[2,512,128]{2,1,0:T(8,128)(2,1)S(1)}, bf16[2,512,128]{2,1,0:T(8,128)(2,1)S(1)}, u32[]{:S(2)}, u32[]{:S(2)}) %collective-permute-start.5) | collective-permute-done | bytes 262176 | tf_op jit(solution)/shard_map/ppermute | solution.py:50
  20.8 0.0 collective-permute-start.6
  20.8 2.3 %collective-permute-done.3.refs_3_ = bf16[2,512,128]{2,1,0:T(8,128)(2,1)S(1)} collective-permute-done((bf16[2,512,128]{2,1,0:T(8,128)(2,1)S(1)}, bf16[2,512,128]{2,1,0:T(8,128)(2,1)S(1)}, u32[]{:S(2)}, u32[]{:S(2)}) %collective-permute-start.3) | collective-permute-done | bytes 262176 | tf_op jit(solution)/shard_map/ppermute | solution.py:50
  23.1 2.2 %collective-permute-start.7 = (bf16[2,512,128]{2,1,0:T(8,128)(2,1)S(1)}, bf16[2,512,128]{2,1,0:T(8,128)(2,1)S(1)}, u32[]{:S(2)}, u32[]{:S(2)}) collective-permute-start(bf16[2,512,128]{2,1,0:T(8,128)(2,1)S(1)} %collective-permute-done.3.refs_3_), channel_id=1, source_target_pairs={{16,32},{0,240},{48,64},{32,16},{80,96},{64,48},{112,128},{96,80},... | collective-permute-start | bytes 786440 | tf_op jit(solution)/shard_map/ppermute | solution.py:50
  25.2 1.4 %collective-permute-done.6.refs_6_ = bf16[2,512,128]{2,1,0:T(8,128)(2,1)S(1)} collective-permute-done((bf16[2,512,128]{2,1,0:T(8,128)(2,1)S(1)}, bf16[2,512,128]{2,1,0:T(8,128)(2,1)S(1)}, u32[]{:S(2)}, u32[]{:S(2)}) %collective-permute-start.6) | collective-permute-done | bytes 262176 | tf_op jit(solution)/shard_map/ppermute | solution.py:50
  26.6 0.3 pick_regions.1
  26.9 1.0 %collective-permute-start.8 = (bf16[2,2,512,128]{3,2,1,0:T(8,128)(2,1)S(1)}, bf16[2,2,512,128]{3,2,1,0:T(8,128)(2,1)S(1)}, u32[]{:S(2)}, u32[]{:S(2)}) collective-permute-start(bf16[2,2,512,128]{3,2,1,0:T(8,128)(2,1)S(1)} %pick_regions.1), channel_id=1, source_target_pairs={{0,16},{16,0},{32,48},{48,32},{64,80},{80,64},{96,112},{112,96},{1... | collective-permute-start | bytes 1572872 | tf_op jit(solution)/shard_map/ppermute | solution.py:227
  27.9 2.3 %collective-permute-done.7.refs_7_ = bf16[2,512,128]{2,1,0:T(8,128)(2,1)S(1)} collective-permute-done((bf16[2,512,128]{2,1,0:T(8,128)(2,1)S(1)}, bf16[2,512,128]{2,1,0:T(8,128)(2,1)S(1)}, u32[]{:S(2)}, u32[]{:S(2)}) %collective-permute-start.7) | collective-permute-done | bytes 262176 | tf_op jit(solution)/shard_map/ppermute | solution.py:50
  30.2 0.1 collective-permute-start.9
  30.3 1.4 %collective-permute-done.9.refs_9_ = bf16[2,512,128]{2,1,0:T(8,128)(2,1)S(1)} collective-permute-done((bf16[2,512,128]{2,1,0:T(8,128)(2,1)S(1)}, bf16[2,512,128]{2,1,0:T(8,128)(2,1)S(1)}, u32[]{:S(2)}, u32[]{:S(2)}) %collective-permute-start.9) | collective-permute-done | bytes 262176 | tf_op jit(solution)/shard_map/ppermute | solution.py:227
  31.7 0.0 collective-permute-done.8.refs_8_
  31.7 0.0 copy-done.3
  31.7 0.5 fan_out.1
  32.2 3.0 %collective-permute-start.10 = (bf16[1296,128]{1,0:T(8,128)(2,1)S(1)}, bf16[1296,128]{1,0:T(8,128)(2,1)S(1)}, u32[]{:S(2)}, u32[]{:S(2)}) collective-permute-start(bf16[1296,128]{1,0:T(8,128)(2,1)S(1)} %get-tuple-element.25), channel_id=1, source_target_pairs={{0,15},{1,14},{2,13},{3,12},{4,11},{5,10},{6,9},{7,8},{8,7},{9,6},... | collective-permute-start | bytes 995336 | tf_op jit(solution)/shard_map/ppermute | solution.py:223
  35.3 0.2 collective-permute-start.11
  35.5 2.8 %collective-permute-start.12 = (bf16[1296,128]{1,0:T(8,128)(2,1)S(1)}, bf16[1296,128]{1,0:T(8,128)(2,1)S(1)}, u32[]{:S(2)}, u32[]{:S(2)}) collective-permute-start(bf16[1296,128]{1,0:T(8,128)(2,1)S(1)} %get-tuple-element.28), channel_id=1, source_target_pairs={{0,3},{1,2},{2,1},{3,0},{4,7},{5,6},{6,5},{7,4},{8,11},{9,10},{10,... | collective-permute-start | bytes 995336 | tf_op jit(solution)/shard_map/ppermute | solution.py:223
  38.2 0.0 copy-done.4
  38.2 1.2 %product_0.1 = (f32[4,256,512]{2,1,0:T(8,128)S(1)}, f32[8,128]{1,0:T(8,128)S(1)}) custom-call(bf16[1296,128]{1,0:T(8,128)(2,1)S(1)} %get-tuple-element.23.part_ref, f32[4]{0:T(128)S(1)} %copy-done.4), custom_call_target="tpu_custom_call" | custom-call | flops 268435456 | bytes 1048576 | tf_op jit(solution)/shard_map/product_0/pallas_call | solution.py:258
  39.4 3.4 %collective-permute-done.10.part_ref = bf16[1296,128]{1,0:T(8,128)(2,1)S(1)} collective-permute-done((bf16[1296,128]{1,0:T(8,128)(2,1)S(1)}, bf16[1296,128]{1,0:T(8,128)(2,1)S(1)}, u32[]{:S(2)}, u32[]{:S(2)}) %collective-permute-start.10) | collective-permute-done | bytes 331808 | tf_op jit(solution)/shard_map/ppermute | solution.py:223
  42.9 0.8 %product_1.1.total_ref = f32[4,256,512]{2,1,0:T(8,128)S(1)} custom-call(f32[4,256,512]{2,1,0:T(8,128)S(1)} %get-tuple-element.24.total_ref, bf16[1296,128]{1,0:T(8,128)(2,1)S(1)} %collective-permute-done.10.part_ref, f32[8,128]{1,0:T(8,128)S(1)} %get-tuple-element.26.speeds_ref), custom_call_target="tpu_custom_call", output_to_operand_aliasing={{}: (0, {})} | custom-call | flops 268435456 | bytes 1048576 | tf_op jit(solution)/shard_map/product_1/pallas_call | solution.py:265
  43.7 2.7 %collective-permute-done.11.part_ref = bf16[1296,128]{1,0:T(8,128)(2,1)S(1)} collective-permute-done((bf16[1296,128]{1,0:T(8,128)(2,1)S(1)}, bf16[1296,128]{1,0:T(8,128)(2,1)S(1)}, u32[]{:S(2)}, u32[]{:S(2)}) %collective-permute-start.11) | collective-permute-done | bytes 331808 | tf_op jit(solution)/shard_map/ppermute | solution.py:223
  46.3 0.4 collective-permute-done.12.other_ref
  46.7 0.8 %product_2.1 = (f32[32,4096]{1,0:T(8,128)S(1)}, bf16[32,4096]{1,0:T(8,128)(2,1)S(1)}, bf16[32,4096]{1,0:T(8,128)(2,1)S(1)}, bf16[32,4096]{1,0:T(8,128)(2,1)S(1)}) custom-call(f32[4,256,512]{2,1,0:T(8,128)S(1)} %product_1.1.total_ref, bf16[1296,128]{1,0:T(8,128)(2,1)S(1)} %collective-permute-done.11.part_ref, ...), custom_call_target="tpu_custom_call" | custom-call | flops 536870912 | bytes 1048576 | tf_op jit(solution)/shard_map/product_2/pallas_call | solution.py:269
  47.5 0.1 collective-permute-start.13
  47.6 1.1 %collective-permute-start.14 = (bf16[32,4096]{1,0:T(8,128)(2,1)S(1)}, bf16[32,4096]{1,0:T(8,128)(2,1)S(1)}, u32[]{:S(2)}, u32[]{:S(2)}) collective-permute-start(bf16[32,4096]{1,0:T(8,128)(2,1)S(1)} %get-tuple-element.31), channel_id=1, source_target_pairs={{0,4},{1,5},{2,6},{3,7},{4,0},{5,1},{6,2},{7,3},{8,12},{9,13},{10,... | collective-permute-start | bytes 786440 | tf_op jit(solution)/shard_map/ppermute | solution.py:223
  48.6 2.4 %collective-permute-start.15 = (bf16[32,4096]{1,0:T(8,128)(2,1)S(1)}, bf16[32,4096]{1,0:T(8,128)(2,1)S(1)}, u32[]{:S(2)}, u32[]{:S(2)}) collective-permute-start(bf16[32,4096]{1,0:T(8,128)(2,1)S(1)} %get-tuple-element.32), channel_id=1, source_target_pairs={{0,1},{1,0},{2,3},{3,2},{4,5},{5,4},{6,7},{7,6},{8,9},{9,8},{10,11... | collective-permute-start | bytes 786440 | tf_op jit(solution)/shard_map/ppermute | solution.py:223
  51.1 3.9 %collective-permute-done.13.refs_1_ = bf16[32,4096]{1,0:T(8,128)(2,1)S(1)} collective-permute-done((bf16[32,4096]{1,0:T(8,128)(2,1)S(1)}, bf16[32,4096]{1,0:T(8,128)(2,1)S(1)}, u32[]{:S(2)}, u32[]{:S(2)}) %collective-permute-start.13) | collective-permute-done | bytes 262176 | tf_op jit(solution)/shard_map/ppermute | solution.py:223
  54.9 1.9 %collective-permute-done.14.refs_2_ = bf16[32,4096]{1,0:T(8,128)(2,1)S(1)} collective-permute-done((bf16[32,4096]{1,0:T(8,128)(2,1)S(1)}, bf16[32,4096]{1,0:T(8,128)(2,1)S(1)}, u32[]{:S(2)}, u32[]{:S(2)}) %collective-permute-start.14) | collective-permute-done | bytes 262176 | tf_op jit(solution)/shard_map/ppermute | solution.py:223
  56.8 0.0 collective-permute-done.15.refs_3_
  56.9 1.0 %sum_terms.1 = f32[32,1,4,2,512]{4,3,2,1,0:T(2,128)} custom-call(f32[32,4096]{1,0:T(8,128)S(1)} %get-tuple-element.29.refs_0_, bf16[32,4096]{1,0:T(8,128)(2,1)S(1)} %collective-permute-done.13.refs_1_, bf16[32,4096]{1,0:T(8,128)(2,1)S(1)} %collective-permute-done.14.refs_2_, bf16[32,4096]{1,0:T(8,128)(2,1)S(1)} %collective-permute-done.15.refs_3_), custom_call_target="tpu_custom_call" | custom-call | bytes 1048576 | tf_op jit(solution)/shard_map/sum_terms/pallas_call | solution.py:277
  (1 shorter events, 0.0 us)
Async XLA Ops:
  0.0 31.7 %copy-start.3 = (s32[1,2]{1,0:T(1,128)S(1)}, s32[1,2]{1,0:T(1,128)}, u32[]{:S(2)}) copy-start(s32[1,2]{1,0:T(1,128)} %pair_ref.1) | copy-start | bytes 28
  0.0 10.3 %collective-permute-start = (bf16[2,512,128]{2,1,0:T(8,128)(2,1)}, bf16[2,512,128]{2,1,0:T(8,128)(2,1)S(1)}, u32[]{:S(2)}, u32[]{:S(2)}) collective-permute-start(bf16[2,512,128]{2,1,0:T(8,128)(2,1)} %bitcast.3), channel_id=1, source_target_pairs={{0,48},{16,224},{32,80},{48,0},{64,112},{80,32},{96,144},{112,64},... | collective-permute-start | bytes 786440 | tf_op jit(solution)/shard_map/ppermute | solution.py:50
  1.4 1.0 %copy-start = (bf16[2,1,512,128]{3,2,1,0:T(8,128)(2,1)S(1)}, bf16[2,1,512,128]{3,2,1,0:T(8,128)(2,1)}, u32[]{:S(2)}) copy-start(bf16[2,1,512,128]{3,2,1,0:T(8,128)(2,1)} %shapes_ref.1) | copy-start | bytes 786436
  2.3 0.7 %copy-start.1 = (f32[128]{0:T(128)S(1)}, f32[128]{0:T(128)}, u32[]{:S(2)}) copy-start(f32[128]{0:T(128)} %param.7) | copy-start | bytes 1540
  3.0 0.7 %copy-start.2 = (f32[128]{0:T(128)S(1)}, f32[128]{0:T(128)}, u32[]{:S(2)}) copy-start(f32[128]{0:T(128)} %param.8) | copy-start | bytes 1540
  3.7 34.6 %copy-start.4 = (f32[4]{0:T(128)S(1)}, f32[4]{0:T(128)}, u32[]{:S(2)}) copy-start(f32[4]{0:T(128)} %speeds_ref.1) | copy-start | bytes 52
  3.7 9.5 %collective-permute-start.4 = (bf16[2,512,128]{2,1,0:T(8,128)(2,1)S(1)}, bf16[2,512,128]{2,1,0:T(8,128)(2,1)S(1)}, u32[]{:S(2)}, u32[]{:S(2)}) collective-permute-start(bf16[2,512,128]{2,1,0:T(8,128)(2,1)S(1)} %get-tuple-element.20.refs_0_), channel_id=1, source_target_pairs={{16,32},{0,240},{48,64},{32,16},{80,96},{64,48},{112,128},{96,80},... | collective-permute-start | bytes 786440 | tf_op jit(solution)/shard_map/ppermute | solution.py:50
  9.0 1.3 %collective-permute-start.1 = (s32[1,2]{1,0:T(1,128)}, s32[1,2]{1,0:T(1,128)S(1)}, u32[]{:S(2)}, u32[]{:S(2)}) collective-permute-start(s32[1,2]{1,0:T(1,128)} %pair_ref.1), channel_id=1, source_target_pairs={{0,16},{16,0},{32,48},{48,32},{64,80},{80,64},{96,112},{112,96},{1... | collective-permute-start | bytes 32 | tf_op jit(solution)/shard_map/ppermute | solution.py:227
  10.3 7.0 %collective-permute-start.2 = (bf16[2,512,128]{2,1,0:T(8,128)(2,1)S(1)}, bf16[2,512,128]{2,1,0:T(8,128)(2,1)S(1)}, u32[]{:S(2)}, u32[]{:S(2)}) collective-permute-start(bf16[2,512,128]{2,1,0:T(8,128)(2,1)S(1)} %collective-permute-done.refs_1_), channel_id=1, source_target_pairs={{16,32},{0,240},{48,64},{32,16},{80,96},{64,48},{112,128},{96,80},... | collective-permute-start | bytes 786440 | tf_op jit(solution)/shard_map/ppermute | solution.py:50
  13.2 7.6 %collective-permute-start.5 = (bf16[2,512,128]{2,1,0:T(8,128)(2,1)S(1)}, bf16[2,512,128]{2,1,0:T(8,128)(2,1)S(1)}, u32[]{:S(2)}, u32[]{:S(2)}) collective-permute-start(bf16[2,512,128]{2,1,0:T(8,128)(2,1)S(1)} %collective-permute-done.4.refs_4_), channel_id=1, source_target_pairs={{0,32},{16,240},{32,64},{48,16},{64,96},{80,48},{96,128},{112,80},... | collective-permute-start | bytes 786440 | tf_op jit(solution)/shard_map/ppermute | solution.py:50
  17.3 5.8 %collective-permute-start.3 = (bf16[2,512,128]{2,1,0:T(8,128)(2,1)S(1)}, bf16[2,512,128]{2,1,0:T(8,128)(2,1)S(1)}, u32[]{:S(2)}, u32[]{:S(2)}) collective-permute-start(bf16[2,512,128]{2,1,0:T(8,128)(2,1)S(1)} %collective-permute-done.2.refs_2_), channel_id=1, source_target_pairs={{0,48},{16,224},{32,80},{48,0},{64,112},{80,32},{96,144},{112,64},... | collective-permute-start | bytes 786440 | tf_op jit(solution)/shard_map/ppermute | solution.py:50
  20.8 5.8 %collective-permute-start.6 = (bf16[2,512,128]{2,1,0:T(8,128)(2,1)S(1)}, bf16[2,512,128]{2,1,0:T(8,128)(2,1)S(1)}, u32[]{:S(2)}, u32[]{:S(2)}) collective-permute-start(bf16[2,512,128]{2,1,0:T(8,128)(2,1)S(1)} %collective-permute-done.5.refs_5_), channel_id=1, source_target_pairs={{0,48},{16,224},{32,80},{48,0},{64,112},{80,32},{96,144},{112,64},... | collective-permute-start | bytes 786440 | tf_op jit(solution)/shard_map/ppermute | solution.py:50
  23.1 7.1 %collective-permute-start.7 = (bf16[2,512,128]{2,1,0:T(8,128)(2,1)S(1)}, bf16[2,512,128]{2,1,0:T(8,128)(2,1)S(1)}, u32[]{:S(2)}, u32[]{:S(2)}) collective-permute-start(bf16[2,512,128]{2,1,0:T(8,128)(2,1)S(1)} %collective-permute-done.3.refs_3_), channel_id=1, source_target_pairs={{16,32},{0,240},{48,64},{32,16},{80,96},{64,48},{112,128},{96,80},... | collective-permute-start | bytes 786440 | tf_op jit(solution)/shard_map/ppermute | solution.py:50
  26.9 4.8 %collective-permute-start.8 = (bf16[2,2,512,128]{3,2,1,0:T(8,128)(2,1)S(1)}, bf16[2,2,512,128]{3,2,1,0:T(8,128)(2,1)S(1)}, u32[]{:S(2)}, u32[]{:S(2)}) collective-permute-start(bf16[2,2,512,128]{3,2,1,0:T(8,128)(2,1)S(1)} %pick_regions.1), channel_id=1, source_target_pairs={{0,16},{16,0},{32,48},{48,32},{64,80},{80,64},{96,112},{112,96},{1... | collective-permute-start | bytes 1572872 | tf_op jit(solution)/shard_map/ppermute | solution.py:227
  30.2 1.5 %collective-permute-start.9 = (bf16[2,512,128]{2,1,0:T(8,128)(2,1)S(1)}, bf16[2,512,128]{2,1,0:T(8,128)(2,1)S(1)}, u32[]{:S(2)}, u32[]{:S(2)}) collective-permute-start(bf16[2,512,128]{2,1,0:T(8,128)(2,1)S(1)} %collective-permute-done.7.refs_7_), channel_id=1, source_target_pairs={{0,16},{16,0},{32,48},{48,32},{64,80},{80,64},{96,112},{112,96},{1... | collective-permute-start | bytes 786440 | tf_op jit(solution)/shard_map/ppermute | solution.py:227
  32.2 10.6 %collective-permute-start.10 = (bf16[1296,128]{1,0:T(8,128)(2,1)S(1)}, bf16[1296,128]{1,0:T(8,128)(2,1)S(1)}, u32[]{:S(2)}, u32[]{:S(2)}) collective-permute-start(bf16[1296,128]{1,0:T(8,128)(2,1)S(1)} %get-tuple-element.25), channel_id=1, source_target_pairs={{0,15},{1,14},{2,13},{3,12},{4,11},{5,10},{6,9},{7,8},{8,7},{9,6},... | collective-permute-start | bytes 995336 | tf_op jit(solution)/shard_map/ppermute | solution.py:223
  35.3 11.1 %collective-permute-start.11 = (bf16[1296,128]{1,0:T(8,128)(2,1)S(1)}, bf16[1296,128]{1,0:T(8,128)(2,1)S(1)}, u32[]{:S(2)}, u32[]{:S(2)}) collective-permute-start(bf16[1296,128]{1,0:T(8,128)(2,1)S(1)} %get-tuple-element.27), channel_id=1, source_target_pairs={{0,12},{1,13},{2,14},{3,15},{4,8},{5,9},{6,10},{7,11},{8,4},{9,5},... | collective-permute-start | bytes 995336 | tf_op jit(solution)/shard_map/ppermute | solution.py:223
  35.5 11.2 %collective-permute-start.12 = (bf16[1296,128]{1,0:T(8,128)(2,1)S(1)}, bf16[1296,128]{1,0:T(8,128)(2,1)S(1)}, u32[]{:S(2)}, u32[]{:S(2)}) collective-permute-start(bf16[1296,128]{1,0:T(8,128)(2,1)S(1)} %get-tuple-element.28), channel_id=1, source_target_pairs={{0,3},{1,2},{2,1},{3,0},{4,7},{5,6},{6,5},{7,4},{8,11},{9,10},{10,... | collective-permute-start | bytes 995336 | tf_op jit(solution)/shard_map/ppermute | solution.py:223
  47.5 7.5 %collective-permute-start.13 = (bf16[32,4096]{1,0:T(8,128)(2,1)S(1)}, bf16[32,4096]{1,0:T(8,128)(2,1)S(1)}, u32[]{:S(2)}, u32[]{:S(2)}) collective-permute-start(bf16[32,4096]{1,0:T(8,128)(2,1)S(1)} %get-tuple-element.30), channel_id=1, source_target_pairs={{0,5},{1,4},{2,7},{3,6},{4,1},{5,0},{6,3},{7,2},{8,13},{9,12},{10,... | collective-permute-start | bytes 786440 | tf_op jit(solution)/shard_map/ppermute | solution.py:223
  47.6 9.3 %collective-permute-start.14 = (bf16[32,4096]{1,0:T(8,128)(2,1)S(1)}, bf16[32,4096]{1,0:T(8,128)(2,1)S(1)}, u32[]{:S(2)}, u32[]{:S(2)}) collective-permute-start(bf16[32,4096]{1,0:T(8,128)(2,1)S(1)} %get-tuple-element.31), channel_id=1, source_target_pairs={{0,4},{1,5},{2,6},{3,7},{4,0},{5,1},{6,2},{7,3},{8,12},{9,13},{10,... | collective-permute-start | bytes 786440 | tf_op jit(solution)/shard_map/ppermute | solution.py:223
  48.6 8.2 %collective-permute-start.15 = (bf16[32,4096]{1,0:T(8,128)(2,1)S(1)}, bf16[32,4096]{1,0:T(8,128)(2,1)S(1)}, u32[]{:S(2)}, u32[]{:S(2)}) collective-permute-start(bf16[32,4096]{1,0:T(8,128)(2,1)S(1)} %get-tuple-element.32), channel_id=1, source_target_pairs={{0,1},{1,0},{2,3},{3,2},{4,5},{5,4},{6,7},{7,6},{8,9},{9,8},{10,11... | collective-permute-start | bytes 786440 | tf_op jit(solution)/shard_map/ppermute | solution.py:223

commit v8 on v7

--- a/solution.py
+++ b/solution.py
@@ -204,14 +204,22 @@
 
 
 def sum_kernel(*refs):
-    terms, out_ref = refs[:4], refs[4]
-    for s in range(4):
-        for c in range(2):
-            at = (2 * s + c) * 512
-            total = terms[0][:, at : at + 512]
-            for ref in terms[1:]:
-                total = total + ref[:, at : at + 512].astype(F32)
-            out_ref[:, 0, s, c, :] = total
+    terms, out_ref, total_ref, sems = refs[:4], refs[4], refs[5], refs[6]
+    copies = []
+    for q in range(4):
+        rows = slice(8 * q, 8 * q + 8)
+        for s in range(4):
+            for c in range(2):
+                at = (2 * s + c) * 512
+                total = terms[0][rows, at : at + 512]
+                for ref in terms[1:]:
+                    total = total + ref[rows, at : at + 512].astype(F32)
+                total_ref[rows, s, c, :] = total
+        copy = pltpu.make_async_copy(total_ref.at[rows], out_ref.at[rows, 0], sems.at[q])
+        copy.start()
+        copies.append(copy)
+    for copy in copies:
+        copy.wait()
 
 
 def exchange(value, d, flip):
@@ -236,7 +244,6 @@
         "prepare",
     )(shapes, omega.reshape(1, 128), damping.reshape(1, 128))
     b1 = step(own, 1, B_UP)
-    a1, other_pair = lax.optimization_barrier((a1, swap_cores(pairs)))
     a2 = step(a1, 2, A_UP)
     b2 = step(b1, 2, B_UP)
     a3 = step(a2, 3, A_UP)
@@ -244,7 +251,7 @@
     a4 = step(a3, 4, A_UP)
     regions = (own, a1, a2, a3, b1, b2, b3)
     other = jax.ShapeDtypeStruct((2, 2, 512, 128), BF)
-    wanted = call(pick_kernel, other, [VMEM] * 8, "pick_regions")(other_pair, *regions)
+    wanted = call(pick_kernel, other, [VMEM] * 8, "pick_regions")(swap_cores(pairs), *regions)
     message = jax.ShapeDtypeStruct((ROWS, 128), BF)
     fanned = call(
         fan_kernel,
@@ -275,7 +282,12 @@
     )(total, parts[2], parts[3], speed_rows)
     terms = [made[0]] + [exchange(made[e], e, 1) for e in (3, 2, 1)]
     return call(
-        sum_kernel, jax.ShapeDtypeStruct((32, 1, 4, 2, 512), F32), [VMEM] * 4, "sum_terms"
+        sum_kernel,
+        jax.ShapeDtypeStruct((32, 1, 4, 2, 512), F32),
+        [VMEM] * 4,
+        "sum_terms",
+        scratch=[pltpu.VMEM((32, 4, 2, 512), F32), pltpu.SemaphoreType.DMA((4,))],
+        out_spec=HBM,
     )(*terms)
 
 

time: 58.2 us -> 58 us (level)
  starting transfers between devices: 23.5 us -> 24.8 us
  waiting for transfers between devices: 27.4 us -> 26.1 us
    ppermute x3, waiting for transfers between devices: 2.68 us -> 1.51 us  [swap_cores(): return lax.ppermute(value, 'group', [(g, g ^ 1) for g in range(16)])]
    ppermute x3, starting transfers between devices: 1.15 us -> 2.14 us  [swap_cores(): return lax.ppermute(value, 'group', [(g, g ^ 1) for g in range(16)])]
  transfers between devices with their start and end apart: 16 -> 16, of which waited for: 13 -> 12; matrix products, arithmetic and copies ran while one was open for 0% -> 0% of each run, Pallas kernels for 4% -> 4%
where the time goes in v8:
time: 58 us; the launch traced here: 57.6 us
  waiting for transfers between devices  26.1 us (45%)
  starting transfers between devices  24.8 us (43%)
  Pallas kernels  4.4 us (8%)
  local copies, waits for them, and re-layouts  2.3 us (4%)
    ppermute x7, starting transfers between devices, step(): return lax.ppermute(value, 'group', perm)  13.1 us
    ppermute x7, waiting for transfers between devices, step(): return lax.ppermute(value, 'group', perm)  12.3 us
    ppermute x6, waiting for transfers between devices, exchange(): return lax.ppermute(value, ('group', 'mode'), perm)  12.3 us
    ppermute x6, starting transfers between devices, exchange(): return lax.ppermute(value, ('group', 'mode'), perm)  9.56 us
    unnamed x10, local copies, waits for them, and re-layouts  2.3 us
    ppermute x3, starting transfers between devices, swap_cores(): return lax.ppermute(value, 'group', [(g, g ^ 1) for g in range(16)])  2.14 us
    ppermute x3, waiting for transfers between devices, swap_cores(): return lax.ppermute(value, 'group', [(g, g ^ 1) for g in range(16)])  1.51 us
    pallas_call x1, Pallas kernels, shards(): call(first_kernel, (sums, jax.ShapeDtypeStruct((8, 128), F32)), [VMEM, SM...  1.2 us
  transfers between devices with their start and end apart: 16, of which 12 were waited for; matrix products, arithmetic and copies ran while one was open for 0% of the time, Pallas kernels for 4%

profile of v8, /device:TPU:6, one launch (start us, length us, event | category | flops | bytes accessed | tf_op | source)
XLA Modules:
  0.0 57.6 jit_solution(6280953017859105484)
XLA Ops:
  0.0 0.0 copy-start.3
  0.0 1.4 %collective-permute-start = (bf16[2,512,128]{2,1,0:T(8,128)(2,1)}, bf16[2,512,128]{2,1,0:T(8,128)(2,1)S(1)}, u32[]{:S(2)}, u32[]{:S(2)}) collective-permute-start(bf16[2,512,128]{2,1,0:T(8,128)(2,1)} %bitcast.3), channel_id=1, source_target_pairs={{0,48},{16,224},{32,80},{48,0},{64,112},{80,32},{96,144},{112,64},... | collective-permute-start | bytes 786440 | tf_op jit(solution)/shard_map/ppermute | solution.py:50
  1.4 0.0 copy-start
  1.4 1.0 %copy-done = bf16[2,1,512,128]{3,2,1,0:T(8,128)(2,1)S(1)} copy-done((bf16[2,1,512,128]{3,2,1,0:T(8,128)(2,1)S(1)}, bf16[2,1,512,128]{3,2,1,0:T(8,128)(2,1)}, u32[]{:S(2)}) %copy-start) | copy-done | bytes 262168
  2.3 0.0 copy-start.1
  2.3 0.7 %copy-done.1 = f32[128]{0:T(128)S(1)} copy-done((f32[128]{0:T(128)S(1)}, f32[128]{0:T(128)}, u32[]{:S(2)}) %copy-start.1) | copy-done | bytes 536
  3.0 0.0 copy-start.2
  3.0 0.7 %copy-done.2 = f32[128]{0:T(128)S(1)} copy-done((f32[128]{0:T(128)S(1)}, f32[128]{0:T(128)}, u32[]{:S(2)}) %copy-start.2) | copy-done | bytes 536
  3.7 0.0 copy-start.4
  3.7 5.3 %collective-permute-start.3 = (bf16[2,512,128]{2,1,0:T(8,128)(2,1)S(1)}, bf16[2,512,128]{2,1,0:T(8,128)(2,1)S(1)}, u32[]{:S(2)}, u32[]{:S(2)}) collective-permute-start(bf16[2,512,128]{2,1,0:T(8,128)(2,1)S(1)} %get-tuple-element.18.refs_0_), channel_id=1, source_target_pairs={{16,32},{0,240},{48,64},{32,16},{80,96},{64,48},{112,128},{96,80},... | collective-permute-start | bytes 786440 | tf_op jit(solution)/shard_map/ppermute | solution.py:50
  9.0 0.0 collective-permute-done.refs_1_
  9.0 3.1 %collective-permute-start.1 = (bf16[2,512,128]{2,1,0:T(8,128)(2,1)S(1)}, bf16[2,512,128]{2,1,0:T(8,128)(2,1)S(1)}, u32[]{:S(2)}, u32[]{:S(2)}) collective-permute-start(bf16[2,512,128]{2,1,0:T(8,128)(2,1)S(1)} %collective-permute-done.refs_1_), channel_id=1, source_target_pairs={{16,32},{0,240},{48,64},{32,16},{80,96},{64,48},{112,128},{96,80},... | collective-permute-start | bytes 786440 | tf_op jit(solution)/shard_map/ppermute | solution.py:50
  12.1 1.1 %collective-permute-done.3.refs_4_ = bf16[2,512,128]{2,1,0:T(8,128)(2,1)S(1)} collective-permute-done((bf16[2,512,128]{2,1,0:T(8,128)(2,1)S(1)}, bf16[2,512,128]{2,1,0:T(8,128)(2,1)S(1)}, u32[]{:S(2)}, u32[]{:S(2)}) %collective-permute-start.3) | collective-permute-done | bytes 262176 | tf_op jit(solution)/shard_map/ppermute | solution.py:50
  13.2 0.9 %collective-permute-start.4 = (bf16[2,512,128]{2,1,0:T(8,128)(2,1)S(1)}, bf16[2,512,128]{2,1,0:T(8,128)(2,1)S(1)}, u32[]{:S(2)}, u32[]{:S(2)}) collective-permute-start(bf16[2,512,128]{2,1,0:T(8,128)(2,1)S(1)} %collective-permute-done.3.refs_4_), channel_id=1, source_target_pairs={{0,32},{16,240},{32,64},{48,16},{64,96},{80,48},{96,128},{112,80},... | collective-permute-start | bytes 786440 | tf_op jit(solution)/shard_map/ppermute | solution.py:50
  14.1 2.1 %collective-permute-done.1.refs_2_ = bf16[2,512,128]{2,1,0:T(8,128)(2,1)S(1)} collective-permute-done((bf16[2,512,128]{2,1,0:T(8,128)(2,1)S(1)}, bf16[2,512,128]{2,1,0:T(8,128)(2,1)S(1)}, u32[]{:S(2)}, u32[]{:S(2)}) %collective-permute-start.1) | collective-permute-done | bytes 262176 | tf_op jit(solution)/shard_map/ppermute | solution.py:50
  16.2 0.0 collective-permute-start.2
  16.2 4.6 %collective-permute-done.4.refs_5_ = bf16[2,512,128]{2,1,0:T(8,128)(2,1)S(1)} collective-permute-done((bf16[2,512,128]{2,1,0:T(8,128)(2,1)S(1)}, bf16[2,512,128]{2,1,0:T(8,128)(2,1)S(1)}, u32[]{:S(2)}, u32[]{:S(2)}) %collective-permute-start.4) | collective-permute-done | bytes 262176 | tf_op jit(solution)/shard_map/ppermute | solution.py:50
  20.8 0.0 collective-permute-start.5
  20.8 1.0 %collective-permute-start.7 = (s32[1,2]{1,0:T(1,128)}, s32[1,2]{1,0:T(1,128)S(1)}, u32[]{:S(2)}, u32[]{:S(2)}) collective-permute-start(s32[1,2]{1,0:T(1,128)} %pair_ref.1), channel_id=1, source_target_pairs={{0,16},{16,0},{32,48},{48,32},{64,80},{80,64},{96,112},{112,96},{1... | collective-permute-start | bytes 32 | tf_op jit(solution)/shard_map/ppermute | solution.py:235
  21.8 1.0 %collective-permute-done.2.refs_3_ = bf16[2,512,128]{2,1,0:T(8,128)(2,1)S(1)} collective-permute-done((bf16[2,512,128]{2,1,0:T(8,128)(2,1)S(1)}, bf16[2,512,128]{2,1,0:T(8,128)(2,1)S(1)}, u32[]{:S(2)}, u32[]{:S(2)}) %collective-permute-start.2) | collective-permute-done | bytes 262176 | tf_op jit(solution)/shard_map/ppermute | solution.py:50
  22.8 2.4 %collective-permute-start.6 = (bf16[2,512,128]{2,1,0:T(8,128)(2,1)S(1)}, bf16[2,512,128]{2,1,0:T(8,128)(2,1)S(1)}, u32[]{:S(2)}, u32[]{:S(2)}) collective-permute-start(bf16[2,512,128]{2,1,0:T(8,128)(2,1)S(1)} %collective-permute-done.2.refs_3_), channel_id=1, source_target_pairs={{16,32},{0,240},{48,64},{32,16},{80,96},{64,48},{112,128},{96,80},... | collective-permute-start | bytes 786440 | tf_op jit(solution)/shard_map/ppermute | solution.py:50
  25.2 0.0 collective-permute-done.7.pair_ref
  25.2 1.4 %collective-permute-done.5.refs_6_ = bf16[2,512,128]{2,1,0:T(8,128)(2,1)S(1)} collective-permute-done((bf16[2,512,128]{2,1,0:T(8,128)(2,1)S(1)}, bf16[2,512,128]{2,1,0:T(8,128)(2,1)S(1)}, u32[]{:S(2)}, u32[]{:S(2)}) %collective-permute-start.5) | collective-permute-done | bytes 262176 | tf_op jit(solution)/shard_map/ppermute | solution.py:50
  26.6 0.3 pick_regions.1
  26.9 1.1 %collective-permute-start.8 = (bf16[2,2,512,128]{3,2,1,0:T(8,128)(2,1)S(1)}, bf16[2,2,512,128]{3,2,1,0:T(8,128)(2,1)S(1)}, u32[]{:S(2)}, u32[]{:S(2)}) collective-permute-start(bf16[2,2,512,128]{3,2,1,0:T(8,128)(2,1)S(1)} %pick_regions.1), channel_id=1, source_target_pairs={{0,16},{16,0},{32,48},{48,32},{64,80},{80,64},{96,112},{112,96},{1... | collective-permute-start | bytes 1572872 | tf_op jit(solution)/shard_map/ppermute | solution.py:235
  28.0 2.1 %collective-permute-done.6.refs_7_ = bf16[2,512,128]{2,1,0:T(8,128)(2,1)S(1)} collective-permute-done((bf16[2,512,128]{2,1,0:T(8,128)(2,1)S(1)}, bf16[2,512,128]{2,1,0:T(8,128)(2,1)S(1)}, u32[]{:S(2)}, u32[]{:S(2)}) %collective-permute-start.6) | collective-permute-done | bytes 262176 | tf_op jit(solution)/shard_map/ppermute | solution.py:50
  30.1 0.0 collective-permute-start.9
  30.1 1.5 %collective-permute-done.9.refs_9_ = bf16[2,512,128]{2,1,0:T(8,128)(2,1)S(1)} collective-permute-done((bf16[2,512,128]{2,1,0:T(8,128)(2,1)S(1)}, bf16[2,512,128]{2,1,0:T(8,128)(2,1)S(1)}, u32[]{:S(2)}, u32[]{:S(2)}) %collective-permute-start.9) | collective-permute-done | bytes 262176 | tf_op jit(solution)/shard_map/ppermute | solution.py:235
  31.6 0.0 collective-permute-done.8.refs_8_
  31.6 0.0 copy-done.3
  31.7 0.5 fan_out.1
  32.2 3.0 %collective-permute-start.10 = (bf16[1296,128]{1,0:T(8,128)(2,1)S(1)}, bf16[1296,128]{1,0:T(8,128)(2,1)S(1)}, u32[]{:S(2)}, u32[]{:S(2)}) collective-permute-start(bf16[1296,128]{1,0:T(8,128)(2,1)S(1)} %get-tuple-element.21), channel_id=1, source_target_pairs={{0,15},{1,14},{2,13},{3,12},{4,11},{5,10},{6,9},{7,8},{8,7},{9,6},... | collective-permute-start | bytes 995336 | tf_op jit(solution)/shard_map/ppermute | solution.py:231
  35.2 0.2 collective-permute-start.11
  35.4 2.8 %collective-permute-start.12 = (bf16[1296,128]{1,0:T(8,128)(2,1)S(1)}, bf16[1296,128]{1,0:T(8,128)(2,1)S(1)}, u32[]{:S(2)}, u32[]{:S(2)}) collective-permute-start(bf16[1296,128]{1,0:T(8,128)(2,1)S(1)} %get-tuple-element.24), channel_id=1, source_target_pairs={{0,3},{1,2},{2,1},{3,0},{4,7},{5,6},{6,5},{7,4},{8,11},{9,10},{10,... | collective-permute-start | bytes 995336 | tf_op jit(solution)/shard_map/ppermute | solution.py:231
  38.1 0.0 copy-done.4
  38.2 1.2 %product_0.1 = (f32[4,256,512]{2,1,0:T(8,128)S(1)}, f32[8,128]{1,0:T(8,128)S(1)}) custom-call(bf16[1296,128]{1,0:T(8,128)(2,1)S(1)} %get-tuple-element.19.part_ref, f32[4]{0:T(128)S(1)} %copy-done.4), custom_call_target="tpu_custom_call" | custom-call | flops 268435456 | bytes 1048576 | tf_op jit(solution)/shard_map/product_0/pallas_call | solution.py:265
  39.4 3.4 %collective-permute-done.10.part_ref = bf16[1296,128]{1,0:T(8,128)(2,1)S(1)} collective-permute-done((bf16[1296,128]{1,0:T(8,128)(2,1)S(1)}, bf16[1296,128]{1,0:T(8,128)(2,1)S(1)}, u32[]{:S(2)}, u32[]{:S(2)}) %collective-permute-start.10) | collective-permute-done | bytes 331808 | tf_op jit(solution)/shard_map/ppermute | solution.py:231
  42.8 0.8 %product_1.1.total_ref = f32[4,256,512]{2,1,0:T(8,128)S(1)} custom-call(f32[4,256,512]{2,1,0:T(8,128)S(1)} %get-tuple-element.20.total_ref, bf16[1296,128]{1,0:T(8,128)(2,1)S(1)} %collective-permute-done.10.part_ref, f32[8,128]{1,0:T(8,128)S(1)} %get-tuple-element.22.speeds_ref), custom_call_target="tpu_custom_call", output_to_operand_aliasing={{}: (0, {})} | custom-call | flops 268435456 | bytes 1048576 | tf_op jit(solution)/shard_map/product_1/pallas_call | solution.py:272
  43.6 2.7 %collective-permute-done.11.part_ref = bf16[1296,128]{1,0:T(8,128)(2,1)S(1)} collective-permute-done((bf16[1296,128]{1,0:T(8,128)(2,1)S(1)}, bf16[1296,128]{1,0:T(8,128)(2,1)S(1)}, u32[]{:S(2)}, u32[]{:S(2)}) %collective-permute-start.11) | collective-permute-done | bytes 331808 | tf_op jit(solution)/shard_map/ppermute | solution.py:231
  46.2 0.4 collective-permute-done.12.other_ref
  46.6 0.8 %product_2.1 = (f32[32,4096]{1,0:T(8,128)S(1)}, bf16[32,4096]{1,0:T(8,128)(2,1)S(1)}, bf16[32,4096]{1,0:T(8,128)(2,1)S(1)}, bf16[32,4096]{1,0:T(8,128)(2,1)S(1)}) custom-call(f32[4,256,512]{2,1,0:T(8,128)S(1)} %product_1.1.total_ref, bf16[1296,128]{1,0:T(8,128)(2,1)S(1)} %collective-permute-done.11.part_ref, ...), custom_call_target="tpu_custom_call" | custom-call | flops 536870912 | bytes 1048576 | tf_op jit(solution)/shard_map/product_2/pallas_call | solution.py:276
  47.4 0.1 collective-permute-start.13
  47.5 1.1 %collective-permute-start.14 = (bf16[32,4096]{1,0:T(8,128)(2,1)S(1)}, bf16[32,4096]{1,0:T(8,128)(2,1)S(1)}, u32[]{:S(2)}, u32[]{:S(2)}) collective-permute-start(bf16[32,4096]{1,0:T(8,128)(2,1)S(1)} %get-tuple-element.27), channel_id=1, source_target_pairs={{0,4},{1,5},{2,6},{3,7},{4,0},{5,1},{6,2},{7,3},{8,12},{9,13},{10,... | collective-permute-start | bytes 786440 | tf_op jit(solution)/shard_map/ppermute | solution.py:231
  48.6 2.4 %collective-permute-start.15 = (bf16[32,4096]{1,0:T(8,128)(2,1)S(1)}, bf16[32,4096]{1,0:T(8,128)(2,1)S(1)}, u32[]{:S(2)}, u32[]{:S(2)}) collective-permute-start(bf16[32,4096]{1,0:T(8,128)(2,1)S(1)} %get-tuple-element.28), channel_id=1, source_target_pairs={{0,1},{1,0},{2,3},{3,2},{4,5},{5,4},{6,7},{7,6},{8,9},{9,8},{10,11... | collective-permute-start | bytes 786440 | tf_op jit(solution)/shard_map/ppermute | solution.py:231
  51.0 3.9 %collective-permute-done.13.refs_1_ = bf16[32,4096]{1,0:T(8,128)(2,1)S(1)} collective-permute-done((bf16[32,4096]{1,0:T(8,128)(2,1)S(1)}, bf16[32,4096]{1,0:T(8,128)(2,1)S(1)}, u32[]{:S(2)}, u32[]{:S(2)}) %collective-permute-start.13) | collective-permute-done | bytes 262176 | tf_op jit(solution)/shard_map/ppermute | solution.py:231
  54.8 1.9 %collective-permute-done.14.refs_2_ = bf16[32,4096]{1,0:T(8,128)(2,1)S(1)} collective-permute-done((bf16[32,4096]{1,0:T(8,128)(2,1)S(1)}, bf16[32,4096]{1,0:T(8,128)(2,1)S(1)}, u32[]{:S(2)}, u32[]{:S(2)}) %collective-permute-start.14) | collective-permute-done | bytes 262176 | tf_op jit(solution)/shard_map/ppermute | solution.py:231
  56.8 0.0 collective-permute-done.15.refs_3_
  56.8 0.9 %sum_terms.1 = f32[32,1,4,2,512]{4,3,2,1,0:T(2,128)} custom-call(f32[32,4096]{1,0:T(8,128)S(1)} %get-tuple-element.25.refs_0_, bf16[32,4096]{1,0:T(8,128)(2,1)S(1)} %collective-permute-done.13.refs_1_, bf16[32,4096]{1,0:T(8,128)(2,1)S(1)} %collective-permute-done.14.refs_2_, bf16[32,4096]{1,0:T(8,128)(2,1)S(1)} %collective-permute-done.15.refs_3_), custom_call_target="tpu_custom_call" | custom-call | bytes 1048576 | tf_op jit(solution)/shard_map/sum_terms/pallas_call | solution.py:284
  (1 shorter events, 0.0 us)
Async XLA Ops:
  0.0 31.7 %copy-start.3 = (s32[1,2]{1,0:T(1,128)S(1)}, s32[1,2]{1,0:T(1,128)}, u32[]{:S(2)}) copy-start(s32[1,2]{1,0:T(1,128)} %pair_ref.1) | copy-start | bytes 28
  0.0 9.0 %collective-permute-start = (bf16[2,512,128]{2,1,0:T(8,128)(2,1)}, bf16[2,512,128]{2,1,0:T(8,128)(2,1)S(1)}, u32[]{:S(2)}, u32[]{:S(2)}) collective-permute-start(bf16[2,512,128]{2,1,0:T(8,128)(2,1)} %bitcast.3), channel_id=1, source_target_pairs={{0,48},{16,224},{32,80},{48,0},{64,112},{80,32},{96,144},{112,64},... | collective-permute-start | bytes 786440 | tf_op jit(solution)/shard_map/ppermute | solution.py:50
  1.4 1.0 %copy-start = (bf16[2,1,512,128]{3,2,1,0:T(8,128)(2,1)S(1)}, bf16[2,1,512,128]{3,2,1,0:T(8,128)(2,1)}, u32[]{:S(2)}) copy-start(bf16[2,1,512,128]{3,2,1,0:T(8,128)(2,1)} %shapes_ref.1) | copy-start | bytes 786436
  2.3 0.7 %copy-start.1 = (f32[128]{0:T(128)S(1)}, f32[128]{0:T(128)}, u32[]{:S(2)}) copy-start(f32[128]{0:T(128)} %param.7) | copy-start | bytes 1540
  3.0 0.7 %copy-start.2 = (f32[128]{0:T(128)S(1)}, f32[128]{0:T(128)}, u32[]{:S(2)}) copy-start(f32[128]{0:T(128)} %param.8) | copy-start | bytes 1540
  3.7 34.5 %copy-start.4 = (f32[4]{0:T(128)S(1)}, f32[4]{0:T(128)}, u32[]{:S(2)}) copy-start(f32[4]{0:T(128)} %speeds_ref.1) | copy-start | bytes 52
  3.7 9.5 %collective-permute-start.3 = (bf16[2,512,128]{2,1,0:T(8,128)(2,1)S(1)}, bf16[2,512,128]{2,1,0:T(8,128)(2,1)S(1)}, u32[]{:S(2)}, u32[]{:S(2)}) collective-permute-start(bf16[2,512,128]{2,1,0:T(8,128)(2,1)S(1)} %get-tuple-element.18.refs_0_), channel_id=1, source_target_pairs={{16,32},{0,240},{48,64},{32,16},{80,96},{64,48},{112,128},{96,80},... | collective-permute-start | bytes 786440 | tf_op jit(solution)/shard_map/ppermute | solution.py:50
  9.0 7.2 %collective-permute-start.1 = (bf16[2,512,128]{2,1,0:T(8,128)(2,1)S(1)}, bf16[2,512,128]{2,1,0:T(8,128)(2,1)S(1)}, u32[]{:S(2)}, u32[]{:S(2)}) collective-permute-start(bf16[2,512,128]{2,1,0:T(8,128)(2,1)S(1)} %collective-permute-done.refs_1_), channel_id=1, source_target_pairs={{16,32},{0,240},{48,64},{32,16},{80,96},{64,48},{112,128},{96,80},... | collective-permute-start | bytes 786440 | tf_op jit(solution)/shard_map/ppermute | solution.py:50
  13.2 7.6 %collective-permute-start.4 = (bf16[2,512,128]{2,1,0:T(8,128)(2,1)S(1)}, bf16[2,512,128]{2,1,0:T(8,128)(2,1)S(1)}, u32[]{:S(2)}, u32[]{:S(2)}) collective-permute-start(bf16[2,512,128]{2,1,0:T(8,128)(2,1)S(1)} %collective-permute-done.3.refs_4_), channel_id=1, source_target_pairs={{0,32},{16,240},{32,64},{48,16},{64,96},{80,48},{96,128},{112,80},... | collective-permute-start | bytes 786440 | tf_op jit(solution)/shard_map/ppermute | solution.py:50
  16.2 6.6 %collective-permute-start.2 = (bf16[2,512,128]{2,1,0:T(8,128)(2,1)S(1)}, bf16[2,512,128]{2,1,0:T(8,128)(2,1)S(1)}, u32[]{:S(2)}, u32[]{:S(2)}) collective-permute-start(bf16[2,512,128]{2,1,0:T(8,128)(2,1)S(1)} %collective-permute-done.1.refs_2_), channel_id=1, source_target_pairs={{0,48},{16,224},{32,80},{48,0},{64,112},{80,32},{96,144},{112,64},... | collective-permute-start | bytes 786440 | tf_op jit(solution)/shard_map/ppermute | solution.py:50
  20.8 5.8 %collective-permute-start.5 = (bf16[2,512,128]{2,1,0:T(8,128)(2,1)S(1)}, bf16[2,512,128]{2,1,0:T(8,128)(2,1)S(1)}, u32[]{:S(2)}, u32[]{:S(2)}) collective-permute-start(bf16[2,512,128]{2,1,0:T(8,128)(2,1)S(1)} %collective-permute-done.4.refs_5_), channel_id=1, source_target_pairs={{0,48},{16,224},{32,80},{48,0},{64,112},{80,32},{96,144},{112,64},... | collective-permute-start | bytes 786440 | tf_op jit(solution)/shard_map/ppermute | solution.py:50
  20.8 4.4 %collective-permute-start.7 = (s32[1,2]{1,0:T(1,128)}, s32[1,2]{1,0:T(1,128)S(1)}, u32[]{:S(2)}, u32[]{:S(2)}) collective-permute-start(s32[1,2]{1,0:T(1,128)} %pair_ref.1), channel_id=1, source_target_pairs={{0,16},{16,0},{32,48},{48,32},{64,80},{80,64},{96,112},{112,96},{1... | collective-permute-start | bytes 32 | tf_op jit(solution)/shard_map/ppermute | solution.py:235
  22.8 7.3 %collective-permute-start.6 = (bf16[2,512,128]{2,1,0:T(8,128)(2,1)S(1)}, bf16[2,512,128]{2,1,0:T(8,128)(2,1)S(1)}, u32[]{:S(2)}, u32[]{:S(2)}) collective-permute-start(bf16[2,512,128]{2,1,0:T(8,128)(2,1)S(1)} %collective-permute-done.2.refs_3_), channel_id=1, source_target_pairs={{16,32},{0,240},{48,64},{32,16},{80,96},{64,48},{112,128},{96,80},... | collective-permute-start | bytes 786440 | tf_op jit(solution)/shard_map/ppermute | solution.py:50
  26.9 4.8 %collective-permute-start.8 = (bf16[2,2,512,128]{3,2,1,0:T(8,128)(2,1)S(1)}, bf16[2,2,512,128]{3,2,1,0:T(8,128)(2,1)S(1)}, u32[]{:S(2)}, u32[]{:S(2)}) collective-permute-start(bf16[2,2,512,128]{3,2,1,0:T(8,128)(2,1)S(1)} %pick_regions.1), channel_id=1, source_target_pairs={{0,16},{16,0},{32,48},{48,32},{64,80},{80,64},{96,112},{112,96},{1... | collective-permute-start | bytes 1572872 | tf_op jit(solution)/shard_map/ppermute | solution.py:235
  30.1 1.5 %collective-permute-start.9 = (bf16[2,512,128]{2,1,0:T(8,128)(2,1)S(1)}, bf16[2,512,128]{2,1,0:T(8,128)(2,1)S(1)}, u32[]{:S(2)}, u32[]{:S(2)}) collective-permute-start(bf16[2,512,128]{2,1,0:T(8,128)(2,1)S(1)} %collective-permute-done.6.refs_7_), channel_id=1, source_target_pairs={{0,16},{16,0},{32,48},{48,32},{64,80},{80,64},{96,112},{112,96},{1... | collective-permute-start | bytes 786440 | tf_op jit(solution)/shard_map/ppermute | solution.py:235
  32.2 10.6 %collective-permute-start.10 = (bf16[1296,128]{1,0:T(8,128)(2,1)S(1)}, bf16[1296,128]{1,0:T(8,128)(2,1)S(1)}, u32[]{:S(2)}, u32[]{:S(2)}) collective-permute-start(bf16[1296,128]{1,0:T(8,128)(2,1)S(1)} %get-tuple-element.21), channel_id=1, source_target_pairs={{0,15},{1,14},{2,13},{3,12},{4,11},{5,10},{6,9},{7,8},{8,7},{9,6},... | collective-permute-start | bytes 995336 | tf_op jit(solution)/shard_map/ppermute | solution.py:231
  35.2 11.1 %collective-permute-start.11 = (bf16[1296,128]{1,0:T(8,128)(2,1)S(1)}, bf16[1296,128]{1,0:T(8,128)(2,1)S(1)}, u32[]{:S(2)}, u32[]{:S(2)}) collective-permute-start(bf16[1296,128]{1,0:T(8,128)(2,1)S(1)} %get-tuple-element.23), channel_id=1, source_target_pairs={{0,12},{1,13},{2,14},{3,15},{4,8},{5,9},{6,10},{7,11},{8,4},{9,5},... | collective-permute-start | bytes 995336 | tf_op jit(solution)/shard_map/ppermute | solution.py:231
  35.4 11.2 %collective-permute-start.12 = (bf16[1296,128]{1,0:T(8,128)(2,1)S(1)}, bf16[1296,128]{1,0:T(8,128)(2,1)S(1)}, u32[]{:S(2)}, u32[]{:S(2)}) collective-permute-start(bf16[1296,128]{1,0:T(8,128)(2,1)S(1)} %get-tuple-element.24), channel_id=1, source_target_pairs={{0,3},{1,2},{2,1},{3,0},{4,7},{5,6},{6,5},{7,4},{8,11},{9,10},{10,... | collective-permute-start | bytes 995336 | tf_op jit(solution)/shard_map/ppermute | solution.py:231
  47.4 7.5 %collective-permute-start.13 = (bf16[32,4096]{1,0:T(8,128)(2,1)S(1)}, bf16[32,4096]{1,0:T(8,128)(2,1)S(1)}, u32[]{:S(2)}, u32[]{:S(2)}) collective-permute-start(bf16[32,4096]{1,0:T(8,128)(2,1)S(1)} %get-tuple-element.26), channel_id=1, source_target_pairs={{0,5},{1,4},{2,7},{3,6},{4,1},{5,0},{6,3},{7,2},{8,13},{9,12},{10,... | collective-permute-start | bytes 786440 | tf_op jit(solution)/shard_map/ppermute | solution.py:231
  47.5 9.3 %collective-permute-start.14 = (bf16[32,4096]{1,0:T(8,128)(2,1)S(1)}, bf16[32,4096]{1,0:T(8,128)(2,1)S(1)}, u32[]{:S(2)}, u32[]{:S(2)}) collective-permute-start(bf16[32,4096]{1,0:T(8,128)(2,1)S(1)} %get-tuple-element.27), channel_id=1, source_target_pairs={{0,4},{1,5},{2,6},{3,7},{4,0},{5,1},{6,2},{7,3},{8,12},{9,13},{10,... | collective-permute-start | bytes 786440 | tf_op jit(solution)/shard_map/ppermute | solution.py:231
  48.6 8.2 %collective-permute-start.15 = (bf16[32,4096]{1,0:T(8,128)(2,1)S(1)}, bf16[32,4096]{1,0:T(8,128)(2,1)S(1)}, u32[]{:S(2)}, u32[]{:S(2)}) collective-permute-start(bf16[32,4096]{1,0:T(8,128)(2,1)S(1)} %get-tuple-element.28), channel_id=1, source_target_pairs={{0,1},{1,0},{2,3},{3,2},{4,5},{5,4},{6,7},{7,6},{8,9},{9,8},{10,11... | collective-permute-start | bytes 786440 | tf_op jit(solution)/shard_map/ppermute | solution.py:231

commit v9 on v8

--- a/solution.py
+++ b/solution.py
@@ -206,8 +206,8 @@
 def sum_kernel(*refs):
     terms, out_ref, total_ref, sems = refs[:4], refs[4], refs[5], refs[6]
     copies = []
-    for q in range(4):
-        rows = slice(8 * q, 8 * q + 8)
+    for q in range(2):
+        rows = slice(16 * q, 16 * q + 16)
         for s in range(4):
             for c in range(2):
                 at = (2 * s + c) * 512
@@ -286,7 +286,7 @@
         jax.ShapeDtypeStruct((32, 1, 4, 2, 512), F32),
         [VMEM] * 4,
         "sum_terms",
-        scratch=[pltpu.VMEM((32, 4, 2, 512), F32), pltpu.SemaphoreType.DMA((4,))],
+        scratch=[pltpu.VMEM((32, 4, 2, 512), F32), pltpu.SemaphoreType.DMA((2,))],
         out_spec=HBM,
     )(*terms)
 

time: 58 us -> 58.1 us (level)
  no operation moved by 1% of the time
where the time goes in v9:
time: 58.1 us; the launch traced here: 57.7 us
  waiting for transfers between devices  26.1 us (45%)
  starting transfers between devices  24.8 us (43%)
  Pallas kernels  4.43 us (8%)
  local copies, waits for them, and re-layouts  2.3 us (4%)
    ppermute x7, starting transfers between devices, step(): return lax.ppermute(value, 'group', perm)  13.1 us
    ppermute x7, waiting for transfers between devices, step(): return lax.ppermute(value, 'group', perm)  12.3 us
    ppermute x6, waiting for transfers between devices, exchange(): return lax.ppermute(value, ('group', 'mode'), perm)  12.3 us
    ppermute x6, starting transfers between devices, exchange(): return lax.ppermute(value, ('group', 'mode'), perm)  9.56 us
    unnamed x10, local copies, waits for them, and re-layouts  2.3 us
    ppermute x3, starting transfers between devices, swap_cores(): return lax.ppermute(value, 'group', [(g, g ^ 1) for g in range(16)])  2.14 us
    ppermute x3, waiting for transfers between devices, swap_cores(): return lax.ppermute(value, 'group', [(g, g ^ 1) for g in range(16)])  1.51 us
    pallas_call x1, Pallas kernels, shards(): call(first_kernel, (sums, jax.ShapeDtypeStruct((8, 128), F32)), [VMEM, SM...  1.19 us
  transfers between devices with their start and end apart: 16, of which 12 were waited for; matrix products, arithmetic and copies ran while one was open for 0% of the time, Pallas kernels for 4%

profile of v9, /device:TPU:6, one launch (start us, length us, event | category | flops | bytes accessed | tf_op | source)
XLA Modules:
  0.0 57.7 jit_solution(5168804813203823953)
XLA Ops:
  0.0 0.0 copy-start.3
  0.0 1.4 %collective-permute-start = (bf16[2,512,128]{2,1,0:T(8,128)(2,1)}, bf16[2,512,128]{2,1,0:T(8,128)(2,1)S(1)}, u32[]{:S(2)}, u32[]{:S(2)}) collective-permute-start(bf16[2,512,128]{2,1,0:T(8,128)(2,1)} %bitcast.3), channel_id=1, source_target_pairs={{0,48},{16,224},{32,80},{48,0},{64,112},{80,32},{96,144},{112,64},... | collective-permute-start | bytes 786440 | tf_op jit(solution)/shard_map/ppermute | solution.py:50
  1.4 0.0 copy-start
  1.4 1.0 %copy-done = bf16[2,1,512,128]{3,2,1,0:T(8,128)(2,1)S(1)} copy-done((bf16[2,1,512,128]{3,2,1,0:T(8,128)(2,1)S(1)}, bf16[2,1,512,128]{3,2,1,0:T(8,128)(2,1)}, u32[]{:S(2)}) %copy-start) | copy-done | bytes 262168
  2.3 0.0 copy-start.1
  2.3 0.7 %copy-done.1 = f32[128]{0:T(128)S(1)} copy-done((f32[128]{0:T(128)S(1)}, f32[128]{0:T(128)}, u32[]{:S(2)}) %copy-start.1) | copy-done | bytes 536
  3.0 0.0 copy-start.2
  3.0 0.7 %copy-done.2 = f32[128]{0:T(128)S(1)} copy-done((f32[128]{0:T(128)S(1)}, f32[128]{0:T(128)}, u32[]{:S(2)}) %copy-start.2) | copy-done | bytes 536
  3.7 0.0 copy-start.4
  3.7 5.3 %collective-permute-start.3 = (bf16[2,512,128]{2,1,0:T(8,128)(2,1)S(1)}, bf16[2,512,128]{2,1,0:T(8,128)(2,1)S(1)}, u32[]{:S(2)}, u32[]{:S(2)}) collective-permute-start(bf16[2,512,128]{2,1,0:T(8,128)(2,1)S(1)} %get-tuple-element.18.refs_0_), channel_id=1, source_target_pairs={{16,32},{0,240},{48,64},{32,16},{80,96},{64,48},{112,128},{96,80},... | collective-permute-start | bytes 786440 | tf_op jit(solution)/shard_map/ppermute | solution.py:50
  9.0 0.0 collective-permute-done.refs_1_
  9.0 3.1 %collective-permute-start.1 = (bf16[2,512,128]{2,1,0:T(8,128)(2,1)S(1)}, bf16[2,512,128]{2,1,0:T(8,128)(2,1)S(1)}, u32[]{:S(2)}, u32[]{:S(2)}) collective-permute-start(bf16[2,512,128]{2,1,0:T(8,128)(2,1)S(1)} %collective-permute-done.refs_1_), channel_id=1, source_target_pairs={{16,32},{0,240},{48,64},{32,16},{80,96},{64,48},{112,128},{96,80},... | collective-permute-start | bytes 786440 | tf_op jit(solution)/shard_map/ppermute | solution.py:50
  12.1 1.1 %collective-permute-done.3.refs_4_ = bf16[2,512,128]{2,1,0:T(8,128)(2,1)S(1)} collective-permute-done((bf16[2,512,128]{2,1,0:T(8,128)(2,1)S(1)}, bf16[2,512,128]{2,1,0:T(8,128)(2,1)S(1)}, u32[]{:S(2)}, u32[]{:S(2)}) %collective-permute-start.3) | collective-permute-done | bytes 262176 | tf_op jit(solution)/shard_map/ppermute | solution.py:50
  13.2 0.9 %collective-permute-start.4 = (bf16[2,512,128]{2,1,0:T(8,128)(2,1)S(1)}, bf16[2,512,128]{2,1,0:T(8,128)(2,1)S(1)}, u32[]{:S(2)}, u32[]{:S(2)}) collective-permute-start(bf16[2,512,128]{2,1,0:T(8,128)(2,1)S(1)} %collective-permute-done.3.refs_4_), channel_id=1, source_target_pairs={{0,32},{16,240},{32,64},{48,16},{64,96},{80,48},{96,128},{112,80},... | collective-permute-start | bytes 786440 | tf_op jit(solution)/shard_map/ppermute | solution.py:50
  14.1 2.1 %collective-permute-done.1.refs_2_ = bf16[2,512,128]{2,1,0:T(8,128)(2,1)S(1)} collective-permute-done((bf16[2,512,128]{2,1,0:T(8,128)(2,1)S(1)}, bf16[2,512,128]{2,1,0:T(8,128)(2,1)S(1)}, u32[]{:S(2)}, u32[]{:S(2)}) %collective-permute-start.1) | collective-permute-done | bytes 262176 | tf_op jit(solution)/shard_map/ppermute | solution.py:50
  16.2 0.0 collective-permute-start.2
  16.2 4.6 %collective-permute-done.4.refs_5_ = bf16[2,512,128]{2,1,0:T(8,128)(2,1)S(1)} collective-permute-done((bf16[2,512,128]{2,1,0:T(8,128)(2,1)S(1)}, bf16[2,512,128]{2,1,0:T(8,128)(2,1)S(1)}, u32[]{:S(2)}, u32[]{:S(2)}) %collective-permute-start.4) | collective-permute-done | bytes 262176 | tf_op jit(solution)/shard_map/ppermute | solution.py:50
  20.8 0.0 collective-permute-start.5
  20.8 1.0 %collective-permute-start.7 = (s32[1,2]{1,0:T(1,128)}, s32[1,2]{1,0:T(1,128)S(1)}, u32[]{:S(2)}, u32[]{:S(2)}) collective-permute-start(s32[1,2]{1,0:T(1,128)} %pair_ref.1), channel_id=1, source_target_pairs={{0,16},{16,0},{32,48},{48,32},{64,80},{80,64},{96,112},{112,96},{1... | collective-permute-start | bytes 32 | tf_op jit(solution)/shard_map/ppermute | solution.py:235
  21.8 1.0 %collective-permute-done.2.refs_3_ = bf16[2,512,128]{2,1,0:T(8,128)(2,1)S(1)} collective-permute-done((bf16[2,512,128]{2,1,0:T(8,128)(2,1)S(1)}, bf16[2,512,128]{2,1,0:T(8,128)(2,1)S(1)}, u32[]{:S(2)}, u32[]{:S(2)}) %collective-permute-start.2) | collective-permute-done | bytes 262176 | tf_op jit(solution)/shard_map/ppermute | solution.py:50
  22.8 2.4 %collective-permute-start.6 = (bf16[2,512,128]{2,1,0:T(8,128)(2,1)S(1)}, bf16[2,512,128]{2,1,0:T(8,128)(2,1)S(1)}, u32[]{:S(2)}, u32[]{:S(2)}) collective-permute-start(bf16[2,512,128]{2,1,0:T(8,128)(2,1)S(1)} %collective-permute-done.2.refs_3_), channel_id=1, source_target_pairs={{16,32},{0,240},{48,64},{32,16},{80,96},{64,48},{112,128},{96,80},... | collective-permute-start | bytes 786440 | tf_op jit(solution)/shard_map/ppermute | solution.py:50
  25.2 0.0 collective-permute-done.7.pair_ref
  25.2 1.4 %collective-permute-done.5.refs_6_ = bf16[2,512,128]{2,1,0:T(8,128)(2,1)S(1)} collective-permute-done((bf16[2,512,128]{2,1,0:T(8,128)(2,1)S(1)}, bf16[2,512,128]{2,1,0:T(8,128)(2,1)S(1)}, u32[]{:S(2)}, u32[]{:S(2)}) %collective-permute-start.5) | collective-permute-done | bytes 262176 | tf_op jit(solution)/shard_map/ppermute | solution.py:50
  26.6 0.3 pick_regions.1
  26.9 1.1 %collective-permute-start.8 = (bf16[2,2,512,128]{3,2,1,0:T(8,128)(2,1)S(1)}, bf16[2,2,512,128]{3,2,1,0:T(8,128)(2,1)S(1)}, u32[]{:S(2)}, u32[]{:S(2)}) collective-permute-start(bf16[2,2,512,128]{3,2,1,0:T(8,128)(2,1)S(1)} %pick_regions.1), channel_id=1, source_target_pairs={{0,16},{16,0},{32,48},{48,32},{64,80},{80,64},{96,112},{112,96},{1... | collective-permute-start | bytes 1572872 | tf_op jit(solution)/shard_map/ppermute | solution.py:235
  28.0 2.1 %collective-permute-done.6.refs_7_ = bf16[2,512,128]{2,1,0:T(8,128)(2,1)S(1)} collective-permute-done((bf16[2,512,128]{2,1,0:T(8,128)(2,1)S(1)}, bf16[2,512,128]{2,1,0:T(8,128)(2,1)S(1)}, u32[]{:S(2)}, u32[]{:S(2)}) %collective-permute-start.6) | collective-permute-done | bytes 262176 | tf_op jit(solution)/shard_map/ppermute | solution.py:50
  30.1 0.0 collective-permute-start.9
  30.1 1.5 %collective-permute-done.9.refs_9_ = bf16[2,512,128]{2,1,0:T(8,128)(2,1)S(1)} collective-permute-done((bf16[2,512,128]{2,1,0:T(8,128)(2,1)S(1)}, bf16[2,512,128]{2,1,0:T(8,128)(2,1)S(1)}, u32[]{:S(2)}, u32[]{:S(2)}) %collective-permute-start.9) | collective-permute-done | bytes 262176 | tf_op jit(solution)/shard_map/ppermute | solution.py:235
  31.6 0.0 collective-permute-done.8.refs_8_
  31.6 0.0 copy-done.3
  31.7 0.5 fan_out.1
  32.1 3.0 %collective-permute-start.10 = (bf16[1296,128]{1,0:T(8,128)(2,1)S(1)}, bf16[1296,128]{1,0:T(8,128)(2,1)S(1)}, u32[]{:S(2)}, u32[]{:S(2)}) collective-permute-start(bf16[1296,128]{1,0:T(8,128)(2,1)S(1)} %get-tuple-element.21), channel_id=1, source_target_pairs={{0,15},{1,14},{2,13},{3,12},{4,11},{5,10},{6,9},{7,8},{8,7},{9,6},... | collective-permute-start | bytes 995336 | tf_op jit(solution)/shard_map/ppermute | solution.py:231
  35.2 0.2 collective-permute-start.11
  35.4 2.8 %collective-permute-start.12 = (bf16[1296,128]{1,0:T(8,128)(2,1)S(1)}, bf16[1296,128]{1,0:T(8,128)(2,1)S(1)}, u32[]{:S(2)}, u32[]{:S(2)}) collective-permute-start(bf16[1296,128]{1,0:T(8,128)(2,1)S(1)} %get-tuple-element.24), channel_id=1, source_target_pairs={{0,3},{1,2},{2,1},{3,0},{4,7},{5,6},{6,5},{7,4},{8,11},{9,10},{10,... | collective-permute-start | bytes 995336 | tf_op jit(solution)/shard_map/ppermute | solution.py:231
  38.1 0.0 copy-done.4
  38.1 1.2 %product_0.1 = (f32[4,256,512]{2,1,0:T(8,128)S(1)}, f32[8,128]{1,0:T(8,128)S(1)}) custom-call(bf16[1296,128]{1,0:T(8,128)(2,1)S(1)} %get-tuple-element.19.part_ref, f32[4]{0:T(128)S(1)} %copy-done.4), custom_call_target="tpu_custom_call" | custom-call | flops 268435456 | bytes 1048576 | tf_op jit(solution)/shard_map/product_0/pallas_call | solution.py:265
  39.3 3.4 %collective-permute-done.10.part_ref = bf16[1296,128]{1,0:T(8,128)(2,1)S(1)} collective-permute-done((bf16[1296,128]{1,0:T(8,128)(2,1)S(1)}, bf16[1296,128]{1,0:T(8,128)(2,1)S(1)}, u32[]{:S(2)}, u32[]{:S(2)}) %collective-permute-start.10) | collective-permute-done | bytes 331808 | tf_op jit(solution)/shard_map/ppermute | solution.py:231
  42.8 0.8 %product_1.1.total_ref = f32[4,256,512]{2,1,0:T(8,128)S(1)} custom-call(f32[4,256,512]{2,1,0:T(8,128)S(1)} %get-tuple-element.20.total_ref, bf16[1296,128]{1,0:T(8,128)(2,1)S(1)} %collective-permute-done.10.part_ref, f32[8,128]{1,0:T(8,128)S(1)} %get-tuple-element.22.speeds_ref), custom_call_target="tpu_custom_call", output_to_operand_aliasing={{}: (0, {})} | custom-call | flops 268435456 | bytes 1048576 | tf_op jit(solution)/shard_map/product_1/pallas_call | solution.py:272
  43.6 2.7 %collective-permute-done.11.part_ref = bf16[1296,128]{1,0:T(8,128)(2,1)S(1)} collective-permute-done((bf16[1296,128]{1,0:T(8,128)(2,1)S(1)}, bf16[1296,128]{1,0:T(8,128)(2,1)S(1)}, u32[]{:S(2)}, u32[]{:S(2)}) %collective-permute-start.11) | collective-permute-done | bytes 331808 | tf_op jit(solution)/shard_map/ppermute | solution.py:231
  46.2 0.4 collective-permute-done.12.other_ref
  46.6 0.8 %product_2.1 = (f32[32,4096]{1,0:T(8,128)S(1)}, bf16[32,4096]{1,0:T(8,128)(2,1)S(1)}, bf16[32,4096]{1,0:T(8,128)(2,1)S(1)}, bf16[32,4096]{1,0:T(8,128)(2,1)S(1)}) custom-call(f32[4,256,512]{2,1,0:T(8,128)S(1)} %product_1.1.total_ref, bf16[1296,128]{1,0:T(8,128)(2,1)S(1)} %collective-permute-done.11.part_ref, ...), custom_call_target="tpu_custom_call" | custom-call | flops 536870912 | bytes 1048576 | tf_op jit(solution)/shard_map/product_2/pallas_call | solution.py:276
  47.4 0.1 collective-permute-start.13
  47.5 1.1 %collective-permute-start.14 = (bf16[32,4096]{1,0:T(8,128)(2,1)S(1)}, bf16[32,4096]{1,0:T(8,128)(2,1)S(1)}, u32[]{:S(2)}, u32[]{:S(2)}) collective-permute-start(bf16[32,4096]{1,0:T(8,128)(2,1)S(1)} %get-tuple-element.27), channel_id=1, source_target_pairs={{0,4},{1,5},{2,6},{3,7},{4,0},{5,1},{6,2},{7,3},{8,12},{9,13},{10,... | collective-permute-start | bytes 786440 | tf_op jit(solution)/shard_map/ppermute | solution.py:231
  48.6 2.4 %collective-permute-start.15 = (bf16[32,4096]{1,0:T(8,128)(2,1)S(1)}, bf16[32,4096]{1,0:T(8,128)(2,1)S(1)}, u32[]{:S(2)}, u32[]{:S(2)}) collective-permute-start(bf16[32,4096]{1,0:T(8,128)(2,1)S(1)} %get-tuple-element.28), channel_id=1, source_target_pairs={{0,1},{1,0},{2,3},{3,2},{4,5},{5,4},{6,7},{7,6},{8,9},{9,8},{10,11... | collective-permute-start | bytes 786440 | tf_op jit(solution)/shard_map/ppermute | solution.py:231
  51.0 3.9 %collective-permute-done.13.refs_1_ = bf16[32,4096]{1,0:T(8,128)(2,1)S(1)} collective-permute-done((bf16[32,4096]{1,0:T(8,128)(2,1)S(1)}, bf16[32,4096]{1,0:T(8,128)(2,1)S(1)}, u32[]{:S(2)}, u32[]{:S(2)}) %collective-permute-start.13) | collective-permute-done | bytes 262176 | tf_op jit(solution)/shard_map/ppermute | solution.py:231
  54.8 1.9 %collective-permute-done.14.refs_2_ = bf16[32,4096]{1,0:T(8,128)(2,1)S(1)} collective-permute-done((bf16[32,4096]{1,0:T(8,128)(2,1)S(1)}, bf16[32,4096]{1,0:T(8,128)(2,1)S(1)}, u32[]{:S(2)}, u32[]{:S(2)}) %collective-permute-start.14) | collective-permute-done | bytes 262176 | tf_op jit(solution)/shard_map/ppermute | solution.py:231
  56.8 0.0 collective-permute-done.15.refs_3_
  56.8 0.9 %sum_terms.1 = f32[32,1,4,2,512]{4,3,2,1,0:T(2,128)} custom-call(f32[32,4096]{1,0:T(8,128)S(1)} %get-tuple-element.25.refs_0_, bf16[32,4096]{1,0:T(8,128)(2,1)S(1)} %collective-permute-done.13.refs_1_, bf16[32,4096]{1,0:T(8,128)(2,1)S(1)} %collective-permute-done.14.refs_2_, bf16[32,4096]{1,0:T(8,128)(2,1)S(1)} %collective-permute-done.15.refs_3_), custom_call_target="tpu_custom_call" | custom-call | bytes 1048576 | tf_op jit(solution)/shard_map/sum_terms/pallas_call | solution.py:284
  (1 shorter events, 0.0 us)
Async XLA Ops:
  0.0 31.7 %copy-start.3 = (s32[1,2]{1,0:T(1,128)S(1)}, s32[1,2]{1,0:T(1,128)}, u32[]{:S(2)}) copy-start(s32[1,2]{1,0:T(1,128)} %pair_ref.1) | copy-start | bytes 28
  0.0 9.0 %collective-permute-start = (bf16[2,512,128]{2,1,0:T(8,128)(2,1)}, bf16[2,512,128]{2,1,0:T(8,128)(2,1)S(1)}, u32[]{:S(2)}, u32[]{:S(2)}) collective-permute-start(bf16[2,512,128]{2,1,0:T(8,128)(2,1)} %bitcast.3), channel_id=1, source_target_pairs={{0,48},{16,224},{32,80},{48,0},{64,112},{80,32},{96,144},{112,64},... | collective-permute-start | bytes 786440 | tf_op jit(solution)/shard_map/ppermute | solution.py:50
  1.4 1.0 %copy-start = (bf16[2,1,512,128]{3,2,1,0:T(8,128)(2,1)S(1)}, bf16[2,1,512,128]{3,2,1,0:T(8,128)(2,1)}, u32[]{:S(2)}) copy-start(bf16[2,1,512,128]{3,2,1,0:T(8,128)(2,1)} %shapes_ref.1) | copy-start | bytes 786436
  2.3 0.7 %copy-start.1 = (f32[128]{0:T(128)S(1)}, f32[128]{0:T(128)}, u32[]{:S(2)}) copy-start(f32[128]{0:T(128)} %param.7) | copy-start | bytes 1540
  3.0 0.7 %copy-start.2 = (f32[128]{0:T(128)S(1)}, f32[128]{0:T(128)}, u32[]{:S(2)}) copy-start(f32[128]{0:T(128)} %param.8) | copy-start | bytes 1540
  3.7 34.5 %copy-start.4 = (f32[4]{0:T(128)S(1)}, f32[4]{0:T(128)}, u32[]{:S(2)}) copy-start(f32[4]{0:T(128)} %speeds_ref.1) | copy-start | bytes 52
  3.7 9.5 %collective-permute-start.3 = (bf16[2,512,128]{2,1,0:T(8,128)(2,1)S(1)}, bf16[2,512,128]{2,1,0:T(8,128)(2,1)S(1)}, u32[]{:S(2)}, u32[]{:S(2)}) collective-permute-start(bf16[2,512,128]{2,1,0:T(8,128)(2,1)S(1)} %get-tuple-element.18.refs_0_), channel_id=1, source_target_pairs={{16,32},{0,240},{48,64},{32,16},{80,96},{64,48},{112,128},{96,80},... | collective-permute-start | bytes 786440 | tf_op jit(solution)/shard_map/ppermute | solution.py:50
  9.0 7.2 %collective-permute-start.1 = (bf16[2,512,128]{2,1,0:T(8,128)(2,1)S(1)}, bf16[2,512,128]{2,1,0:T(8,128)(2,1)S(1)}, u32[]{:S(2)}, u32[]{:S(2)}) collective-permute-start(bf16[2,512,128]{2,1,0:T(8,128)(2,1)S(1)} %collective-permute-done.refs_1_), channel_id=1, source_target_pairs={{16,32},{0,240},{48,64},{32,16},{80,96},{64,48},{112,128},{96,80},... | collective-permute-start | bytes 786440 | tf_op jit(solution)/shard_map/ppermute | solution.py:50
  13.2 7.6 %collective-permute-start.4 = (bf16[2,512,128]{2,1,0:T(8,128)(2,1)S(1)}, bf16[2,512,128]{2,1,0:T(8,128)(2,1)S(1)}, u32[]{:S(2)}, u32[]{:S(2)}) collective-permute-start(bf16[2,512,128]{2,1,0:T(8,128)(2,1)S(1)} %collective-permute-done.3.refs_4_), channel_id=1, source_target_pairs={{0,32},{16,240},{32,64},{48,16},{64,96},{80,48},{96,128},{112,80},... | collective-permute-start | bytes 786440 | tf_op jit(solution)/shard_map/ppermute | solution.py:50
  16.2 6.6 %collective-permute-start.2 = (bf16[2,512,128]{2,1,0:T(8,128)(2,1)S(1)}, bf16[2,512,128]{2,1,0:T(8,128)(2,1)S(1)}, u32[]{:S(2)}, u32[]{:S(2)}) collective-permute-start(bf16[2,512,128]{2,1,0:T(8,128)(2,1)S(1)} %collective-permute-done.1.refs_2_), channel_id=1, source_target_pairs={{0,48},{16,224},{32,80},{48,0},{64,112},{80,32},{96,144},{112,64},... | collective-permute-start | bytes 786440 | tf_op jit(solution)/shard_map/ppermute | solution.py:50
  20.8 5.8 %collective-permute-start.5 = (bf16[2,512,128]{2,1,0:T(8,128)(2,1)S(1)}, bf16[2,512,128]{2,1,0:T(8,128)(2,1)S(1)}, u32[]{:S(2)}, u32[]{:S(2)}) collective-permute-start(bf16[2,512,128]{2,1,0:T(8,128)(2,1)S(1)} %collective-permute-done.4.refs_5_), channel_id=1, source_target_pairs={{0,48},{16,224},{32,80},{48,0},{64,112},{80,32},{96,144},{112,64},... | collective-permute-start | bytes 786440 | tf_op jit(solution)/shard_map/ppermute | solution.py:50
  20.8 4.4 %collective-permute-start.7 = (s32[1,2]{1,0:T(1,128)}, s32[1,2]{1,0:T(1,128)S(1)}, u32[]{:S(2)}, u32[]{:S(2)}) collective-permute-start(s32[1,2]{1,0:T(1,128)} %pair_ref.1), channel_id=1, source_target_pairs={{0,16},{16,0},{32,48},{48,32},{64,80},{80,64},{96,112},{112,96},{1... | collective-permute-start | bytes 32 | tf_op jit(solution)/shard_map/ppermute | solution.py:235
  22.8 7.3 %collective-permute-start.6 = (bf16[2,512,128]{2,1,0:T(8,128)(2,1)S(1)}, bf16[2,512,128]{2,1,0:T(8,128)(2,1)S(1)}, u32[]{:S(2)}, u32[]{:S(2)}) collective-permute-start(bf16[2,512,128]{2,1,0:T(8,128)(2,1)S(1)} %collective-permute-done.2.refs_3_), channel_id=1, source_target_pairs={{16,32},{0,240},{48,64},{32,16},{80,96},{64,48},{112,128},{96,80},... | collective-permute-start | bytes 786440 | tf_op jit(solution)/shard_map/ppermute | solution.py:50
  26.9 4.8 %collective-permute-start.8 = (bf16[2,2,512,128]{3,2,1,0:T(8,128)(2,1)S(1)}, bf16[2,2,512,128]{3,2,1,0:T(8,128)(2,1)S(1)}, u32[]{:S(2)}, u32[]{:S(2)}) collective-permute-start(bf16[2,2,512,128]{3,2,1,0:T(8,128)(2,1)S(1)} %pick_regions.1), channel_id=1, source_target_pairs={{0,16},{16,0},{32,48},{48,32},{64,80},{80,64},{96,112},{112,96},{1... | collective-permute-start | bytes 1572872 | tf_op jit(solution)/shard_map/ppermute | solution.py:235
  30.1 1.5 %collective-permute-start.9 = (bf16[2,512,128]{2,1,0:T(8,128)(2,1)S(1)}, bf16[2,512,128]{2,1,0:T(8,128)(2,1)S(1)}, u32[]{:S(2)}, u32[]{:S(2)}) collective-permute-start(bf16[2,512,128]{2,1,0:T(8,128)(2,1)S(1)} %collective-permute-done.6.refs_7_), channel_id=1, source_target_pairs={{0,16},{16,0},{32,48},{48,32},{64,80},{80,64},{96,112},{112,96},{1... | collective-permute-start | bytes 786440 | tf_op jit(solution)/shard_map/ppermute | solution.py:235
  32.1 10.6 %collective-permute-start.10 = (bf16[1296,128]{1,0:T(8,128)(2,1)S(1)}, bf16[1296,128]{1,0:T(8,128)(2,1)S(1)}, u32[]{:S(2)}, u32[]{:S(2)}) collective-permute-start(bf16[1296,128]{1,0:T(8,128)(2,1)S(1)} %get-tuple-element.21), channel_id=1, source_target_pairs={{0,15},{1,14},{2,13},{3,12},{4,11},{5,10},{6,9},{7,8},{8,7},{9,6},... | collective-permute-start | bytes 995336 | tf_op jit(solution)/shard_map/ppermute | solution.py:231
  35.2 11.1 %collective-permute-start.11 = (bf16[1296,128]{1,0:T(8,128)(2,1)S(1)}, bf16[1296,128]{1,0:T(8,128)(2,1)S(1)}, u32[]{:S(2)}, u32[]{:S(2)}) collective-permute-start(bf16[1296,128]{1,0:T(8,128)(2,1)S(1)} %get-tuple-element.23), channel_id=1, source_target_pairs={{0,12},{1,13},{2,14},{3,15},{4,8},{5,9},{6,10},{7,11},{8,4},{9,5},... | collective-permute-start | bytes 995336 | tf_op jit(solution)/shard_map/ppermute | solution.py:231
  35.4 11.2 %collective-permute-start.12 = (bf16[1296,128]{1,0:T(8,128)(2,1)S(1)}, bf16[1296,128]{1,0:T(8,128)(2,1)S(1)}, u32[]{:S(2)}, u32[]{:S(2)}) collective-permute-start(bf16[1296,128]{1,0:T(8,128)(2,1)S(1)} %get-tuple-element.24), channel_id=1, source_target_pairs={{0,3},{1,2},{2,1},{3,0},{4,7},{5,6},{6,5},{7,4},{8,11},{9,10},{10,... | collective-permute-start | bytes 995336 | tf_op jit(solution)/shard_map/ppermute | solution.py:231
  47.4 7.5 %collective-permute-start.13 = (bf16[32,4096]{1,0:T(8,128)(2,1)S(1)}, bf16[32,4096]{1,0:T(8,128)(2,1)S(1)}, u32[]{:S(2)}, u32[]{:S(2)}) collective-permute-start(bf16[32,4096]{1,0:T(8,128)(2,1)S(1)} %get-tuple-element.26), channel_id=1, source_target_pairs={{0,5},{1,4},{2,7},{3,6},{4,1},{5,0},{6,3},{7,2},{8,13},{9,12},{10,... | collective-permute-start | bytes 786440 | tf_op jit(solution)/shard_map/ppermute | solution.py:231
  47.5 9.3 %collective-permute-start.14 = (bf16[32,4096]{1,0:T(8,128)(2,1)S(1)}, bf16[32,4096]{1,0:T(8,128)(2,1)S(1)}, u32[]{:S(2)}, u32[]{:S(2)}) collective-permute-start(bf16[32,4096]{1,0:T(8,128)(2,1)S(1)} %get-tuple-element.27), channel_id=1, source_target_pairs={{0,4},{1,5},{2,6},{3,7},{4,0},{5,1},{6,2},{7,3},{8,12},{9,13},{10,... | collective-permute-start | bytes 786440 | tf_op jit(solution)/shard_map/ppermute | solution.py:231
  48.6 8.2 %collective-permute-start.15 = (bf16[32,4096]{1,0:T(8,128)(2,1)S(1)}, bf16[32,4096]{1,0:T(8,128)(2,1)S(1)}, u32[]{:S(2)}, u32[]{:S(2)}) collective-permute-start(bf16[32,4096]{1,0:T(8,128)(2,1)S(1)} %get-tuple-element.28), channel_id=1, source_target_pairs={{0,1},{1,0},{2,3},{3,2},{4,5},{5,4},{6,7},{7,6},{8,9},{9,8},{10,11... | collective-permute-start | bytes 786440 | tf_op jit(solution)/shard_map/ppermute | solution.py:231

commit v10 on v9

--- a/solution.py
+++ b/solution.py
@@ -260,7 +260,7 @@
         "fan_out",
         scratch=[pltpu.VMEM((2, 2, 512, 128), BF)],
     )(pairs, table, *regions, a4, swap_cores(wanted), swap_cores(a4))
-    parts = [fanned[0]] + [exchange(fanned[d], d, 0) for d in (3, 2, 1)]
+    parts = [fanned[0]] + [exchange(fanned[d], d, 0) for d in (3, 1, 2)]
     sums = jax.ShapeDtypeStruct((4, 256, 512), F32)
     total, speed_rows = call(
         first_kernel,

time: 58.1 us -> 58.1 us (level)
  transfers between devices with their start and end apart: 16 -> 16, of which waited for: 12 -> 11; matrix products, arithmetic and copies ran while one was open for 0% -> 0% of each run, Pallas kernels for 4% -> 4%
where the time goes in v10:
time: 58.1 us; the launch traced here: 57.6 us
  waiting for transfers between devices  26.1 us (45%)
  starting transfers between devices  24.8 us (43%)
  Pallas kernels  4.42 us (8%)
  local copies, waits for them, and re-layouts  2.3 us (4%)
    ppermute x7, starting transfers between devices, step(): return lax.ppermute(value, 'group', perm)  13.1 us
    ppermute x7, waiting for transfers between devices, step(): return lax.ppermute(value, 'group', perm)  12.3 us
    ppermute x6, waiting for transfers between devices, exchange(): return lax.ppermute(value, ('group', 'mode'), perm)  12.2 us
    ppermute x6, starting transfers between devices, exchange(): return lax.ppermute(value, ('group', 'mode'), perm)  9.56 us
    unnamed x10, local copies, waits for them, and re-layouts  2.3 us
    ppermute x3, starting transfers between devices, swap_cores(): return lax.ppermute(value, 'group', [(g, g ^ 1) for g in range(16)])  2.14 us
    ppermute x3, waiting for transfers between devices, swap_cores(): return lax.ppermute(value, 'group', [(g, g ^ 1) for g in range(16)])  1.51 us
    pallas_call x1, Pallas kernels, shards(): call(first_kernel, (sums, jax.ShapeDtypeStruct((8, 128), F32)), [VMEM, SM...  1.19 us
  transfers between devices with their start and end apart: 16, of which 11 were waited for; matrix products, arithmetic and copies ran while one was open for 0% of the time, Pallas kernels for 4%

profile of v10, /device:TPU:6, one launch (start us, length us, event | category | flops | bytes accessed | tf_op | source)
XLA Modules:
  0.0 57.6 jit_solution(7986259505209846252)
XLA Ops:
  0.0 0.0 copy-start.3
  0.0 1.4 %collective-permute-start = (bf16[2,512,128]{2,1,0:T(8,128)(2,1)}, bf16[2,512,128]{2,1,0:T(8,128)(2,1)S(1)}, u32[]{:S(2)}, u32[]{:S(2)}) collective-permute-start(bf16[2,512,128]{2,1,0:T(8,128)(2,1)} %bitcast.3), channel_id=1, source_target_pairs={{0,48},{16,224},{32,80},{48,0},{64,112},{80,32},{96,144},{112,64},... | collective-permute-start | bytes 786440 | tf_op jit(solution)/shard_map/ppermute | solution.py:50
  1.4 0.0 copy-start
  1.4 1.0 %copy-done = bf16[2,1,512,128]{3,2,1,0:T(8,128)(2,1)S(1)} copy-done((bf16[2,1,512,128]{3,2,1,0:T(8,128)(2,1)S(1)}, bf16[2,1,512,128]{3,2,1,0:T(8,128)(2,1)}, u32[]{:S(2)}) %copy-start) | copy-done | bytes 262168
  2.3 0.0 copy-start.1
  2.3 0.7 %copy-done.1 = f32[128]{0:T(128)S(1)} copy-done((f32[128]{0:T(128)S(1)}, f32[128]{0:T(128)}, u32[]{:S(2)}) %copy-start.1) | copy-done | bytes 536
  3.0 0.0 copy-start.2
  3.0 0.7 %copy-done.2 = f32[128]{0:T(128)S(1)} copy-done((f32[128]{0:T(128)S(1)}, f32[128]{0:T(128)}, u32[]{:S(2)}) %copy-start.2) | copy-done | bytes 536
  3.7 0.0 copy-start.4
  3.7 5.3 %collective-permute-start.3 = (bf16[2,512,128]{2,1,0:T(8,128)(2,1)S(1)}, bf16[2,512,128]{2,1,0:T(8,128)(2,1)S(1)}, u32[]{:S(2)}, u32[]{:S(2)}) collective-permute-start(bf16[2,512,128]{2,1,0:T(8,128)(2,1)S(1)} %get-tuple-element.18.refs_0_), channel_id=1, source_target_pairs={{16,32},{0,240},{48,64},{32,16},{80,96},{64,48},{112,128},{96,80},... | collective-permute-start | bytes 786440 | tf_op jit(solution)/shard_map/ppermute | solution.py:50
  9.0 0.0 collective-permute-done.refs_1_
  9.0 3.1 %collective-permute-start.1 = (bf16[2,512,128]{2,1,0:T(8,128)(2,1)S(1)}, bf16[2,512,128]{2,1,0:T(8,128)(2,1)S(1)}, u32[]{:S(2)}, u32[]{:S(2)}) collective-permute-start(bf16[2,512,128]{2,1,0:T(8,128)(2,1)S(1)} %collective-permute-done.refs_1_), channel_id=1, source_target_pairs={{16,32},{0,240},{48,64},{32,16},{80,96},{64,48},{112,128},{96,80},... | collective-permute-start | bytes 786440 | tf_op jit(solution)/shard_map/ppermute | solution.py:50
  12.1 1.1 %collective-permute-done.3.refs_4_ = bf16[2,512,128]{2,1,0:T(8,128)(2,1)S(1)} collective-permute-done((bf16[2,512,128]{2,1,0:T(8,128)(2,1)S(1)}, bf16[2,512,128]{2,1,0:T(8,128)(2,1)S(1)}, u32[]{:S(2)}, u32[]{:S(2)}) %collective-permute-start.3) | collective-permute-done | bytes 262176 | tf_op jit(solution)/shard_map/ppermute | solution.py:50
  13.2 0.9 %collective-permute-start.4 = (bf16[2,512,128]{2,1,0:T(8,128)(2,1)S(1)}, bf16[2,512,128]{2,1,0:T(8,128)(2,1)S(1)}, u32[]{:S(2)}, u32[]{:S(2)}) collective-permute-start(bf16[2,512,128]{2,1,0:T(8,128)(2,1)S(1)} %collective-permute-done.3.refs_4_), channel_id=1, source_target_pairs={{0,32},{16,240},{32,64},{48,16},{64,96},{80,48},{96,128},{112,80},... | collective-permute-start | bytes 786440 | tf_op jit(solution)/shard_map/ppermute | solution.py:50
  14.1 2.1 %collective-permute-done.1.refs_2_ = bf16[2,512,128]{2,1,0:T(8,128)(2,1)S(1)} collective-permute-done((bf16[2,512,128]{2,1,0:T(8,128)(2,1)S(1)}, bf16[2,512,128]{2,1,0:T(8,128)(2,1)S(1)}, u32[]{:S(2)}, u32[]{:S(2)}) %collective-permute-start.1) | collective-permute-done | bytes 262176 | tf_op jit(solution)/shard_map/ppermute | solution.py:50
  16.2 0.0 collective-permute-start.2
  16.2 4.6 %collective-permute-done.4.refs_5_ = bf16[2,512,128]{2,1,0:T(8,128)(2,1)S(1)} collective-permute-done((bf16[2,512,128]{2,1,0:T(8,128)(2,1)S(1)}, bf16[2,512,128]{2,1,0:T(8,128)(2,1)S(1)}, u32[]{:S(2)}, u32[]{:S(2)}) %collective-permute-start.4) | collective-permute-done | bytes 262176 | tf_op jit(solution)/shard_map/ppermute | solution.py:50
  20.8 0.0 collective-permute-start.5
  20.8 1.0 %collective-permute-start.7 = (s32[1,2]{1,0:T(1,128)}, s32[1,2]{1,0:T(1,128)S(1)}, u32[]{:S(2)}, u32[]{:S(2)}) collective-permute-start(s32[1,2]{1,0:T(1,128)} %pair_ref.1), channel_id=1, source_target_pairs={{0,16},{16,0},{32,48},{48,32},{64,80},{80,64},{96,112},{112,96},{1... | collective-permute-start | bytes 32 | tf_op jit(solution)/shard_map/ppermute | solution.py:235
  21.8 1.0 %collective-permute-done.2.refs_3_ = bf16[2,512,128]{2,1,0:T(8,128)(2,1)S(1)} collective-permute-done((bf16[2,512,128]{2,1,0:T(8,128)(2,1)S(1)}, bf16[2,512,128]{2,1,0:T(8,128)(2,1)S(1)}, u32[]{:S(2)}, u32[]{:S(2)}) %collective-permute-start.2) | collective-permute-done | bytes 262176 | tf_op jit(solution)/shard_map/ppermute | solution.py:50
  22.8 2.4 %collective-permute-start.6 = (bf16[2,512,128]{2,1,0:T(8,128)(2,1)S(1)}, bf16[2,512,128]{2,1,0:T(8,128)(2,1)S(1)}, u32[]{:S(2)}, u32[]{:S(2)}) collective-permute-start(bf16[2,512,128]{2,1,0:T(8,128)(2,1)S(1)} %collective-permute-done.2.refs_3_), channel_id=1, source_target_pairs={{16,32},{0,240},{48,64},{32,16},{80,96},{64,48},{112,128},{96,80},... | collective-permute-start | bytes 786440 | tf_op jit(solution)/shard_map/ppermute | solution.py:50
  25.2 0.0 collective-permute-done.7.pair_ref
  25.2 1.4 %collective-permute-done.5.refs_6_ = bf16[2,512,128]{2,1,0:T(8,128)(2,1)S(1)} collective-permute-done((bf16[2,512,128]{2,1,0:T(8,128)(2,1)S(1)}, bf16[2,512,128]{2,1,0:T(8,128)(2,1)S(1)}, u32[]{:S(2)}, u32[]{:S(2)}) %collective-permute-start.5) | collective-permute-done | bytes 262176 | tf_op jit(solution)/shard_map/ppermute | solution.py:50
  26.6 0.2 pick_regions.1
  26.9 1.1 %collective-permute-start.8 = (bf16[2,2,512,128]{3,2,1,0:T(8,128)(2,1)S(1)}, bf16[2,2,512,128]{3,2,1,0:T(8,128)(2,1)S(1)}, u32[]{:S(2)}, u32[]{:S(2)}) collective-permute-start(bf16[2,2,512,128]{3,2,1,0:T(8,128)(2,1)S(1)} %pick_regions.1), channel_id=1, source_target_pairs={{0,16},{16,0},{32,48},{48,32},{64,80},{80,64},{96,112},{112,96},{1... | collective-permute-start | bytes 1572872 | tf_op jit(solution)/shard_map/ppermute | solution.py:235
  28.0 2.1 %collective-permute-done.6.refs_7_ = bf16[2,512,128]{2,1,0:T(8,128)(2,1)S(1)} collective-permute-done((bf16[2,512,128]{2,1,0:T(8,128)(2,1)S(1)}, bf16[2,512,128]{2,1,0:T(8,128)(2,1)S(1)}, u32[]{:S(2)}, u32[]{:S(2)}) %collective-permute-start.6) | collective-permute-done | bytes 262176 | tf_op jit(solution)/shard_map/ppermute | solution.py:50
  30.1 0.0 collective-permute-start.9
  30.1 1.5 %collective-permute-done.9.refs_9_ = bf16[2,512,128]{2,1,0:T(8,128)(2,1)S(1)} collective-permute-done((bf16[2,512,128]{2,1,0:T(8,128)(2,1)S(1)}, bf16[2,512,128]{2,1,0:T(8,128)(2,1)S(1)}, u32[]{:S(2)}, u32[]{:S(2)}) %collective-permute-start.9) | collective-permute-done | bytes 262176 | tf_op jit(solution)/shard_map/ppermute | solution.py:235
  31.6 0.0 collective-permute-done.8.refs_8_
  31.6 0.0 copy-done.3
  31.7 0.5 fan_out.1
  32.1 3.0 %collective-permute-start.10 = (bf16[1296,128]{1,0:T(8,128)(2,1)S(1)}, bf16[1296,128]{1,0:T(8,128)(2,1)S(1)}, u32[]{:S(2)}, u32[]{:S(2)}) collective-permute-start(bf16[1296,128]{1,0:T(8,128)(2,1)S(1)} %get-tuple-element.21), channel_id=1, source_target_pairs={{0,15},{1,14},{2,13},{3,12},{4,11},{5,10},{6,9},{7,8},{8,7},{9,6},... | collective-permute-start | bytes 995336 | tf_op jit(solution)/shard_map/ppermute | solution.py:231
  35.2 2.8 %collective-permute-start.11 = (bf16[1296,128]{1,0:T(8,128)(2,1)S(1)}, bf16[1296,128]{1,0:T(8,128)(2,1)S(1)}, u32[]{:S(2)}, u32[]{:S(2)}) collective-permute-start(bf16[1296,128]{1,0:T(8,128)(2,1)S(1)} %get-tuple-element.23), channel_id=1, source_target_pairs={{0,3},{1,2},{2,1},{3,0},{4,7},{5,6},{6,5},{7,4},{8,11},{9,10},{10,... | collective-permute-start | bytes 995336 | tf_op jit(solution)/shard_map/ppermute | solution.py:231
  37.9 0.2 collective-permute-start.12
  38.1 0.0 copy-done.4
  38.1 1.2 %product_0.1 = (f32[4,256,512]{2,1,0:T(8,128)S(1)}, f32[8,128]{1,0:T(8,128)S(1)}) custom-call(bf16[1296,128]{1,0:T(8,128)(2,1)S(1)} %get-tuple-element.19.part_ref, f32[4]{0:T(128)S(1)} %copy-done.4), custom_call_target="tpu_custom_call" | custom-call | flops 268435456 | bytes 1048576 | tf_op jit(solution)/shard_map/product_0/pallas_call | solution.py:265
  39.3 3.3 %collective-permute-done.10.part_ref = bf16[1296,128]{1,0:T(8,128)(2,1)S(1)} collective-permute-done((bf16[1296,128]{1,0:T(8,128)(2,1)S(1)}, bf16[1296,128]{1,0:T(8,128)(2,1)S(1)}, u32[]{:S(2)}, u32[]{:S(2)}) %collective-permute-start.10) | collective-permute-done | bytes 331808 | tf_op jit(solution)/shard_map/ppermute | solution.py:231
  42.7 0.8 %product_1.1.total_ref = f32[4,256,512]{2,1,0:T(8,128)S(1)} custom-call(f32[4,256,512]{2,1,0:T(8,128)S(1)} %get-tuple-element.20.total_ref, bf16[1296,128]{1,0:T(8,128)(2,1)S(1)} %collective-permute-done.10.part_ref, f32[8,128]{1,0:T(8,128)S(1)} %get-tuple-element.22.speeds_ref), custom_call_target="tpu_custom_call", output_to_operand_aliasing={{}: (0, {})} | custom-call | flops 268435456 | bytes 1048576 | tf_op jit(solution)/shard_map/product_1/pallas_call | solution.py:272
  43.5 3.1 %collective-permute-done.11.part_ref = bf16[1296,128]{1,0:T(8,128)(2,1)S(1)} collective-permute-done((bf16[1296,128]{1,0:T(8,128)(2,1)S(1)}, bf16[1296,128]{1,0:T(8,128)(2,1)S(1)}, u32[]{:S(2)}, u32[]{:S(2)}) %collective-permute-start.11) | collective-permute-done | bytes 331808 | tf_op jit(solution)/shard_map/ppermute | solution.py:231
  46.6 0.0 collective-permute-done.12.other_ref
  46.6 0.8 %product_2.1 = (f32[32,4096]{1,0:T(8,128)S(1)}, bf16[32,4096]{1,0:T(8,128)(2,1)S(1)}, bf16[32,4096]{1,0:T(8,128)(2,1)S(1)}, bf16[32,4096]{1,0:T(8,128)(2,1)S(1)}) custom-call(f32[4,256,512]{2,1,0:T(8,128)S(1)} %product_1.1.total_ref, bf16[1296,128]{1,0:T(8,128)(2,1)S(1)} %collective-permute-done.11.part_ref, ...), custom_call_target="tpu_custom_call" | custom-call | flops 536870912 | bytes 1048576 | tf_op jit(solution)/shard_map/product_2/pallas_call | solution.py:276
  47.3 0.1 collective-permute-start.13
  47.4 1.1 %collective-permute-start.14 = (bf16[32,4096]{1,0:T(8,128)(2,1)S(1)}, bf16[32,4096]{1,0:T(8,128)(2,1)S(1)}, u32[]{:S(2)}, u32[]{:S(2)}) collective-permute-start(bf16[32,4096]{1,0:T(8,128)(2,1)S(1)} %get-tuple-element.27), channel_id=1, source_target_pairs={{0,4},{1,5},{2,6},{3,7},{4,0},{5,1},{6,2},{7,3},{8,12},{9,13},{10,... | collective-permute-start | bytes 786440 | tf_op jit(solution)/shard_map/ppermute | solution.py:231
  48.5 2.4 %collective-permute-start.15 = (bf16[32,4096]{1,0:T(8,128)(2,1)S(1)}, bf16[32,4096]{1,0:T(8,128)(2,1)S(1)}, u32[]{:S(2)}, u32[]{:S(2)}) collective-permute-start(bf16[32,4096]{1,0:T(8,128)(2,1)S(1)} %get-tuple-element.28), channel_id=1, source_target_pairs={{0,1},{1,0},{2,3},{3,2},{4,5},{5,4},{6,7},{7,6},{8,9},{9,8},{10,11... | collective-permute-start | bytes 786440 | tf_op jit(solution)/shard_map/ppermute | solution.py:231
  50.9 3.9 %collective-permute-done.13.refs_1_ = bf16[32,4096]{1,0:T(8,128)(2,1)S(1)} collective-permute-done((bf16[32,4096]{1,0:T(8,128)(2,1)S(1)}, bf16[32,4096]{1,0:T(8,128)(2,1)S(1)}, u32[]{:S(2)}, u32[]{:S(2)}) %collective-permute-start.13) | collective-permute-done | bytes 262176 | tf_op jit(solution)/shard_map/ppermute | solution.py:231
  54.8 1.9 %collective-permute-done.14.refs_2_ = bf16[32,4096]{1,0:T(8,128)(2,1)S(1)} collective-permute-done((bf16[32,4096]{1,0:T(8,128)(2,1)S(1)}, bf16[32,4096]{1,0:T(8,128)(2,1)S(1)}, u32[]{:S(2)}, u32[]{:S(2)}) %collective-permute-start.14) | collective-permute-done | bytes 262176 | tf_op jit(solution)/shard_map/ppermute | solution.py:231
  56.7 0.0 collective-permute-done.15.refs_3_
  56.7 0.9 %sum_terms.1 = f32[32,1,4,2,512]{4,3,2,1,0:T(2,128)} custom-call(f32[32,4096]{1,0:T(8,128)S(1)} %get-tuple-element.25.refs_0_, bf16[32,4096]{1,0:T(8,128)(2,1)S(1)} %collective-permute-done.13.refs_1_, bf16[32,4096]{1,0:T(8,128)(2,1)S(1)} %collective-permute-done.14.refs_2_, bf16[32,4096]{1,0:T(8,128)(2,1)S(1)} %collective-permute-done.15.refs_3_), custom_call_target="tpu_custom_call" | custom-call | bytes 1048576 | tf_op jit(solution)/shard_map/sum_terms/pallas_call | solution.py:284
  (1 shorter events, 0.0 us)
Async XLA Ops:
  0.0 31.7 %copy-start.3 = (s32[1,2]{1,0:T(1,128)S(1)}, s32[1,2]{1,0:T(1,128)}, u32[]{:S(2)}) copy-start(s32[1,2]{1,0:T(1,128)} %pair_ref.1) | copy-start | bytes 28
  0.0 9.0 %collective-permute-start = (bf16[2,512,128]{2,1,0:T(8,128)(2,1)}, bf16[2,512,128]{2,1,0:T(8,128)(2,1)S(1)}, u32[]{:S(2)}, u32[]{:S(2)}) collective-permute-start(bf16[2,512,128]{2,1,0:T(8,128)(2,1)} %bitcast.3), channel_id=1, source_target_pairs={{0,48},{16,224},{32,80},{48,0},{64,112},{80,32},{96,144},{112,64},... | collective-permute-start | bytes 786440 | tf_op jit(solution)/shard_map/ppermute | solution.py:50
  1.4 1.0 %copy-start = (bf16[2,1,512,128]{3,2,1,0:T(8,128)(2,1)S(1)}, bf16[2,1,512,128]{3,2,1,0:T(8,128)(2,1)}, u32[]{:S(2)}) copy-start(bf16[2,1,512,128]{3,2,1,0:T(8,128)(2,1)} %shapes_ref.1) | copy-start | bytes 786436
  2.3 0.7 %copy-start.1 = (f32[128]{0:T(128)S(1)}, f32[128]{0:T(128)}, u32[]{:S(2)}) copy-start(f32[128]{0:T(128)} %param.7) | copy-start | bytes 1540
  3.0 0.7 %copy-start.2 = (f32[128]{0:T(128)S(1)}, f32[128]{0:T(128)}, u32[]{:S(2)}) copy-start(f32[128]{0:T(128)} %param.8) | copy-start | bytes 1540
  3.7 34.5 %copy-start.4 = (f32[4]{0:T(128)S(1)}, f32[4]{0:T(128)}, u32[]{:S(2)}) copy-start(f32[4]{0:T(128)} %speeds_ref.1) | copy-start | bytes 52
  3.7 9.5 %collective-permute-start.3 = (bf16[2,512,128]{2,1,0:T(8,128)(2,1)S(1)}, bf16[2,512,128]{2,1,0:T(8,128)(2,1)S(1)}, u32[]{:S(2)}, u32[]{:S(2)}) collective-permute-start(bf16[2,512,128]{2,1,0:T(8,128)(2,1)S(1)} %get-tuple-element.18.refs_0_), channel_id=1, source_target_pairs={{16,32},{0,240},{48,64},{32,16},{80,96},{64,48},{112,128},{96,80},... | collective-permute-start | bytes 786440 | tf_op jit(solution)/shard_map/ppermute | solution.py:50
  9.0 7.2 %collective-permute-start.1 = (bf16[2,512,128]{2,1,0:T(8,128)(2,1)S(1)}, bf16[2,512,128]{2,1,0:T(8,128)(2,1)S(1)}, u32[]{:S(2)}, u32[]{:S(2)}) collective-permute-start(bf16[2,512,128]{2,1,0:T(8,128)(2,1)S(1)} %collective-permute-done.refs_1_), channel_id=1, source_target_pairs={{16,32},{0,240},{48,64},{32,16},{80,96},{64,48},{112,128},{96,80},... | collective-permute-start | bytes 786440 | tf_op jit(solution)/shard_map/ppermute | solution.py:50
  13.2 7.6 %collective-permute-start.4 = (bf16[2,512,128]{2,1,0:T(8,128)(2,1)S(1)}, bf16[2,512,128]{2,1,0:T(8,128)(2,1)S(1)}, u32[]{:S(2)}, u32[]{:S(2)}) collective-permute-start(bf16[2,512,128]{2,1,0:T(8,128)(2,1)S(1)} %collective-permute-done.3.refs_4_), channel_id=1, source_target_pairs={{0,32},{16,240},{32,64},{48,16},{64,96},{80,48},{96,128},{112,80},... | collective-permute-start | bytes 786440 | tf_op jit(solution)/shard_map/ppermute | solution.py:50
  16.2 6.6 %collective-permute-start.2 = (bf16[2,512,128]{2,1,0:T(8,128)(2,1)S(1)}, bf16[2,512,128]{2,1,0:T(8,128)(2,1)S(1)}, u32[]{:S(2)}, u32[]{:S(2)}) collective-permute-start(bf16[2,512,128]{2,1,0:T(8,128)(2,1)S(1)} %collective-permute-done.1.refs_2_), channel_id=1, source_target_pairs={{0,48},{16,224},{32,80},{48,0},{64,112},{80,32},{96,144},{112,64},... | collective-permute-start | bytes 786440 | tf_op jit(solution)/shard_map/ppermute | solution.py:50
  20.8 5.8 %collective-permute-start.5 = (bf16[2,512,128]{2,1,0:T(8,128)(2,1)S(1)}, bf16[2,512,128]{2,1,0:T(8,128)(2,1)S(1)}, u32[]{:S(2)}, u32[]{:S(2)}) collective-permute-start(bf16[2,512,128]{2,1,0:T(8,128)(2,1)S(1)} %collective-permute-done.4.refs_5_), channel_id=1, source_target_pairs={{0,48},{16,224},{32,80},{48,0},{64,112},{80,32},{96,144},{112,64},... | collective-permute-start | bytes 786440 | tf_op jit(solution)/shard_map/ppermute | solution.py:50
  20.8 4.4 %collective-permute-start.7 = (s32[1,2]{1,0:T(1,128)}, s32[1,2]{1,0:T(1,128)S(1)}, u32[]{:S(2)}, u32[]{:S(2)}) collective-permute-start(s32[1,2]{1,0:T(1,128)} %pair_ref.1), channel_id=1, source_target_pairs={{0,16},{16,0},{32,48},{48,32},{64,80},{80,64},{96,112},{112,96},{1... | collective-permute-start | bytes 32 | tf_op jit(solution)/shard_map/ppermute | solution.py:235
  22.8 7.3 %collective-permute-start.6 = (bf16[2,512,128]{2,1,0:T(8,128)(2,1)S(1)}, bf16[2,512,128]{2,1,0:T(8,128)(2,1)S(1)}, u32[]{:S(2)}, u32[]{:S(2)}) collective-permute-start(bf16[2,512,128]{2,1,0:T(8,128)(2,1)S(1)} %collective-permute-done.2.refs_3_), channel_id=1, source_target_pairs={{16,32},{0,240},{48,64},{32,16},{80,96},{64,48},{112,128},{96,80},... | collective-permute-start | bytes 786440 | tf_op jit(solution)/shard_map/ppermute | solution.py:50
  26.9 4.8 %collective-permute-start.8 = (bf16[2,2,512,128]{3,2,1,0:T(8,128)(2,1)S(1)}, bf16[2,2,512,128]{3,2,1,0:T(8,128)(2,1)S(1)}, u32[]{:S(2)}, u32[]{:S(2)}) collective-permute-start(bf16[2,2,512,128]{3,2,1,0:T(8,128)(2,1)S(1)} %pick_regions.1), channel_id=1, source_target_pairs={{0,16},{16,0},{32,48},{48,32},{64,80},{80,64},{96,112},{112,96},{1... | collective-permute-start | bytes 1572872 | tf_op jit(solution)/shard_map/ppermute | solution.py:235
  30.1 1.5 %collective-permute-start.9 = (bf16[2,512,128]{2,1,0:T(8,128)(2,1)S(1)}, bf16[2,512,128]{2,1,0:T(8,128)(2,1)S(1)}, u32[]{:S(2)}, u32[]{:S(2)}) collective-permute-start(bf16[2,512,128]{2,1,0:T(8,128)(2,1)S(1)} %collective-permute-done.6.refs_7_), channel_id=1, source_target_pairs={{0,16},{16,0},{32,48},{48,32},{64,80},{80,64},{96,112},{112,96},{1... | collective-permute-start | bytes 786440 | tf_op jit(solution)/shard_map/ppermute | solution.py:235
  32.1 10.5 %collective-permute-start.10 = (bf16[1296,128]{1,0:T(8,128)(2,1)S(1)}, bf16[1296,128]{1,0:T(8,128)(2,1)S(1)}, u32[]{:S(2)}, u32[]{:S(2)}) collective-permute-start(bf16[1296,128]{1,0:T(8,128)(2,1)S(1)} %get-tuple-element.21), channel_id=1, source_target_pairs={{0,15},{1,14},{2,13},{3,12},{4,11},{5,10},{6,9},{7,8},{8,7},{9,6},... | collective-permute-start | bytes 995336 | tf_op jit(solution)/shard_map/ppermute | solution.py:231
  35.2 11.4 %collective-permute-start.11 = (bf16[1296,128]{1,0:T(8,128)(2,1)S(1)}, bf16[1296,128]{1,0:T(8,128)(2,1)S(1)}, u32[]{:S(2)}, u32[]{:S(2)}) collective-permute-start(bf16[1296,128]{1,0:T(8,128)(2,1)S(1)} %get-tuple-element.23), channel_id=1, source_target_pairs={{0,3},{1,2},{2,1},{3,0},{4,7},{5,6},{6,5},{7,4},{8,11},{9,10},{10,... | collective-permute-start | bytes 995336 | tf_op jit(solution)/shard_map/ppermute | solution.py:231
  37.9 8.7 %collective-permute-start.12 = (bf16[1296,128]{1,0:T(8,128)(2,1)S(1)}, bf16[1296,128]{1,0:T(8,128)(2,1)S(1)}, u32[]{:S(2)}, u32[]{:S(2)}) collective-permute-start(bf16[1296,128]{1,0:T(8,128)(2,1)S(1)} %get-tuple-element.24), channel_id=1, source_target_pairs={{0,12},{1,13},{2,14},{3,15},{4,8},{5,9},{6,10},{7,11},{8,4},{9,5},... | collective-permute-start | bytes 995336 | tf_op jit(solution)/shard_map/ppermute | solution.py:231
  47.3 7.5 %collective-permute-start.13 = (bf16[32,4096]{1,0:T(8,128)(2,1)S(1)}, bf16[32,4096]{1,0:T(8,128)(2,1)S(1)}, u32[]{:S(2)}, u32[]{:S(2)}) collective-permute-start(bf16[32,4096]{1,0:T(8,128)(2,1)S(1)} %get-tuple-element.26), channel_id=1, source_target_pairs={{0,5},{1,4},{2,7},{3,6},{4,1},{5,0},{6,3},{7,2},{8,13},{9,12},{10,... | collective-permute-start | bytes 786440 | tf_op jit(solution)/shard_map/ppermute | solution.py:231
  47.4 9.3 %collective-permute-start.14 = (bf16[32,4096]{1,0:T(8,128)(2,1)S(1)}, bf16[32,4096]{1,0:T(8,128)(2,1)S(1)}, u32[]{:S(2)}, u32[]{:S(2)}) collective-permute-start(bf16[32,4096]{1,0:T(8,128)(2,1)S(1)} %get-tuple-element.27), channel_id=1, source_target_pairs={{0,4},{1,5},{2,6},{3,7},{4,0},{5,1},{6,2},{7,3},{8,12},{9,13},{10,... | collective-permute-start | bytes 786440 | tf_op jit(solution)/shard_map/ppermute | solution.py:231
  48.5 8.2 %collective-permute-start.15 = (bf16[32,4096]{1,0:T(8,128)(2,1)S(1)}, bf16[32,4096]{1,0:T(8,128)(2,1)S(1)}, u32[]{:S(2)}, u32[]{:S(2)}) collective-permute-start(bf16[32,4096]{1,0:T(8,128)(2,1)S(1)} %get-tuple-element.28), channel_id=1, source_target_pairs={{0,1},{1,0},{2,3},{3,2},{4,5},{5,4},{6,7},{7,6},{8,9},{9,8},{10,11... | collective-permute-start | bytes 786440 | tf_op jit(solution)/shard_map/ppermute | solution.py:231

commit v11 on v10

--- a/solution.py
+++ b/solution.py
@@ -206,16 +206,14 @@
 def sum_kernel(*refs):
     terms, out_ref, total_ref, sems = refs[:4], refs[4], refs[5], refs[6]
     copies = []
-    for q in range(2):
-        rows = slice(16 * q, 16 * q + 16)
-        for s in range(4):
-            for c in range(2):
-                at = (2 * s + c) * 512
-                total = terms[0][rows, at : at + 512]
-                for ref in terms[1:]:
-                    total = total + ref[rows, at : at + 512].astype(F32)
-                total_ref[rows, s, c, :] = total
-        copy = pltpu.make_async_copy(total_ref.at[rows], out_ref.at[rows, 0], sems.at[q])
+    for s in range(4):
+        for c in range(2):
+            at = (2 * s + c) * 512
+            total = terms[0][:, at : at + 512]
+            for ref in terms[1:]:
+                total = total + ref[:, at : at + 512].astype(F32)
+            total_ref[:, s, c, :] = total
+        copy = pltpu.make_async_copy(total_ref.at[:, s], out_ref.at[:, 0, s], sems.at[s])
         copy.start()
         copies.append(copy)
     for copy in copies:
@@ -286,7 +284,7 @@
         jax.ShapeDtypeStruct((32, 1, 4, 2, 512), F32),
         [VMEM] * 4,
         "sum_terms",
-        scratch=[pltpu.VMEM((32, 4, 2, 512), F32), pltpu.SemaphoreType.DMA((2,))],
+        scratch=[pltpu.VMEM((32, 4, 2, 512), F32), pltpu.SemaphoreType.DMA((4,))],
         out_spec=HBM,
     )(*terms)
 

time: 58.1 us -> 58 us (level)
  no operation moved by 1% of the time
where the time goes in v11:
time: 58 us; the launch traced here: 57.6 us
  waiting for transfers between devices  26 us (45%)
  starting transfers between devices  24.8 us (43%)
  Pallas kernels  4.4 us (8%)
  local copies, waits for them, and re-layouts  2.3 us (4%)
    ppermute x7, starting transfers between devices, step(): return lax.ppermute(value, 'group', perm)  13.1 us
    ppermute x7, waiting for transfers between devices, step(): return lax.ppermute(value, 'group', perm)  12.3 us
    ppermute x6, waiting for transfers between devices, exchange(): return lax.ppermute(value, ('group', 'mode'), perm)  12.2 us
    ppermute x6, starting transfers between devices, exchange(): return lax.ppermute(value, ('group', 'mode'), perm)  9.56 us
    unnamed x10, local copies, waits for them, and re-layouts  2.3 us
    ppermute x3, starting transfers between devices, swap_cores(): return lax.ppermute(value, 'group', [(g, g ^ 1) for g in range(16)])  2.14 us
    ppermute x3, waiting for transfers between devices, swap_cores(): return lax.ppermute(value, 'group', [(g, g ^ 1) for g in range(16)])  1.51 us
    pallas_call x1, Pallas kernels, shards(): call(first_kernel, (sums, jax.ShapeDtypeStruct((8, 128), F32)), [VMEM, SM...  1.19 us
  transfers between devices with their start and end apart: 16, of which 11 were waited for; matrix products, arithmetic and copies ran while one was open for 0% of the time, Pallas kernels for 4%

profile of v11, /device:TPU:6, one launch (start us, length us, event | category | flops | bytes accessed | tf_op | source)
XLA Modules:
  0.0 57.6 jit_solution(17573821648310769251)
XLA Ops:
  0.0 0.0 copy-start.3
  0.0 1.4 %collective-permute-start = (bf16[2,512,128]{2,1,0:T(8,128)(2,1)}, bf16[2,512,128]{2,1,0:T(8,128)(2,1)S(1)}, u32[]{:S(2)}, u32[]{:S(2)}) collective-permute-start(bf16[2,512,128]{2,1,0:T(8,128)(2,1)} %bitcast.3), channel_id=1, source_target_pairs={{0,48},{16,224},{32,80},{48,0},{64,112},{80,32},{96,144},{112,64},... | collective-permute-start | bytes 786440 | tf_op jit(solution)/shard_map/ppermute | solution.py:50
  1.4 0.0 copy-start
  1.4 1.0 %copy-done = bf16[2,1,512,128]{3,2,1,0:T(8,128)(2,1)S(1)} copy-done((bf16[2,1,512,128]{3,2,1,0:T(8,128)(2,1)S(1)}, bf16[2,1,512,128]{3,2,1,0:T(8,128)(2,1)}, u32[]{:S(2)}) %copy-start) | copy-done | bytes 262168
  2.3 0.0 copy-start.1
  2.3 0.7 %copy-done.1 = f32[128]{0:T(128)S(1)} copy-done((f32[128]{0:T(128)S(1)}, f32[128]{0:T(128)}, u32[]{:S(2)}) %copy-start.1) | copy-done | bytes 536
  3.0 0.0 copy-start.2
  3.0 0.7 %copy-done.2 = f32[128]{0:T(128)S(1)} copy-done((f32[128]{0:T(128)S(1)}, f32[128]{0:T(128)}, u32[]{:S(2)}) %copy-start.2) | copy-done | bytes 536
  3.7 0.0 copy-start.4
  3.7 5.3 %collective-permute-start.3 = (bf16[2,512,128]{2,1,0:T(8,128)(2,1)S(1)}, bf16[2,512,128]{2,1,0:T(8,128)(2,1)S(1)}, u32[]{:S(2)}, u32[]{:S(2)}) collective-permute-start(bf16[2,512,128]{2,1,0:T(8,128)(2,1)S(1)} %get-tuple-element.18.refs_0_), channel_id=1, source_target_pairs={{16,32},{0,240},{48,64},{32,16},{80,96},{64,48},{112,128},{96,80},... | collective-permute-start | bytes 786440 | tf_op jit(solution)/shard_map/ppermute | solution.py:50
  9.0 0.0 collective-permute-done.refs_1_
  9.0 3.1 %collective-permute-start.1 = (bf16[2,512,128]{2,1,0:T(8,128)(2,1)S(1)}, bf16[2,512,128]{2,1,0:T(8,128)(2,1)S(1)}, u32[]{:S(2)}, u32[]{:S(2)}) collective-permute-start(bf16[2,512,128]{2,1,0:T(8,128)(2,1)S(1)} %collective-permute-done.refs_1_), channel_id=1, source_target_pairs={{16,32},{0,240},{48,64},{32,16},{80,96},{64,48},{112,128},{96,80},... | collective-permute-start | bytes 786440 | tf_op jit(solution)/shard_map/ppermute | solution.py:50
  12.1 1.1 %collective-permute-done.3.refs_4_ = bf16[2,512,128]{2,1,0:T(8,128)(2,1)S(1)} collective-permute-done((bf16[2,512,128]{2,1,0:T(8,128)(2,1)S(1)}, bf16[2,512,128]{2,1,0:T(8,128)(2,1)S(1)}, u32[]{:S(2)}, u32[]{:S(2)}) %collective-permute-start.3) | collective-permute-done | bytes 262176 | tf_op jit(solution)/shard_map/ppermute | solution.py:50
  13.2 0.9 %collective-permute-start.4 = (bf16[2,512,128]{2,1,0:T(8,128)(2,1)S(1)}, bf16[2,512,128]{2,1,0:T(8,128)(2,1)S(1)}, u32[]{:S(2)}, u32[]{:S(2)}) collective-permute-start(bf16[2,512,128]{2,1,0:T(8,128)(2,1)S(1)} %collective-permute-done.3.refs_4_), channel_id=1, source_target_pairs={{0,32},{16,240},{32,64},{48,16},{64,96},{80,48},{96,128},{112,80},... | collective-permute-start | bytes 786440 | tf_op jit(solution)/shard_map/ppermute | solution.py:50
  14.1 2.1 %collective-permute-done.1.refs_2_ = bf16[2,512,128]{2,1,0:T(8,128)(2,1)S(1)} collective-permute-done((bf16[2,512,128]{2,1,0:T(8,128)(2,1)S(1)}, bf16[2,512,128]{2,1,0:T(8,128)(2,1)S(1)}, u32[]{:S(2)}, u32[]{:S(2)}) %collective-permute-start.1) | collective-permute-done | bytes 262176 | tf_op jit(solution)/shard_map/ppermute | solution.py:50
  16.2 0.0 collective-permute-start.2
  16.2 4.6 %collective-permute-done.4.refs_5_ = bf16[2,512,128]{2,1,0:T(8,128)(2,1)S(1)} collective-permute-done((bf16[2,512,128]{2,1,0:T(8,128)(2,1)S(1)}, bf16[2,512,128]{2,1,0:T(8,128)(2,1)S(1)}, u32[]{:S(2)}, u32[]{:S(2)}) %collective-permute-start.4) | collective-permute-done | bytes 262176 | tf_op jit(solution)/shard_map/ppermute | solution.py:50
  20.8 0.0 collective-permute-start.5
  20.8 1.0 %collective-permute-start.7 = (s32[1,2]{1,0:T(1,128)}, s32[1,2]{1,0:T(1,128)S(1)}, u32[]{:S(2)}, u32[]{:S(2)}) collective-permute-start(s32[1,2]{1,0:T(1,128)} %pair_ref.1), channel_id=1, source_target_pairs={{0,16},{16,0},{32,48},{48,32},{64,80},{80,64},{96,112},{112,96},{1... | collective-permute-start | bytes 32 | tf_op jit(solution)/shard_map/ppermute | solution.py:233
  21.8 1.0 %collective-permute-done.2.refs_3_ = bf16[2,512,128]{2,1,0:T(8,128)(2,1)S(1)} collective-permute-done((bf16[2,512,128]{2,1,0:T(8,128)(2,1)S(1)}, bf16[2,512,128]{2,1,0:T(8,128)(2,1)S(1)}, u32[]{:S(2)}, u32[]{:S(2)}) %collective-permute-start.2) | collective-permute-done | bytes 262176 | tf_op jit(solution)/shard_map/ppermute | solution.py:50
  22.8 2.4 %collective-permute-start.6 = (bf16[2,512,128]{2,1,0:T(8,128)(2,1)S(1)}, bf16[2,512,128]{2,1,0:T(8,128)(2,1)S(1)}, u32[]{:S(2)}, u32[]{:S(2)}) collective-permute-start(bf16[2,512,128]{2,1,0:T(8,128)(2,1)S(1)} %collective-permute-done.2.refs_3_), channel_id=1, source_target_pairs={{16,32},{0,240},{48,64},{32,16},{80,96},{64,48},{112,128},{96,80},... | collective-permute-start | bytes 786440 | tf_op jit(solution)/shard_map/ppermute | solution.py:50
  25.2 0.0 collective-permute-done.7.pair_ref
  25.2 1.4 %collective-permute-done.5.refs_6_ = bf16[2,512,128]{2,1,0:T(8,128)(2,1)S(1)} collective-permute-done((bf16[2,512,128]{2,1,0:T(8,128)(2,1)S(1)}, bf16[2,512,128]{2,1,0:T(8,128)(2,1)S(1)}, u32[]{:S(2)}, u32[]{:S(2)}) %collective-permute-start.5) | collective-permute-done | bytes 262176 | tf_op jit(solution)/shard_map/ppermute | solution.py:50
  26.6 0.3 pick_regions.1
  26.9 1.1 %collective-permute-start.8 = (bf16[2,2,512,128]{3,2,1,0:T(8,128)(2,1)S(1)}, bf16[2,2,512,128]{3,2,1,0:T(8,128)(2,1)S(1)}, u32[]{:S(2)}, u32[]{:S(2)}) collective-permute-start(bf16[2,2,512,128]{3,2,1,0:T(8,128)(2,1)S(1)} %pick_regions.1), channel_id=1, source_target_pairs={{0,16},{16,0},{32,48},{48,32},{64,80},{80,64},{96,112},{112,96},{1... | collective-permute-start | bytes 1572872 | tf_op jit(solution)/shard_map/ppermute | solution.py:233
  28.0 2.1 %collective-permute-done.6.refs_7_ = bf16[2,512,128]{2,1,0:T(8,128)(2,1)S(1)} collective-permute-done((bf16[2,512,128]{2,1,0:T(8,128)(2,1)S(1)}, bf16[2,512,128]{2,1,0:T(8,128)(2,1)S(1)}, u32[]{:S(2)}, u32[]{:S(2)}) %collective-permute-start.6) | collective-permute-done | bytes 262176 | tf_op jit(solution)/shard_map/ppermute | solution.py:50
  30.1 0.0 collective-permute-start.9
  30.1 1.5 %collective-permute-done.9.refs_9_ = bf16[2,512,128]{2,1,0:T(8,128)(2,1)S(1)} collective-permute-done((bf16[2,512,128]{2,1,0:T(8,128)(2,1)S(1)}, bf16[2,512,128]{2,1,0:T(8,128)(2,1)S(1)}, u32[]{:S(2)}, u32[]{:S(2)}) %collective-permute-start.9) | collective-permute-done | bytes 262176 | tf_op jit(solution)/shard_map/ppermute | solution.py:233
  31.6 0.0 collective-permute-done.8.refs_8_
  31.6 0.0 copy-done.3
  31.7 0.5 fan_out.1
  32.1 3.0 %collective-permute-start.10 = (bf16[1296,128]{1,0:T(8,128)(2,1)S(1)}, bf16[1296,128]{1,0:T(8,128)(2,1)S(1)}, u32[]{:S(2)}, u32[]{:S(2)}) collective-permute-start(bf16[1296,128]{1,0:T(8,128)(2,1)S(1)} %get-tuple-element.21), channel_id=1, source_target_pairs={{0,15},{1,14},{2,13},{3,12},{4,11},{5,10},{6,9},{7,8},{8,7},{9,6},... | collective-permute-start | bytes 995336 | tf_op jit(solution)/shard_map/ppermute | solution.py:229
  35.2 2.8 %collective-permute-start.11 = (bf16[1296,128]{1,0:T(8,128)(2,1)S(1)}, bf16[1296,128]{1,0:T(8,128)(2,1)S(1)}, u32[]{:S(2)}, u32[]{:S(2)}) collective-permute-start(bf16[1296,128]{1,0:T(8,128)(2,1)S(1)} %get-tuple-element.23), channel_id=1, source_target_pairs={{0,3},{1,2},{2,1},{3,0},{4,7},{5,6},{6,5},{7,4},{8,11},{9,10},{10,... | collective-permute-start | bytes 995336 | tf_op jit(solution)/shard_map/ppermute | solution.py:229
  37.9 0.2 collective-permute-start.12
  38.1 0.0 copy-done.4
  38.1 1.2 %product_0.1 = (f32[4,256,512]{2,1,0:T(8,128)S(1)}, f32[8,128]{1,0:T(8,128)S(1)}) custom-call(bf16[1296,128]{1,0:T(8,128)(2,1)S(1)} %get-tuple-element.19.part_ref, f32[4]{0:T(128)S(1)} %copy-done.4), custom_call_target="tpu_custom_call" | custom-call | flops 268435456 | bytes 1048576 | tf_op jit(solution)/shard_map/product_0/pallas_call | solution.py:263
  39.3 3.3 %collective-permute-done.10.part_ref = bf16[1296,128]{1,0:T(8,128)(2,1)S(1)} collective-permute-done((bf16[1296,128]{1,0:T(8,128)(2,1)S(1)}, bf16[1296,128]{1,0:T(8,128)(2,1)S(1)}, u32[]{:S(2)}, u32[]{:S(2)}) %collective-permute-start.10) | collective-permute-done | bytes 331808 | tf_op jit(solution)/shard_map/ppermute | solution.py:229
  42.7 0.8 %product_1.1.total_ref = f32[4,256,512]{2,1,0:T(8,128)S(1)} custom-call(f32[4,256,512]{2,1,0:T(8,128)S(1)} %get-tuple-element.20.total_ref, bf16[1296,128]{1,0:T(8,128)(2,1)S(1)} %collective-permute-done.10.part_ref, f32[8,128]{1,0:T(8,128)S(1)} %get-tuple-element.22.speeds_ref), custom_call_target="tpu_custom_call", output_to_operand_aliasing={{}: (0, {})} | custom-call | flops 268435456 | bytes 1048576 | tf_op jit(solution)/shard_map/product_1/pallas_call | solution.py:270
  43.5 3.1 %collective-permute-done.11.part_ref = bf16[1296,128]{1,0:T(8,128)(2,1)S(1)} collective-permute-done((bf16[1296,128]{1,0:T(8,128)(2,1)S(1)}, bf16[1296,128]{1,0:T(8,128)(2,1)S(1)}, u32[]{:S(2)}, u32[]{:S(2)}) %collective-permute-start.11) | collective-permute-done | bytes 331808 | tf_op jit(solution)/shard_map/ppermute | solution.py:229
  46.6 0.0 collective-permute-done.12.other_ref
  46.6 0.8 %product_2.1 = (f32[32,4096]{1,0:T(8,128)S(1)}, bf16[32,4096]{1,0:T(8,128)(2,1)S(1)}, bf16[32,4096]{1,0:T(8,128)(2,1)S(1)}, bf16[32,4096]{1,0:T(8,128)(2,1)S(1)}) custom-call(f32[4,256,512]{2,1,0:T(8,128)S(1)} %product_1.1.total_ref, bf16[1296,128]{1,0:T(8,128)(2,1)S(1)} %collective-permute-done.11.part_ref, ...), custom_call_target="tpu_custom_call" | custom-call | flops 536870912 | bytes 1048576 | tf_op jit(solution)/shard_map/product_2/pallas_call | solution.py:274
  47.3 0.1 collective-permute-start.13
  47.4 1.1 %collective-permute-start.14 = (bf16[32,4096]{1,0:T(8,128)(2,1)S(1)}, bf16[32,4096]{1,0:T(8,128)(2,1)S(1)}, u32[]{:S(2)}, u32[]{:S(2)}) collective-permute-start(bf16[32,4096]{1,0:T(8,128)(2,1)S(1)} %get-tuple-element.27), channel_id=1, source_target_pairs={{0,4},{1,5},{2,6},{3,7},{4,0},{5,1},{6,2},{7,3},{8,12},{9,13},{10,... | collective-permute-start | bytes 786440 | tf_op jit(solution)/shard_map/ppermute | solution.py:229
  48.6 2.4 %collective-permute-start.15 = (bf16[32,4096]{1,0:T(8,128)(2,1)S(1)}, bf16[32,4096]{1,0:T(8,128)(2,1)S(1)}, u32[]{:S(2)}, u32[]{:S(2)}) collective-permute-start(bf16[32,4096]{1,0:T(8,128)(2,1)S(1)} %get-tuple-element.28), channel_id=1, source_target_pairs={{0,1},{1,0},{2,3},{3,2},{4,5},{5,4},{6,7},{7,6},{8,9},{9,8},{10,11... | collective-permute-start | bytes 786440 | tf_op jit(solution)/shard_map/ppermute | solution.py:229
  50.9 3.9 %collective-permute-done.13.refs_1_ = bf16[32,4096]{1,0:T(8,128)(2,1)S(1)} collective-permute-done((bf16[32,4096]{1,0:T(8,128)(2,1)S(1)}, bf16[32,4096]{1,0:T(8,128)(2,1)S(1)}, u32[]{:S(2)}, u32[]{:S(2)}) %collective-permute-start.13) | collective-permute-done | bytes 262176 | tf_op jit(solution)/shard_map/ppermute | solution.py:229
  54.8 1.9 %collective-permute-done.14.refs_2_ = bf16[32,4096]{1,0:T(8,128)(2,1)S(1)} collective-permute-done((bf16[32,4096]{1,0:T(8,128)(2,1)S(1)}, bf16[32,4096]{1,0:T(8,128)(2,1)S(1)}, u32[]{:S(2)}, u32[]{:S(2)}) %collective-permute-start.14) | collective-permute-done | bytes 262176 | tf_op jit(solution)/shard_map/ppermute | solution.py:229
  56.7 0.0 collective-permute-done.15.refs_3_
  56.7 0.9 %sum_terms.1 = f32[32,1,4,2,512]{4,3,2,1,0:T(2,128)} custom-call(f32[32,4096]{1,0:T(8,128)S(1)} %get-tuple-element.25.refs_0_, bf16[32,4096]{1,0:T(8,128)(2,1)S(1)} %collective-permute-done.13.refs_1_, bf16[32,4096]{1,0:T(8,128)(2,1)S(1)} %collective-permute-done.14.refs_2_, bf16[32,4096]{1,0:T(8,128)(2,1)S(1)} %collective-permute-done.15.refs_3_), custom_call_target="tpu_custom_call" | custom-call | bytes 1048576 | tf_op jit(solution)/shard_map/sum_terms/pallas_call | solution.py:282
  (1 shorter events, 0.0 us)
Async XLA Ops:
  0.0 31.7 %copy-start.3 = (s32[1,2]{1,0:T(1,128)S(1)}, s32[1,2]{1,0:T(1,128)}, u32[]{:S(2)}) copy-start(s32[1,2]{1,0:T(1,128)} %pair_ref.1) | copy-start | bytes 28
  0.0 9.0 %collective-permute-start = (bf16[2,512,128]{2,1,0:T(8,128)(2,1)}, bf16[2,512,128]{2,1,0:T(8,128)(2,1)S(1)}, u32[]{:S(2)}, u32[]{:S(2)}) collective-permute-start(bf16[2,512,128]{2,1,0:T(8,128)(2,1)} %bitcast.3), channel_id=1, source_target_pairs={{0,48},{16,224},{32,80},{48,0},{64,112},{80,32},{96,144},{112,64},... | collective-permute-start | bytes 786440 | tf_op jit(solution)/shard_map/ppermute | solution.py:50
  1.4 1.0 %copy-start = (bf16[2,1,512,128]{3,2,1,0:T(8,128)(2,1)S(1)}, bf16[2,1,512,128]{3,2,1,0:T(8,128)(2,1)}, u32[]{:S(2)}) copy-start(bf16[2,1,512,128]{3,2,1,0:T(8,128)(2,1)} %shapes_ref.1) | copy-start | bytes 786436
  2.3 0.7 %copy-start.1 = (f32[128]{0:T(128)S(1)}, f32[128]{0:T(128)}, u32[]{:S(2)}) copy-start(f32[128]{0:T(128)} %param.7) | copy-start | bytes 1540
  3.0 0.7 %copy-start.2 = (f32[128]{0:T(128)S(1)}, f32[128]{0:T(128)}, u32[]{:S(2)}) copy-start(f32[128]{0:T(128)} %param.8) | copy-start | bytes 1540
  3.7 34.5 %copy-start.4 = (f32[4]{0:T(128)S(1)}, f32[4]{0:T(128)}, u32[]{:S(2)}) copy-start(f32[4]{0:T(128)} %speeds_ref.1) | copy-start | bytes 52
  3.7 9.5 %collective-permute-start.3 = (bf16[2,512,128]{2,1,0:T(8,128)(2,1)S(1)}, bf16[2,512,128]{2,1,0:T(8,128)(2,1)S(1)}, u32[]{:S(2)}, u32[]{:S(2)}) collective-permute-start(bf16[2,512,128]{2,1,0:T(8,128)(2,1)S(1)} %get-tuple-element.18.refs_0_), channel_id=1, source_target_pairs={{16,32},{0,240},{48,64},{32,16},{80,96},{64,48},{112,128},{96,80},... | collective-permute-start | bytes 786440 | tf_op jit(solution)/shard_map/ppermute | solution.py:50
  9.0 7.2 %collective-permute-start.1 = (bf16[2,512,128]{2,1,0:T(8,128)(2,1)S(1)}, bf16[2,512,128]{2,1,0:T(8,128)(2,1)S(1)}, u32[]{:S(2)}, u32[]{:S(2)}) collective-permute-start(bf16[2,512,128]{2,1,0:T(8,128)(2,1)S(1)} %collective-permute-done.refs_1_), channel_id=1, source_target_pairs={{16,32},{0,240},{48,64},{32,16},{80,96},{64,48},{112,128},{96,80},... | collective-permute-start | bytes 786440 | tf_op jit(solution)/shard_map/ppermute | solution.py:50
  13.2 7.6 %collective-permute-start.4 = (bf16[2,512,128]{2,1,0:T(8,128)(2,1)S(1)}, bf16[2,512,128]{2,1,0:T(8,128)(2,1)S(1)}, u32[]{:S(2)}, u32[]{:S(2)}) collective-permute-start(bf16[2,512,128]{2,1,0:T(8,128)(2,1)S(1)} %collective-permute-done.3.refs_4_), channel_id=1, source_target_pairs={{0,32},{16,240},{32,64},{48,16},{64,96},{80,48},{96,128},{112,80},... | collective-permute-start | bytes 786440 | tf_op jit(solution)/shard_map/ppermute | solution.py:50
  16.2 6.6 %collective-permute-start.2 = (bf16[2,512,128]{2,1,0:T(8,128)(2,1)S(1)}, bf16[2,512,128]{2,1,0:T(8,128)(2,1)S(1)}, u32[]{:S(2)}, u32[]{:S(2)}) collective-permute-start(bf16[2,512,128]{2,1,0:T(8,128)(2,1)S(1)} %collective-permute-done.1.refs_2_), channel_id=1, source_target_pairs={{0,48},{16,224},{32,80},{48,0},{64,112},{80,32},{96,144},{112,64},... | collective-permute-start | bytes 786440 | tf_op jit(solution)/shard_map/ppermute | solution.py:50
  20.8 5.8 %collective-permute-start.5 = (bf16[2,512,128]{2,1,0:T(8,128)(2,1)S(1)}, bf16[2,512,128]{2,1,0:T(8,128)(2,1)S(1)}, u32[]{:S(2)}, u32[]{:S(2)}) collective-permute-start(bf16[2,512,128]{2,1,0:T(8,128)(2,1)S(1)} %collective-permute-done.4.refs_5_), channel_id=1, source_target_pairs={{0,48},{16,224},{32,80},{48,0},{64,112},{80,32},{96,144},{112,64},... | collective-permute-start | bytes 786440 | tf_op jit(solution)/shard_map/ppermute | solution.py:50
  20.8 4.4 %collective-permute-start.7 = (s32[1,2]{1,0:T(1,128)}, s32[1,2]{1,0:T(1,128)S(1)}, u32[]{:S(2)}, u32[]{:S(2)}) collective-permute-start(s32[1,2]{1,0:T(1,128)} %pair_ref.1), channel_id=1, source_target_pairs={{0,16},{16,0},{32,48},{48,32},{64,80},{80,64},{96,112},{112,96},{1... | collective-permute-start | bytes 32 | tf_op jit(solution)/shard_map/ppermute | solution.py:233
  22.8 7.3 %collective-permute-start.6 = (bf16[2,512,128]{2,1,0:T(8,128)(2,1)S(1)}, bf16[2,512,128]{2,1,0:T(8,128)(2,1)S(1)}, u32[]{:S(2)}, u32[]{:S(2)}) collective-permute-start(bf16[2,512,128]{2,1,0:T(8,128)(2,1)S(1)} %collective-permute-done.2.refs_3_), channel_id=1, source_target_pairs={{16,32},{0,240},{48,64},{32,16},{80,96},{64,48},{112,128},{96,80},... | collective-permute-start | bytes 786440 | tf_op jit(solution)/shard_map/ppermute | solution.py:50
  26.9 4.8 %collective-permute-start.8 = (bf16[2,2,512,128]{3,2,1,0:T(8,128)(2,1)S(1)}, bf16[2,2,512,128]{3,2,1,0:T(8,128)(2,1)S(1)}, u32[]{:S(2)}, u32[]{:S(2)}) collective-permute-start(bf16[2,2,512,128]{3,2,1,0:T(8,128)(2,1)S(1)} %pick_regions.1), channel_id=1, source_target_pairs={{0,16},{16,0},{32,48},{48,32},{64,80},{80,64},{96,112},{112,96},{1... | collective-permute-start | bytes 1572872 | tf_op jit(solution)/shard_map/ppermute | solution.py:233
  30.1 1.5 %collective-permute-start.9 = (bf16[2,512,128]{2,1,0:T(8,128)(2,1)S(1)}, bf16[2,512,128]{2,1,0:T(8,128)(2,1)S(1)}, u32[]{:S(2)}, u32[]{:S(2)}) collective-permute-start(bf16[2,512,128]{2,1,0:T(8,128)(2,1)S(1)} %collective-permute-done.6.refs_7_), channel_id=1, source_target_pairs={{0,16},{16,0},{32,48},{48,32},{64,80},{80,64},{96,112},{112,96},{1... | collective-permute-start | bytes 786440 | tf_op jit(solution)/shard_map/ppermute | solution.py:233
  32.1 10.5 %collective-permute-start.10 = (bf16[1296,128]{1,0:T(8,128)(2,1)S(1)}, bf16[1296,128]{1,0:T(8,128)(2,1)S(1)}, u32[]{:S(2)}, u32[]{:S(2)}) collective-permute-start(bf16[1296,128]{1,0:T(8,128)(2,1)S(1)} %get-tuple-element.21), channel_id=1, source_target_pairs={{0,15},{1,14},{2,13},{3,12},{4,11},{5,10},{6,9},{7,8},{8,7},{9,6},... | collective-permute-start | bytes 995336 | tf_op jit(solution)/shard_map/ppermute | solution.py:229
  35.2 11.4 %collective-permute-start.11 = (bf16[1296,128]{1,0:T(8,128)(2,1)S(1)}, bf16[1296,128]{1,0:T(8,128)(2,1)S(1)}, u32[]{:S(2)}, u32[]{:S(2)}) collective-permute-start(bf16[1296,128]{1,0:T(8,128)(2,1)S(1)} %get-tuple-element.23), channel_id=1, source_target_pairs={{0,3},{1,2},{2,1},{3,0},{4,7},{5,6},{6,5},{7,4},{8,11},{9,10},{10,... | collective-permute-start | bytes 995336 | tf_op jit(solution)/shard_map/ppermute | solution.py:229
  37.9 8.7 %collective-permute-start.12 = (bf16[1296,128]{1,0:T(8,128)(2,1)S(1)}, bf16[1296,128]{1,0:T(8,128)(2,1)S(1)}, u32[]{:S(2)}, u32[]{:S(2)}) collective-permute-start(bf16[1296,128]{1,0:T(8,128)(2,1)S(1)} %get-tuple-element.24), channel_id=1, source_target_pairs={{0,12},{1,13},{2,14},{3,15},{4,8},{5,9},{6,10},{7,11},{8,4},{9,5},... | collective-permute-start | bytes 995336 | tf_op jit(solution)/shard_map/ppermute | solution.py:229
  47.3 7.5 %collective-permute-start.13 = (bf16[32,4096]{1,0:T(8,128)(2,1)S(1)}, bf16[32,4096]{1,0:T(8,128)(2,1)S(1)}, u32[]{:S(2)}, u32[]{:S(2)}) collective-permute-start(bf16[32,4096]{1,0:T(8,128)(2,1)S(1)} %get-tuple-element.26), channel_id=1, source_target_pairs={{0,5},{1,4},{2,7},{3,6},{4,1},{5,0},{6,3},{7,2},{8,13},{9,12},{10,... | collective-permute-start | bytes 786440 | tf_op jit(solution)/shard_map/ppermute | solution.py:229
  47.4 9.3 %collective-permute-start.14 = (bf16[32,4096]{1,0:T(8,128)(2,1)S(1)}, bf16[32,4096]{1,0:T(8,128)(2,1)S(1)}, u32[]{:S(2)}, u32[]{:S(2)}) collective-permute-start(bf16[32,4096]{1,0:T(8,128)(2,1)S(1)} %get-tuple-element.27), channel_id=1, source_target_pairs={{0,4},{1,5},{2,6},{3,7},{4,0},{5,1},{6,2},{7,3},{8,12},{9,13},{10,... | collective-permute-start | bytes 786440 | tf_op jit(solution)/shard_map/ppermute | solution.py:229
  48.6 8.2 %collective-permute-start.15 = (bf16[32,4096]{1,0:T(8,128)(2,1)S(1)}, bf16[32,4096]{1,0:T(8,128)(2,1)S(1)}, u32[]{:S(2)}, u32[]{:S(2)}) collective-permute-start(bf16[32,4096]{1,0:T(8,128)(2,1)S(1)} %get-tuple-element.28), channel_id=1, source_target_pairs={{0,1},{1,0},{2,3},{3,2},{4,5},{5,4},{6,7},{7,6},{8,9},{9,8},{10,11... | collective-permute-start | bytes 786440 | tf_op jit(solution)/shard_map/ppermute | solution.py:229
